TPU v7x, 512 devices: a whole 4x8x8 slice. The times are simulated.
512 devices in a mesh: layer: 8 (over z), row: 64 (over x, y, core).
Axes of the slice: x: 4, y: 8, z: 8, core: 2. Of those that a mesh axis runs over, the one named last changes fastest.
Arguments:
- leaf_rhs: float32 [8, 64, 256, 384], P('layer', 'row'), may hold values from -6 to 6
- leaf_inverse: float32 [8, 64, 256, 256], P('layer', 'row'), may hold values from -0.375 to 0.375
- leaf_coupling: float32 [8, 64, 4, 512, 256], P('layer', 'row'), may hold values from -0.046875 to 0.046875
- parent: int32 [8, 64], P('layer', 'row'), may hold values from 0 to 3
- sep_rhs: float32 [8, 4, 512, 384], P('layer', None, 'row'), may hold values from -6 to 6
- sep_inverse: float32 [8, 4, 512, 512], P('layer', None, 'row'), may hold values from -0.25 to 0.25
- sep_coupling: float32 [8, 3, 512, 512], P('layer', None, 'row'), may hold values from -0.125 to 0.125
- root_coupling: float32 [8, 512, 512], P('layer', 'row'), may hold values from -0.09375 to 0.09375
- root_rhs: float32 [512, 384], P('row'), may hold values from -6 to 6
- root_inverse: float32 [512, 512], P('row'), may hold values from -0.25 to 0.25
Outputs:
- sep_solution: float32 [8, 4, 512, 384], P('layer', None, 'row')
- root_solution: float32 [512, 384], P('row')
All inputs are finite; a program needn't handle non-finite values.
Results may differ from a plain program's by a relative error of at most 0.0003.
Values sent between devices are 32-bit elements; how exact they have to be, the bound alone decides.
No kernel may reach another device: no remote copies, remote signals or barrier semaphores. Data moves between devices by JAX's collectives and lax.ppermute only.
A program may use at most 64 MiB of HBM per device.

v0:
```python
import jax
import jax.numpy as jnp
from jax import lax
from jax.sharding import PartitionSpec as P


def body(
    leaf_rhs,
    leaf_inverse,
    leaf_coupling,
    parent,
    sep_rhs,
    sep_inverse,
    sep_coupling,
    root_coupling,
    root_rhs,
    root_inverse,
):
    highest = lax.Precision.HIGHEST
    sep_count = sep_rhs.shape[1]
    row_count = sep_rhs.shape[2]
    row_start = lax.axis_index("row") * row_count
    leaf_solution = jnp.dot(leaf_inverse[0, 0], leaf_rhs[0, 0], precision=highest)
    levels = jnp.arange(sep_count, dtype=jnp.int32)
    keep_mask = (levels >= parent[0, 0]).astype(jnp.float32)
    coupled = (
        jnp.einsum("kwb,bc->kwc", leaf_coupling[0, 0], leaf_solution, precision=highest)
        * keep_mask[:, None, None]
    )
    own_rhs = lax.dynamic_update_slice_in_dim(jnp.zeros_like(coupled), sep_rhs[0], row_start, 1)
    residual = lax.psum(own_rhs - coupled, "row")
    residual_list = [residual[k] for k in range(sep_count)]
    local_rows = [
        jnp.dot(sep_inverse[0, k], residual_list[k], precision=highest) for k in range(sep_count)
    ]
    solved = []
    gathered = None
    for k in range(sep_count):
        current = local_rows[k]
        if k > 0:
            current = current - jnp.dot(sep_coupling[0, k - 1], gathered, precision=highest)
        solved.append(current)
        gathered = lax.all_gather(current, "row", axis=0, tiled=True)
    sep_out = jnp.stack(solved)[None]
    root_term = jnp.dot(root_coupling[0], gathered, precision=highest)
    root_sum = lax.psum(root_term, "layer")
    root_residual = root_rhs - root_sum
    root_out = jnp.dot(
        root_inverse, lax.all_gather(root_residual, "row", axis=0, tiled=True), precision=highest
    )
    return (sep_out, root_out)


def solution(mesh):
    return jax.shard_map(
        body,
        mesh=mesh,
        in_specs=(
            P("layer", "row", None, None),
            P("layer", "row", None, None),
            P("layer", "row", None, None, None),
            P("layer", "row"),
            P("layer", None, "row", None),
            P("layer", None, "row", None),
            P("layer", None, "row", None),
            P("layer", "row", None),
            P("row", None),
            P("row", None),
        ),
        out_specs=(P("layer", None, "row", None), P("row", None)),
        check_vma=False,
    )
```

profile of v0, /device:TPU:1, one launch (start us, length us, event | category | flops | bytes accessed | tf_op | source)
XLA Modules:
  0.0 522.9 jit_solution(4747656309365464238)
XLA Ops:
  7.2 0.0 copy-start
  7.2 0.0 all-reduce.2.cloned.1.call-start
  7.2 1.2 copy.12
  9.1 1.9 convolution_bitcast_fusion
  11.0 2.1 broadcast_in_dim.7
  13.1 4.4 dynamic_update_slice.3
  17.5 0.0 copy-done
  17.5 5.6 %bitcast_subtract_fusion = f32[4,512,384]{1,2,0:T(8,128)} fusion(f32[4,512,384]{1,2,0:T(8,128)} %dynamic_update_slice.3, f32[256,384,1]{0,1,2:T(8,128)S(1)} %convolution_bitcast_fusion, f32[1,1,4,512,256]{4,3,2,1,0:T(8,128)S(1)} %copy-done, f32[4]{0:T(128)S(1)} %compare_convert_fusion), kind=kOutput, calls=%fused_computation | convolution fusion | flops 2417491968 | bytes 8781840 | tf_op jit(solution)/shard_map/kwb,bc->kwc/dot_general | solution.py:27
  23.1 0.0 copy-start.2
  23.1 0.0 copy-start.3
  23.1 0.0 all-reduce.2.cloned.1.call-update
  23.2 207.1 %all-reduce.2.cloned.1.call-done = f32[4,512,384]{1,2,0:T(8,128)} async-done(((f32[4,512,384]{1,2,0:T(8,128)}), f32[4,512,384]{1,2,0:T(8,128)}) %all-reduce.2.cloned.1.call-update) | async-done | bytes 3145744 | tf_op jit(solution)/shard_map/psum | solution.py:31
  230.2 0.0 copy-done.2
  230.2 0.0 copy-start.1
  230.2 2.0 fusion.7
  232.2 50.8 %all_gather.15 = f32[512,384]{1,0:T(8,128)S(1)} all-gather(f32[8,384]{1,0:T(8,128)S(1)} %bitcast.80), channel_id=1, replica_groups=mesh['layer'=8,'row'=64] {'row'}, dimensions={0}, use_global_device_ids=true | all-gather | bytes 798720 | tf_op jit(solution)/shard_map/all_gather | solution.py:43
  283.0 1.8 fusion.6
  284.9 0.0 copy-done.3
  284.9 0.0 copy-start.4
  284.9 0.5 convolution_subtract_fusion.2
  285.4 0.0 copy-start.6
  285.4 48.8 %all_gather.16 = f32[512,384]{1,0:T(8,128)S(1)} all-gather(f32[8,384]{1,0:T(8,128)S(1)} %bitcast.82), channel_id=1, replica_groups=mesh['layer'=8,'row'=64] {'row'}, dimensions={0}, use_global_device_ids=true | all-gather | bytes 798720 | tf_op jit(solution)/shard_map/all_gather | solution.py:43
  334.2 0.0 copy-done.1
  334.2 0.0 copy-start.5
  334.2 0.7 fusion.5
  334.9 0.5 convolution_subtract_fusion.1
  335.5 48.9 %all_gather.17 = f32[512,384]{1,0:T(8,128)S(1)} all-gather(f32[8,384]{1,0:T(8,128)S(1)} %bitcast.84), channel_id=1, replica_groups=mesh['layer'=8,'row'=64] {'row'}, dimensions={0}, use_global_device_ids=true | all-gather | bytes 798720 | tf_op jit(solution)/shard_map/all_gather | solution.py:43
  384.3 0.7 fusion.4
  385.1 0.5 convolution_subtract_fusion
  385.6 48.7 %all_gather.18 = f32[512,384]{1,0:T(8,128)S(1)} all-gather(f32[8,384]{1,0:T(8,128)S(1)} %bitcast.86), channel_id=1, replica_groups=mesh['layer'=8,'row'=64] {'row'}, dimensions={0}, use_global_device_ids=true | all-gather | bytes 798720 | tf_op jit(solution)/shard_map/all_gather | solution.py:43
  434.3 0.0 copy-done.4
  434.3 0.5 convolution_bitcast_fusion.2
  434.8 23.6 %psum.15 = f32[8,384]{1,0:T(8,128)S(1)} all-reduce(f32[8,384]{1,0:T(8,128)S(1)} %convolution_bitcast_fusion.2), channel_id=1, replica_groups=mesh['layer'=8,'row'=64] {'layer'}, use_global_device_ids=true, to_apply=%region_1.0 | all-reduce | flops 3072 | bytes 24576 | tf_op jit(solution)/shard_map/psum | solution.py:46
  458.4 0.0 copy-done.6
  458.4 55.9 %all_gather.19 = f32[512,384]{1,0:T(8,128)S(1)} all-gather(f32[8,384]{1,0:T(8,128)S(1)} %sub.31), channel_id=1, replica_groups=mesh['layer'=8,'row'=64] {'row'}, dimensions={0}, use_global_device_ids=true | all-gather | bytes 798720 | tf_op jit(solution)/shard_map/all_gather | solution.py:49
  514.3 0.0 copy-done.5
  514.3 1.1 convolution_bitcast_fusion.1
  515.4 0.6 maximum_bitcast_fusion
  (2 shorter events, 0.0 us)
Async XLA Ops:
  7.2 10.3 %copy-start = (f32[1,1,4,512,256]{4,3,2,1,0:T(8,128)S(1)}, f32[1,1,4,512,256]{4,3,2,1,0:T(8,128)}, u32[]{:S(2)}) copy-start(f32[1,1,4,512,256]{4,3,2,1,0:T(8,128)} %param.12) | copy-start | bytes 6291460
  7.2 223.1 %all-reduce.2.cloned.1.call-start = ((), (), s32[]{:S(2)}) async-start(), calls=%async_computation | async-start | bytes 6291456 | tf_op jit(solution)/shard_map/psum | solution.py:31
  23.1 207.1 %copy-start.2 = (f32[1,4,8,512]{3,2,1,0:T(8,128)S(1)}, f32[1,4,8,512]{3,2,1,0:T(8,128)}, u32[]{:S(2)}) copy-start(f32[1,4,8,512]{3,2,1,0:T(8,128)} %param.15) | copy-start | bytes 196612
  23.1 261.7 %copy-start.3 = (f32[1,3,8,512]{3,2,1,0:T(8,128)S(1)}, f32[1,3,8,512]{3,2,1,0:T(8,128)}, u32[]{:S(2)}) copy-start(f32[1,3,8,512]{3,2,1,0:T(8,128)} %param.16) | copy-start | bytes 147460
  230.2 104.0 %copy-start.1 = (f32[4,512,384]{1,2,0:T(8,128)S(1)}, f32[4,512,384]{1,2,0:T(8,128)}, u32[]{:S(2)}) copy-start(f32[4,512,384]{1,2,0:T(8,128)} %all-reduce.2.cloned.1.call-done) | copy-start | bytes 9437188
  284.9 149.4 %copy-start.4 = (f32[1,8,512]{2,1,0:T(8,128)S(1)}, f32[1,8,512]{2,1,0:T(8,128)}, u32[]{:S(2)}) copy-start(f32[1,8,512]{2,1,0:T(8,128)} %param.17) | copy-start | bytes 49156
  285.4 173.0 %copy-start.6 = (f32[8,384]{1,0:T(8,128)S(1)}, f32[8,384]{1,0:T(8,128)}, u32[]{:S(2)}) copy-start(f32[8,384]{1,0:T(8,128)} %param.18) | copy-start | bytes 36868
  334.2 180.1 %copy-start.5 = (f32[8,512]{1,0:T(8,128)S(1)}, f32[8,512]{1,0:T(8,128)}, u32[]{:S(2)}) copy-start(f32[8,512]{1,0:T(8,128)} %param.19) | copy-start | bytes 49156
Sparse Core Ops, SparseCore 0:
  23.3 206.9 all-reduce.1
where the time goes:
time: 523 us
  blocking collectives  277 us (53%)
  waiting for transfers between devices  207 us (40%)
  matrix products  16 us (3%)
  between operations  14.8 us (3%)
  local copies, waits for them, and re-layouts  7.74 us (1%)
    psum x1, waiting for transfers between devices, body(): residual = lax.psum(own_rhs - coupled, 'row')  207 us
    all_gather x4, blocking collectives, body(): gathered = lax.all_gather(current, 'row', axis=0, tiled=True)  197 us
    all_gather x1, blocking collectives, body(): lax.all_gather(root_residual, 'row', axis=0, tiled=True)  55.9 us
    psum x1, blocking collectives, body(): root_sum = lax.psum(root_term, 'layer')  23.6 us
  transfers between devices with their start and end apart: 1, of which 1 were waited for; matrix products, arithmetic and copies ran while one was open for 0% of the time, Pallas kernels for 0%

commit v1 on v0

v1 whole, which is shorter than its diff:
```python
import functools

import jax
import jax.numpy as jnp
from jax import lax
from jax.experimental import pallas as pl
from jax.experimental.pallas import tpu as pltpu
from jax.sharding import Mesh, PartitionSpec as P

ROW = ("xl", "xh", "y", "c")
NT = (((1,), (1,)), ((), ()))


def split(a):
    high = a.astype(jnp.bfloat16)
    return high, (a - high.astype(jnp.float32)).astype(jnp.bfloat16)


def dot3(a, b, dims):
    mm = functools.partial(lax.dot_general, dimension_numbers=dims, preferred_element_type=jnp.float32)
    return mm(a[0], b[0]) + (mm(a[0], b[1]) + mm(a[1], b[0]))


def leaf_kernel(meta, rhs, inv, coupling, sep, out, xt_hi, xt_lo, place):
    step = pl.program_id(0)
    parent, core, block = meta[0], meta[1], meta[2]
    k = 2 * (step % 2) + jnp.where(step < 2, 1 - core, core)

    @pl.when(step == 0)
    def _():
        x = dot3(split(inv[0, 0]), split(rhs[0, 0]), (((1,), (0,)), ((), ())))
        xt_hi[...], xt_lo[...] = split(x.T)
        place[...] = jnp.zeros_like(place)

    keep = jnp.where(k >= parent, 1.0, 0.0)
    got = dot3((xt_hi[...], xt_lo[...]), split(coupling[0, 0, 0]), NT)
    half = got.shape[0] // 2
    out[0, 0, 0] = got[:half] * -keep
    out[0, 1, 0] = got[half:] * -keep
    place[pl.ds(pl.multiple_of(8 * (block % 16), 8), 8), :] = sep[0, 0]
    lanes = pl.ds(pl.multiple_of(128 * (block // 16), 128), 128)
    own = place[...].T
    out[0, 0, 0, :, lanes] += own[:half]
    out[0, 1, 0, :, lanes] += own[half:]


def leaves(meta, rhs, inv, coupling, sep):
    n, width = coupling.shape[2], coupling.shape[3]
    leaf, cols = rhs.shape[2], rhs.shape[3]

    def level(s, m):
        return 2 * (s % 2) + jnp.where(s < 2, 1 - m[1], m[1])

    return pl.pallas_call(
        leaf_kernel,
        grid_spec=pltpu.PrefetchScalarGridSpec(
            num_scalar_prefetch=1,
            grid=(n,),
            in_specs=[
                pl.BlockSpec((1, 1, leaf, cols), lambda s, m: (0, 0, 0, 0)),
                pl.BlockSpec((1, 1, leaf, leaf), lambda s, m: (0, 0, 0, 0)),
                pl.BlockSpec((1, 1, 1, width, leaf), lambda s, m: (0, 0, level(s, m), 0, 0)),
                pl.BlockSpec((1, 1, 8, cols), lambda s, m: (0, level(s, m), 0, 0)),
            ],
            out_specs=pl.BlockSpec((1, 2, 1, cols // 2, width), lambda s, m: (s // 2, 0, s % 2, 0, 0)),
            scratch_shapes=[
                pltpu.VMEM((cols, leaf), jnp.bfloat16),
                pltpu.VMEM((cols, leaf), jnp.bfloat16),
                pltpu.VMEM((128, cols), jnp.float32),
            ],
        ),
        out_shape=jax.ShapeDtypeStruct((2, 2, 2, cols // 2, width), jnp.float32),
        compiler_params=pltpu.CompilerParams(vmem_limit_bytes=24 * 2**20),
        name="leaves",
    )(meta, rhs, inv, coupling, sep)


def body(
    leaf_rhs,
    leaf_inverse,
    leaf_coupling,
    parent,
    sep_rhs,
    sep_inverse,
    sep_coupling,
    root_coupling,
    root_rhs,
    root_inverse,
):
    layer = lax.axis_index("layer")
    xh, c = lax.axis_index("xh"), lax.axis_index("c")
    xl, y = lax.axis_index("xl"), lax.axis_index("y")
    width, cols = leaf_coupling.shape[3], leaf_rhs.shape[3]
    part = cols // 16

    rr = jnp.pad(root_rhs, ((0, 0), (0, width - cols)))
    table = [
        [sep_inverse[0, 0], root_coupling[0], root_inverse],
        [sep_inverse[0, 1], sep_coupling[0, 0], rr],
        [sep_inverse[0, 2], sep_coupling[0, 1], rr],
        [sep_inverse[0, 3], sep_coupling[0, 2], rr],
    ]
    for_core = [jnp.stack([jnp.stack(table[2 * h + k]) for h in range(2)]) for k in range(2)]
    keep = jnp.where(c == 0, for_core[0], for_core[1])
    send = jnp.where(c == 0, for_core[1], for_core[0])
    came = lax.ppermute(send, "c", [(0, 1), (1, 0)])
    both = jnp.stack([jnp.where(c == 0, keep, came), jnp.where(c == 0, came, keep)], axis=2)
    keep = jnp.where(xh == 0, both[0], both[1])
    send = jnp.where(xh == 0, both[1], both[0])
    came = lax.ppermute(send, "xh", [(0, 1), (1, 0)])
    mine = jnp.stack([jnp.where(xh == 0, keep, came), jnp.where(xh == 0, came, keep)], axis=1)
    full = lax.all_gather(mine, ("xl", "y"), axis=0, tiled=False)
    full = full.reshape(2, 8, 3, 2, 16, width).transpose(2, 0, 3, 1, 4, 5).reshape(3, width, width)

    block = lax.axis_index(ROW)
    meta = jnp.stack([parent[0, 0], c, block]).astype(jnp.int32)
    update = leaves(meta, leaf_rhs, leaf_inverse, leaf_coupling, sep_rhs)
    res = update[1] + lax.ppermute(update[0], "c", [(0, 1), (1, 0)])
    res = res.reshape(4, cols // 2, width)
    res = lax.all_to_all(res, ("xl", "xh"), 0, 0).sum(0)
    res = res.reshape(8, part, width)
    res = lax.all_to_all(res, "y", 0, 0).sum(0)

    mm = functools.partial(lax.dot_general, dimension_numbers=NT, precision=lax.Precision.HIGH)
    hop = functools.partial(lax.ppermute, axis_name=("xh", "c"))
    rr_own = lax.dynamic_slice_in_dim(full[2], (xl * 8 + y) * part, part, 1).T
    rr_cols = hop(rr_own, perm=[(1, 0)]) * jnp.where(layer == 0, 1.0, 0.0)
    sol = mm(res, full[0])
    for k in range(3):
        sol = sol - mm(hop(sol, perm=[(k, k + 1)]), full[1])
    term = mm(rr_cols - mm(hop(sol, perm=[(3, 0)]), full[1]), full[2])

    out = jnp.concatenate([sol.T.reshape(64, 8, part), term.T.reshape(64, 8, part)], axis=2)
    out = lax.all_to_all(out, ROW, 0, 0).reshape(2, 2, 8, 2, 8, 2, part)
    out = out.transpose(1, 3, 5, 4, 0, 2, 6).reshape(4, 2, 8, cols)
    sep_out = out[:, 0][None]
    term = jnp.broadcast_to(out[0, 1][None], (8, 8, cols))
    root_out = lax.all_to_all(term, "layer", 0, 0).sum(0)
    return (sep_out, root_out)


def solution(mesh):
    layers, rows = mesh.devices.shape
    fine = Mesh(mesh.devices.reshape(layers, 2, 2, 8, 2), ("layer",) + ROW)
    return jax.shard_map(
        body,
        mesh=fine,
        in_specs=(
            P("layer", ROW, None, None),
            P("layer", ROW, None, None),
            P("layer", ROW, None, None, None),
            P("layer", ROW),
            P("layer", None, ROW, None),
            P("layer", None, ROW, None),
            P("layer", None, ROW, None),
            P("layer", ROW, None),
            P(ROW, None),
            P(ROW, None),
        ),
        out_specs=(P("layer", None, ROW, None), P(ROW, None)),
        check_vma=False,
    )
```

time: 523 us -> 186 us (0.36)
  blocking collectives: 277 us -> 61.5 us
  waiting for transfers between devices: 207 us -> 63.8 us
  starting transfers between devices: 0.04 us -> 26.1 us
  matrix products: 16 us -> 3.19 us
    all_gather x5 -> x0, blocking collectives: 253 us -> none  [the longest x4 197 us: body(): gathered = lax.all_gather(current, 'row', axis=0, tiled=True)]
    psum x1 -> x0, waiting for transfers between devices: 207 us -> none  [body(): residual = lax.psum(own_rhs - coupled, 'row')]
    all_to_all x0 -> x3, blocking collectives: none -> 61.5 us  [the longest x1 25 us: body(): res = lax.all_to_all(res, ('xl', 'xh'), 0, 0).sum(0)]
    all_gather x0 -> x1, waiting for transfers between devices: none -> 43.1 us  [body(): full = lax.all_gather(mine, ('xl', 'y'), axis=0, tiled=False)]
    psum x1 -> x0, blocking collectives: 23.6 us -> none  [body(): root_sum = lax.psum(root_term, 'layer')]
    ppermute x0 -> x8, starting transfers between devices: none -> 19 us  [the longest x1 8.79 us: body(): came = lax.ppermute(send, 'c', [(0, 1), (1, 0)])]
    ppermute x0 -> x8, waiting for transfers between devices: none -> 13.9 us  [the longest x3 5.76 us: body(): sol = sol - mm(hop(sol, perm=[(k, k + 1)]), full[1])]
    dot_general x11 -> x6, matrix products: 16 us -> 3.19 us  [the longest x3 1.59 us: body(): sol = sol - mm(hop(sol, perm=[(k, k + 1)]), full[1])]
  transfers between devices with their start and end apart: 1 -> 10, of which waited for: 1 -> 8; matrix products, arithmetic and copies ran while one was open for 0% -> 1% of each run, Pallas kernels for 0% -> 2%
where the time goes in v1:
time: 186 us; the launch traced here: 185 us
  waiting for transfers between devices  63.8 us (34%)
  blocking collectives  61.5 us (33%)
  starting transfers between devices  26.1 us (14%)
  between operations  15 us (8%)
  local copies, waits for them, and re-layouts  8.37 us (4%)
  other arithmetic  3.75 us (2%)
  Pallas kernels  3.55 us (2%)
  matrix products  3.19 us (2%)
    all_gather x1, waiting for transfers between devices, body(): full = lax.all_gather(mine, ('xl', 'y'), axis=0, tiled=False)  43.1 us
    all_to_all x1, blocking collectives, body(): res = lax.all_to_all(res, ('xl', 'xh'), 0, 0).sum(0)  25 us
    all_to_all x1, blocking collectives, body(): out = lax.all_to_all(out, ROW, 0, 0).reshape(2, 2, 8, 2, 8, 2, part)  20.5 us
    all_to_all x1, blocking collectives, body(): res = lax.all_to_all(res, 'y', 0, 0).sum(0)  16 us
    ppermute x1, starting transfers between devices, body(): came = lax.ppermute(send, 'c', [(0, 1), (1, 0)])  8.79 us
    all_to_all x1, starting transfers between devices, body(): root_out = lax.all_to_all(term, 'layer', 0, 0).sum(0)  7.1 us
    all_to_all x1, waiting for transfers between devices, body(): root_out = lax.all_to_all(term, 'layer', 0, 0).sum(0)  6.83 us
    ppermute x3, waiting for transfers between devices, body(): sol = sol - mm(hop(sol, perm=[(k, k + 1)]), full[1])  5.76 us
  transfers between devices with their start and end apart: 10, of which 8 were waited for; matrix products, arithmetic and copies ran while one was open for 1% of the time, Pallas kernels for 2%

profile of v1, /device:TPU:1, one launch (start us, length us, event | category | flops | bytes accessed | tf_op | source)
XLA Modules:
  0.0 185.3 jit_solution(2199180812671681465)
XLA Ops:
  7.3 0.9 slice_bitcast_fusion.9
  8.2 0.8 slice_bitcast_fusion.7
  8.9 0.7 pad_bitcast_fusion
  9.6 0.7 fusion.6
  10.4 8.8 %collective-permute-start.1 = (f32[2,3,8,512]{3,2,1,0:T(8,128)S(1)}, f32[2,3,8,512]{3,2,1,0:T(8,128)S(1)}, u32[]{:S(2)}, u32[]{:S(2)}) collective-permute-start(f32[2,3,8,512]{3,2,1,0:T(8,128)S(1)} %fusion.4), channel_id=1, source_target_pairs={{0,1},{1,0},{2,3},{3,2},{4,5},{5,4},{6,7},{7,6},{8,9},{9,8},{10,11... | collective-permute-start | bytes 294920 | tf_op jit(solution)/shard_map/ppermute | solution.py:106
  19.2 0.9 collective-permute-done.1
  20.2 1.9 %collective-permute-start.2 = (f32[3,2,8,512]{3,2,1,0:T(8,128)S(1)}, f32[3,2,8,512]{3,2,1,0:T(8,128)S(1)}, u32[]{:S(2)}, u32[]{:S(2)}) collective-permute-start(f32[3,2,8,512]{3,2,1,0:T(8,128)S(1)} %select_bitcast_fusion), channel_id=1, source_target_pairs={{0,16},{16,0},{1,17},{17,1},{2,18},{18,2},{3,19},{19,3},{4,20},{20... | collective-permute-start | bytes 294920 | tf_op jit(solution)/shard_map/ppermute | solution.py:110
  22.1 4.0 %collective-permute-done.2 = f32[3,2,8,512]{3,2,1,0:T(8,128)S(1)} collective-permute-done((f32[3,2,8,512]{3,2,1,0:T(8,128)S(1)}, f32[3,2,8,512]{3,2,1,0:T(8,128)S(1)}, u32[]{:S(2)}, u32[]{:S(2)}) %collective-permute-start.2) | collective-permute-done | bytes 98336 | tf_op jit(solution)/shard_map/ppermute | solution.py:110
  26.1 0.7 pad_maximum_fusion.1
  27.6 3.5 %leaves.1 = f32[2,2,2,192,512]{4,3,2,1,0:T(8,128)S(1)} custom-call(s32[3]{0:T(128)S(1)} %pad_add_fusion.meta, f32[1,1,256,384]{3,2,1,0:T(8,128)S(1)} %copy-done.1, f32[1,1,256,256]{3,2,1,0:T(8,128)S(1)} %copy-done.2, f32[1,1,4,512,256]{4,3,2,1,0:T(8,128)S(1)} %copy-done, f32[1,4,8,384]{3,2,1,0:T(8,128)S(1)} %copy-done.3), custom_call_target="tpu_custom_call" | custom-call | tf_op jit(solution)/shard_map/leaves/pallas_call | solution.py:54
  31.3 3.1 %collective-permute-start = (f32[2,2,192,512]{3,2,1,0:T(8,128)S(1)}, f32[2,2,192,512]{3,2,1,0:T(8,128)S(1)}, u32[]{:S(2)}, u32[]{:S(2)}) collective-permute-start(f32[2,2,192,512]{3,2,1,0:T(8,128)S(1)} %slice_bitcast_fusion), channel_id=1, source_target_pairs={{0,1},{1,0},{2,3},{3,2},{4,5},{5,4},{6,7},{7,6},{8,9},{9,8},{10,11... | collective-permute-start | bytes 4718600 | tf_op jit(solution)/shard_map/ppermute | solution.py:118
  34.4 3.0 %collective-permute-done = f32[2,2,192,512]{3,2,1,0:T(8,128)S(1)} collective-permute-done((f32[2,2,192,512]{3,2,1,0:T(8,128)S(1)}, f32[2,2,192,512]{3,2,1,0:T(8,128)S(1)}, u32[]{:S(2)}, u32[]{:S(2)}) %collective-permute-start) | collective-permute-done | bytes 1572896 | tf_op jit(solution)/shard_map/ppermute | solution.py:118
  37.4 0.3 fusion
  37.8 25.0 %all_to_all.20 = f32[4,192,512]{2,1,0:T(8,128)S(1)} all-to-all(f32[4,192,512]{2,1,0:T(8,128)S(1)} %bitcast.93), channel_id=1, replica_groups=mesh['layer'=8,'xl'=2,'xh'=2,'y'=8,'c'=2] {'xl','xh'}, dimensions={0} | all-to-all | bytes 3145728 | tf_op jit(solution)/shard_map/all_to_all | solution.py:120
  62.8 0.2 reduce_sum.27
  62.9 16.0 %all_to_all.21 = f32[8,24,512]{2,1,0:T(8,128)S(1)} all-to-all(f32[8,24,512]{2,1,0:T(8,128)S(1)} %bitcast.99), channel_id=1, replica_groups=mesh['layer'=8,'xl'=2,'xh'=2,'y'=8,'c'=2] {'y'}, dimensions={0} | all-to-all | bytes 786432 | tf_op jit(solution)/shard_map/all_to_all | solution.py:122
  79.0 43.1 %all-gather.3.cloned.1.call-done = f32[48,2,2,8,512]{4,3,2,1,0:T(8,128)} async-done(((f32[3,2,2,8,512]{4,3,2,1,0:T(8,128)}), f32[48,2,2,8,512]{4,3,2,1,0:T(8,128)}) %all-gather.3.cloned.1.call-update) | async-done | bytes 3145744 | tf_op jit(solution)/shard_map/all_gather | solution.py:112
  122.1 2.2 %fusion.14 = (f32[1,2,2,8,16,512]{5,4,2,0,3,1:T(8,128)S(1)}, f32[1,2,2,8,16,512]{5,4,2,0,3,1:T(8,128)S(1)}, f32[1,2,2,8,16,512]{5,4,2,0,3,1:T(8,128)S(1)}) fusion(f32[3,2,2,8,16,512]{5,4,2,0,3,1:T(8,128)} %bitcast.97), kind=kLoop, calls=%fused_computation.48 | loop fusion | bytes 6291456 | tf_op jit(solution)/shard_map/slice | solution.py:130
  124.3 0.5 fusion.15
  124.8 1.3 collective-permute-start.3
  126.2 4.6 %collective-permute-done.3 = f32[24,512]{1,0:T(8,128)S(1)} collective-permute-done((f32[24,512]{1,0:T(8,128)S(1)}, f32[24,512]{1,0:T(8,128)S(1)}, u32[]{:S(2)}, u32[]{:S(2)}) %collective-permute-start.3) | collective-permute-done | bytes 49184 | tf_op jit(solution)/shard_map/ppermute | solution.py:130
  130.8 0.5 convolution_subtract_fusion.2
  131.4 1.3 collective-permute-start.4
  132.7 1.2 collective-permute-done.4
  133.8 0.5 convolution_subtract_fusion.1
  134.4 0.7 collective-permute-start.5
  135.2 0.5 convolution_subtract_fusion
  135.7 0.7 collective-permute-start.7
  136.4 0.1 constant_dynamic-slice_fusion
  136.6 1.3 collective-permute-start.6
  137.9 0.1 copy.47
  138.1 0.5 fusion.16
  138.6 0.2 collective-permute-done.6
  138.8 0.6 fusion.9
  139.4 0.1 pad_maximum_fusion
  139.5 0.2 reshape.46
  139.8 20.5 %all_to_all.22 = f32[64,1,384]{2,1,0:T(1,128)S(1)} all-to-all(f32[64,1,384]{2,1,0:T(1,128)S(1)} %reshape.46), channel_id=1, replica_groups=mesh['layer'=8,'xl'=2,'xh'=2,'y'=8,'c'=2] {'xl','xh','y','c'}, dimensions={0} | all-to-all | bytes 196608 | tf_op jit(solution)/shard_map/all_to_all | solution.py:134
  160.2 0.5 broadcast.5
  160.8 0.9 reduce
  161.6 0.1 reshape.47
  161.8 0.3 reshape.41
  162.1 0.3 copy.51
  162.4 0.3 reshape.42
  162.7 0.6 broadcast_in_dim.8
  163.3 7.1 %all-to-all-start.3 = ((f32[8,8,384]{2,1,0:T(8,128)}), f32[8,8,384]{2,1,0:T(8,128)S(1)}, u32[]{:S(2)}, u32[]{:S(2)}) async-start(f32[8,8,384]{2,1,0:T(8,128)} %broadcast_in_dim.8), calls=%async_computation.3 | async-start | bytes 196608 | tf_op jit(solution)/shard_map/all_to_all | solution.py:138
  170.4 0.6 slice_bitcast_fusion.2
  171.0 6.8 %all-to-all-done.3 = f32[8,8,384]{2,1,0:T(8,128)S(1)} async-done(((f32[8,8,384]{2,1,0:T(8,128)}), f32[8,8,384]{2,1,0:T(8,128)S(1)}, u32[]{:S(2)}, u32[]{:S(2)}) %all-to-all-start.3) | async-done | bytes 98336 | tf_op jit(solution)/shard_map/all_to_all | solution.py:138
  177.9 0.6 reduce_sum.29
  (24 shorter events, 0.7 us)
Async XLA Ops:
  7.2 20.4 %copy-start.1 = (f32[1,1,256,384]{3,2,1,0:T(8,128)S(1)}, f32[1,1,256,384]{3,2,1,0:T(8,128)}, u32[]{:S(2)}) copy-start(f32[1,1,256,384]{3,2,1,0:T(8,128)} %rhs.2) | copy-start | bytes 1179652
  7.2 20.4 %copy-start.2 = (f32[1,1,256,256]{3,2,1,0:T(8,128)S(1)}, f32[1,1,256,256]{3,2,1,0:T(8,128)}, u32[]{:S(2)}) copy-start(f32[1,1,256,256]{3,2,1,0:T(8,128)} %inv.1) | copy-start | bytes 786436
  7.2 20.4 %copy-start = (f32[1,1,4,512,256]{4,3,2,1,0:T(8,128)S(1)}, f32[1,1,4,512,256]{4,3,2,1,0:T(8,128)}, u32[]{:S(2)}) copy-start(f32[1,1,4,512,256]{4,3,2,1,0:T(8,128)} %coupling.1) | copy-start | bytes 6291460
  7.2 20.4 %copy-start.3 = (f32[1,4,8,384]{3,2,1,0:T(8,128)S(1)}, f32[1,4,8,384]{3,2,1,0:T(8,128)}, u32[]{:S(2)}) copy-start(f32[1,4,8,384]{3,2,1,0:T(8,128)} %sep.1) | copy-start | bytes 147460
  7.2 114.8 %all-gather.3.cloned.1.call-start = ((), (), s32[]{:S(2)}) async-start(), calls=%async_computation.4 | async-start | bytes 3342336 | tf_op jit(solution)/shard_map/all_gather | solution.py:112
  10.4 9.7 %collective-permute-start.1 = (f32[2,3,8,512]{3,2,1,0:T(8,128)S(1)}, f32[2,3,8,512]{3,2,1,0:T(8,128)S(1)}, u32[]{:S(2)}, u32[]{:S(2)}) collective-permute-start(f32[2,3,8,512]{3,2,1,0:T(8,128)S(1)} %fusion.4), channel_id=1, source_target_pairs={{0,1},{1,0},{2,3},{3,2},{4,5},{5,4},{6,7},{7,6},{8,9},{9,8},{10,11... | collective-permute-start | bytes 294920 | tf_op jit(solution)/shard_map/ppermute | solution.py:106
  20.2 5.9 %collective-permute-start.2 = (f32[3,2,8,512]{3,2,1,0:T(8,128)S(1)}, f32[3,2,8,512]{3,2,1,0:T(8,128)S(1)}, u32[]{:S(2)}, u32[]{:S(2)}) collective-permute-start(f32[3,2,8,512]{3,2,1,0:T(8,128)S(1)} %select_bitcast_fusion), channel_id=1, source_target_pairs={{0,16},{16,0},{1,17},{17,1},{2,18},{18,2},{3,19},{19,3},{4,20},{20... | collective-permute-start | bytes 294920 | tf_op jit(solution)/shard_map/ppermute | solution.py:110
  31.3 6.1 %collective-permute-start = (f32[2,2,192,512]{3,2,1,0:T(8,128)S(1)}, f32[2,2,192,512]{3,2,1,0:T(8,128)S(1)}, u32[]{:S(2)}, u32[]{:S(2)}) collective-permute-start(f32[2,2,192,512]{3,2,1,0:T(8,128)S(1)} %slice_bitcast_fusion), channel_id=1, source_target_pairs={{0,1},{1,0},{2,3},{3,2},{4,5},{5,4},{6,7},{7,6},{8,9},{9,8},{10,11... | collective-permute-start | bytes 4718600 | tf_op jit(solution)/shard_map/ppermute | solution.py:118
  124.8 6.0 %collective-permute-start.3 = (f32[24,512]{1,0:T(8,128)S(1)}, f32[24,512]{1,0:T(8,128)S(1)}, u32[]{:S(2)}, u32[]{:S(2)}) collective-permute-start(f32[24,512]{1,0:T(8,128)S(1)} %fusion.15), channel_id=1, source_target_pairs={{0,1},{2,3},{4,5},{6,7},{8,9},{10,11},{12,13},{14,15},{32,33},{34,... | collective-permute-start | bytes 147464 | tf_op jit(solution)/shard_map/ppermute | solution.py:130
  131.4 2.5 %collective-permute-start.4 = (f32[24,512]{1,0:T(8,128)S(1)}, f32[24,512]{1,0:T(8,128)S(1)}, u32[]{:S(2)}, u32[]{:S(2)}) collective-permute-start(f32[24,512]{1,0:T(8,128)S(1)} %convolution_subtract_fusion.2), channel_id=1, source_target_pairs={{1,16},{3,18},{5,20},{7,22},{9,24},{11,26},{13,28},{15,30},{33,48}... | collective-permute-start | bytes 147464 | tf_op jit(solution)/shard_map/ppermute | solution.py:130
  134.4 0.8 collective-permute-start.5
  135.7 2.3 %collective-permute-start.7 = (f32[24,512]{1,0:T(8,128)S(1)}, f32[24,512]{1,0:T(8,128)S(1)}, u32[]{:S(2)}, u32[]{:S(2)}) collective-permute-start(f32[24,512]{1,0:T(8,128)S(1)} %convolution_subtract_fusion), channel_id=1, source_target_pairs={{17,0},{19,2},{21,4},{23,6},{25,8},{27,10},{29,12},{31,14},{49,32}... | collective-permute-start | bytes 147464 | tf_op jit(solution)/shard_map/ppermute | solution.py:131
  136.6 2.2 %collective-permute-start.6 = (f32[24,512]{1,0:T(8,128)S(1)}, f32[24,512]{1,0:T(8,128)S(1)}, u32[]{:S(2)}, u32[]{:S(2)}) collective-permute-start(f32[24,512]{1,0:T(8,128)S(1)} %bitcast.102), channel_id=1, source_target_pairs={{1,0},{3,2},{5,4},{7,6},{9,8},{11,10},{13,12},{15,14},{33,32},{35,... | collective-permute-start | bytes 147464 | tf_op jit(solution)/shard_map/ppermute | solution.py:127
  163.3 14.6 %all-to-all-start.3 = ((f32[8,8,384]{2,1,0:T(8,128)}), f32[8,8,384]{2,1,0:T(8,128)S(1)}, u32[]{:S(2)}, u32[]{:S(2)}) async-start(f32[8,8,384]{2,1,0:T(8,128)} %broadcast_in_dim.8), calls=%async_computation.3 | async-start | bytes 196608 | tf_op jit(solution)/shard_map/all_to_all | solution.py:138
Sparse Core Ops, SparseCore 0:
  27.0 95.0 all-gather.2

commit v2 on v1

v2 whole, which is shorter than its diff:
```python
import functools

import jax
import jax.numpy as jnp
from jax import lax
from jax.experimental import pallas as pl
from jax.experimental.pallas import tpu as pltpu
from jax.sharding import Mesh, PartitionSpec as P

ROW = ("x", "y", "c")
NX, NY, NC = 4, 8, 2
NT = (((1,), (1,)), ((), ()))
NN = (((1,), (0,)), ((), ()))
VMEM = pl.BlockSpec(memory_space=pltpu.VMEM)


def split(a):
    high = a.astype(jnp.bfloat16)
    return high, (a - high.astype(jnp.float32)).astype(jnp.bfloat16)


def dot3(a, b, dims):
    mm = functools.partial(lax.dot_general, dimension_numbers=dims, preferred_element_type=jnp.float32)
    return mm(a[0], b[0]) + (mm(a[0], b[1]) + mm(a[1], b[0]))


def by_tiles(ref, part):
    tiles, rows, _ = ref.shape

    def column(tile):
        return jnp.concatenate(
            [
                ref[tile, pl.ds(base + t, 8, stride=part), :]
                for base in range(0, rows, 8 * part)
                for t in range(part)
            ],
            axis=0,
        )

    return jnp.concatenate([column(tile) for tile in range(tiles)], axis=1)


def leaf_kernel(part, meta, rhs, inv, coupling, sep, out, xt, xt_hi, xt_lo, place, own):
    k = pl.program_id(0)
    parent, core, block = meta[0], meta[1], meta[2]

    @pl.when(k == 0)
    def _():
        solved = dot3(split(inv[0, 0]), split(rhs[0, 0]), NN).T
        for tile in range(xt.shape[0]):
            xt[tile] = solved[:, 128 * tile : 128 * (tile + 1)]
        xt_hi[...], xt_lo[...] = split(by_tiles(xt, part))
        place[...] = jnp.zeros_like(place)

    keep = jnp.where(k >= parent, 1.0, 0.0)
    got = dot3((xt_hi[...], xt_lo[...]), split(coupling[0, 0, 0]), NT) * -keep
    place[pl.ds(pl.multiple_of(8 * (block % 16), 8), 8), :] = sep[0, 0]
    own[0] = place[...].T
    mine = by_tiles(own, part)
    group = 8 * part
    for half in range(NC):
        slot = jnp.where(core == half, 1, 0)
        for x in range(NX):
            rows = slice((half * NX + x) * group, (half * NX + x + 1) * group)
            for tile in range(out.shape[3]):
                out[slot, x, 0, tile] = got[rows, 128 * tile : 128 * (tile + 1)]
            out[slot, x, 0, block // 16] += mine[rows]


def leaves(meta, rhs, inv, coupling, sep):
    n, width = coupling.shape[2], coupling.shape[3]
    leaf, cols = rhs.shape[2], rhs.shape[3]
    part = cols // 64
    return pl.pallas_call(
        functools.partial(leaf_kernel, part),
        grid_spec=pltpu.PrefetchScalarGridSpec(
            num_scalar_prefetch=1,
            grid=(n,),
            in_specs=[
                pl.BlockSpec((1, 1, leaf, cols), lambda k, m: (0, 0, 0, 0)),
                pl.BlockSpec((1, 1, leaf, leaf), lambda k, m: (0, 0, 0, 0)),
                pl.BlockSpec((1, 1, 1, width, leaf), lambda k, m: (0, 0, k, 0, 0)),
                pl.BlockSpec((1, 1, 8, cols), lambda k, m: (0, k, 0, 0)),
            ],
            out_specs=pl.BlockSpec(
                (NC, NX, 1, width // 128, 8 * part, 128), lambda k, m: (0, 0, k, 0, 0, 0)
            ),
            scratch_shapes=[
                pltpu.VMEM((leaf // 128, cols, 128), jnp.float32),
                pltpu.VMEM((cols, leaf), jnp.bfloat16),
                pltpu.VMEM((cols, leaf), jnp.bfloat16),
                pltpu.VMEM((128, cols), jnp.float32),
                pltpu.VMEM((1, cols, 128), jnp.float32),
            ],
        ),
        out_shape=jax.ShapeDtypeStruct((NC, NX, n, width // 128, 8 * part, 128), jnp.float32),
        compiler_params=pltpu.CompilerParams(vmem_limit_bytes=24 * 2**20),
        name="leaves",
    )(meta, rhs, inv, coupling, sep)


def sum_kernel(parts, out):
    count = out.shape[1]
    for s in range(8):
        rows = pl.ds(s, count, stride=8)
        out[s] = (parts[0, rows, :] + parts[1, rows, :]) + (parts[2, rows, :] + parts[3, rows, :])


def chain_kernel(part, meta, parts, root_inverse, weights, out, own, full, wide, sems):
    x = meta[0]
    n = full.shape[0]
    copies = []
    for m in range(n):
        copies.append([])
        for back in range(NX):
            rows = pl.multiple_of(((x + NX - back) % NX) * 16, 16)
            copy = pltpu.make_async_copy(
                weights.at[:, back, m], full.at[m, pl.ds(rows, 16)], sems.at[m, back]
            )
            copy.start()
            copies[-1].append(copy)

    def matrix(m):
        for copy in copies[m]:
            copy.wait()
        return full[m].reshape(full.shape[1] * 8, full.shape[3])

    res = parts[0]
    for p in range(1, parts.shape[0]):
        res = res + parts[p]
    tiles = res.shape[0] // (4 * part)

    def residual(k):
        starts = [part * (tiles * k + tile) for tile in range(tiles)]
        return jnp.concatenate([res[at : at + part] for at in starts], axis=1)

    wide[...] = jnp.zeros_like(wide)
    sol = None
    for k in range(4):
        now = dot3(split(residual(k)), split(matrix(k)), NT)
        if k > 0:
            now = now - dot3(split(sol), split(matrix(3 + k)), NT)
        sol = now
        wide[part * k : part * (k + 1), :] = sol
    term = dot3(split(sol), split(matrix(7)), NT)
    wide[4 * part : 5 * part, :] = dot3(split(term), split(matrix(8)), NT)
    back = wide[...].T
    out[...] = back.reshape(out.shape)
    own[...] = dot3(split(root_inverse[...]), split(matrix(9)), NN)[:, : own.shape[1]]


def body(
    leaf_rhs,
    leaf_inverse,
    leaf_coupling,
    parent,
    sep_rhs,
    sep_inverse,
    sep_coupling,
    root_coupling,
    root_rhs,
    root_inverse,
):
    x, c = lax.axis_index("x"), lax.axis_index("c")
    width, cols = leaf_coupling.shape[3], leaf_rhs.shape[3]
    part = cols // 64

    pack = jnp.concatenate(
        [
            sep_inverse[0],
            sep_coupling[0],
            root_coupling,
            root_inverse[None],
            jnp.pad(root_rhs, ((0, 0), (0, width - cols)))[None],
        ]
    )
    ring = [pack] + [
        lax.ppermute(pack, "x", [(i, (i + j) % NX) for i in range(NX)]) for j in range(1, NX)
    ]
    weights = lax.all_gather(jnp.stack(ring), ("y", "c"))

    meta = jnp.stack([parent[0, 0], c, lax.axis_index(ROW)]).astype(jnp.int32)
    update = leaves(meta, leaf_rhs, leaf_inverse, leaf_coupling, sep_rhs)
    res = update[1] + lax.ppermute(update[0], "c", [(0, 1), (1, 0)])
    tall = width // 128 * part
    res = lax.all_to_all(res.reshape(NX, 4 * 8 * tall, 128), "x", 0, 0)
    res = pl.pallas_call(
        sum_kernel,
        in_specs=[VMEM],
        out_specs=VMEM,
        out_shape=jax.ShapeDtypeStruct((8, 4 * tall, 128), jnp.float32),
        compiler_params=pltpu.CompilerParams(vmem_limit_bytes=16 * 2**20),
        name="sum_x",
    )(res)
    res = lax.all_to_all(res, "y", 0, 0)

    out, own = pl.pallas_call(
        functools.partial(chain_kernel, part),
        in_specs=[pl.BlockSpec(memory_space=pltpu.SMEM), VMEM, VMEM, pl.BlockSpec(memory_space=pl.ANY)],
        out_specs=[VMEM, VMEM],
        out_shape=[
            jax.ShapeDtypeStruct((64, 8, 128), jnp.float32),
            jax.ShapeDtypeStruct((8, cols), jnp.float32),
        ],
        scratch_shapes=[
            pltpu.VMEM((10, 64, 8, width), jnp.float32),
            pltpu.VMEM((128, width), jnp.float32),
            pltpu.SemaphoreType.DMA((10, NX)),
        ],
        compiler_params=pltpu.CompilerParams(vmem_limit_bytes=40 * 2**20),
        name="chain",
    )(x.reshape(1).astype(jnp.int32), res, root_inverse, weights)

    out = lax.all_to_all(out, ROW, 0, 0)[:, :, : 5 * part]
    out = out.reshape(NX, NY, NC, 8, 5, part).transpose(4, 3, 2, 0, 1, 5).reshape(5, 8, cols)
    term = jnp.broadcast_to(out[4][None], (8, 8, cols))
    root_out = own - lax.all_to_all(term, "layer", 0, 0).sum(0)
    return (out[:4][None], root_out)


def solution(mesh):
    fine = Mesh(mesh.devices.reshape(-1, NX, NY, NC), ("layer",) + ROW)
    return jax.shard_map(
        body,
        mesh=fine,
        in_specs=(
            P("layer", ROW, None, None),
            P("layer", ROW, None, None),
            P("layer", ROW, None, None, None),
            P("layer", ROW),
            P("layer", None, ROW, None),
            P("layer", None, ROW, None),
            P("layer", None, ROW, None),
            P("layer", ROW, None),
            P(ROW, None),
            P(ROW, None),
        ),
        out_specs=(P("layer", None, ROW, None), P(ROW, None)),
        check_vma=False,
    )
```

time: 186 us -> 165 us (0.89)
  waiting for transfers between devices: 63.8 us -> 31.4 us
  local copies, waits for them, and re-layouts: 8.37 us -> 15.2 us
  Pallas kernels: 3.55 us -> 10.1 us
  blocking collectives: 61.5 us -> 64.8 us
  matrix products: 3.19 us -> 0 us
  other arithmetic: 3.75 us -> 1.82 us
    all_gather x1, waiting for transfers between devices: 43.1 us -> 20.6 us  [body(): weights = lax.all_gather(jnp.stack(ring), ('y', 'c'))]
    unnamed x11 -> x16, local copies, waits for them, and re-layouts: 0.5 us -> 9.16 us
    ppermute x7 -> x3, waiting for transfers between devices: 10.9 us -> 3.28 us  [body(): lax.ppermute(pack, 'x', [(i, (i + j) % NX) for i in range(NX)])]
    pallas_call x1 -> x3, Pallas kernels: 3.55 us -> 10.1 us  [the longest x1 6.36 us: body(): pl.pallas_call(functools.partial(chain_kernel, part), in_specs=[pl.BlockS...]
    ppermute x7 -> x3, starting transfers between devices: 15.9 us -> 11.4 us  [body(): lax.ppermute(pack, 'x', [(i, (i + j) % NX) for i in range(NX)])]
    ppermute x1, starting transfers between devices: 3.1 us -> 7.23 us  [body(): res = update[1] + lax.ppermute(update[0], 'c', [(0, 1), (1, 0)])]
    all_to_all x3, blocking collectives: 61.5 us -> 64.8 us  [the longest x1 23.2 us: body(): res = lax.all_to_all(res.reshape(NX, 4 * 8 * tall, 128), 'x', 0, 0)]
    dot_general x6 -> x0, matrix products: 3.19 us -> none  [the longest x3 1.59 us: body(): sol = sol - mm(hop(sol, perm=[(k, k + 1)]), full[1])]
  transfers between devices with their start and end apart: 10 -> 6, of which waited for: 8 -> 5; matrix products, arithmetic and copies ran while one was open for 1% -> 2% of each run, Pallas kernels for 2% -> 2%
where the time goes in v2:
time: 165 us; the launch traced here: 164 us
  blocking collectives  64.8 us (39%)
  waiting for transfers between devices  31.4 us (19%)
  starting transfers between devices  25.7 us (16%)
  local copies, waits for them, and re-layouts  15.2 us (9%)
  between operations  14.8 us (9%)
  Pallas kernels  10.1 us (6%)
  other arithmetic  1.82 us (1%)
    all_to_all x1, blocking collectives, body(): res = lax.all_to_all(res.reshape(NX, 4 * 8 * tall, 128), 'x', 0, 0)  23.2 us
    all_to_all x1, blocking collectives, body(): res = lax.all_to_all(res, 'y', 0, 0)  22.1 us
    all_gather x1, waiting for transfers between devices, body(): weights = lax.all_gather(jnp.stack(ring), ('y', 'c'))  20.6 us
    all_to_all x1, blocking collectives, body(): out = lax.all_to_all(out, ROW, 0, 0)[:, :, :5 * part]  19.5 us
    ppermute x3, starting transfers between devices, body(): lax.ppermute(pack, 'x', [(i, (i + j) % NX) for i in range(NX)])  11.4 us
    unnamed x16, local copies, waits for them, and re-layouts  9.16 us
    ppermute x1, starting transfers between devices, body(): res = update[1] + lax.ppermute(update[0], 'c', [(0, 1), (1, 0)])  7.23 us
    all_to_all x1, starting transfers between devices, body(): root_out = own - lax.all_to_all(term, 'layer', 0, 0).sum(0)  7.1 us
  transfers between devices with their start and end apart: 6, of which 5 were waited for; matrix products, arithmetic and copies ran while one was open for 2% of the time, Pallas kernels for 2%

profile of v2, /device:TPU:1, one launch (start us, length us, event | category | flops | bytes accessed | tf_op | source)
XLA Modules:
  0.0 163.8 jit_solution(15070771953323808000)
XLA Ops:
  7.2 0.0 copy-start.1
  7.2 0.0 copy-start.5
  7.2 0.0 all-gather.3.cloned.1.call-start
  7.2 1.0 bitcast_dynamic-update-slice_fusion
  8.2 0.8 bitcast_dynamic-update-slice_fusion.1
  9.0 0.7 constant_dynamic-update-slice_fusion
  9.7 0.7 bitcast_dynamic-update-slice_fusion.3
  10.5 0.7 bitcast_dynamic-update-slice_fusion.2
  11.2 3.9 %collective-permute-start.1 = (f32[10,8,512]{2,1,0:T(8,128)S(1)}, f32[10,8,512]{2,1,0:T(8,128)S(1)}, u32[]{:S(2)}, u32[]{:S(2)}) collective-permute-start(f32[10,8,512]{2,1,0:T(8,128)S(1)} %bitcast_dynamic-update-slice_fusion.2), channel_id=1, source_target_pairs={{0,16},{16,32},{32,48},{48,0},{1,17},{17,33},{33,49},{49,1},{2,18}... | collective-permute-start | bytes 491528 | tf_op jit(solution)/shard_map/ppermute | solution.py:178
  15.1 4.4 %collective-permute-start.2 = (f32[10,8,512]{2,1,0:T(8,128)S(1)}, f32[10,8,512]{2,1,0:T(8,128)S(1)}, u32[]{:S(2)}, u32[]{:S(2)}) collective-permute-start(f32[10,8,512]{2,1,0:T(8,128)S(1)} %bitcast_dynamic-update-slice_fusion.2), channel_id=1, source_target_pairs={{0,32},{16,48},{32,0},{48,16},{1,33},{17,49},{33,1},{49,17},{2,34}... | collective-permute-start | bytes 491528 | tf_op jit(solution)/shard_map/ppermute | solution.py:178
  19.5 3.1 %collective-permute-start.3 = (f32[10,8,512]{2,1,0:T(8,128)S(1)}, f32[10,8,512]{2,1,0:T(8,128)S(1)}, u32[]{:S(2)}, u32[]{:S(2)}) collective-permute-start(f32[10,8,512]{2,1,0:T(8,128)S(1)} %bitcast_dynamic-update-slice_fusion.2), channel_id=1, source_target_pairs={{0,48},{16,0},{32,16},{48,32},{1,49},{17,1},{33,17},{49,33},{2,50}... | collective-permute-start | bytes 491528 | tf_op jit(solution)/shard_map/ppermute | solution.py:178
  22.5 0.0 collective-permute-done.1
  22.6 1.2 collective-permute-done.2
  23.7 2.1 %collective-permute-done.3 = f32[10,8,512]{2,1,0:T(8,128)S(1)} collective-permute-done((f32[10,8,512]{2,1,0:T(8,128)S(1)}, f32[10,8,512]{2,1,0:T(8,128)S(1)}, u32[]{:S(2)}, u32[]{:S(2)}) %collective-permute-start.3) | collective-permute-done | bytes 163872 | tf_op jit(solution)/shard_map/ppermute | solution.py:178
  25.8 0.9 pad_maximum_fusion
  26.7 0.0 all-gather.3.cloned.1.call-update
  27.4 0.1 pad_add_fusion.meta
  27.5 0.0 copy-done.1
  27.5 0.0 copy-done.5
  27.5 0.0 copy-start.2
  27.5 1.0 copy-done.2
  28.5 0.0 copy-start.3
  28.5 0.9 copy-done.3
  29.4 3.4 %leaves.1 = f32[2,4,4,4,48,128]{5,4,3,2,1,0:T(8,128)S(1)} custom-call(s32[3]{0:T(128)S(1)} %pad_add_fusion.meta, f32[1,1,256,384]{3,2,1,0:T(8,128)S(1)} %copy-done.2, f32[1,1,256,256]{3,2,1,0:T(8,128)S(1)} %copy-done.3, f32[1,1,4,512,256]{4,3,2,1,0:T(8,128)S(1)} %copy-done.1, f32[1,4,8,384]{3,2,1,0:T(8,128)S(1)} %copy-done.5), custom_call_target="tpu_custom_call" | custom-call | tf_op jit(solution)/shard_map/leaves/pallas_call | solution.py:74
  32.8 0.1 slice_bitcast_fusion
  33.0 7.2 %collective-permute-start = (f32[4,4,4,48,128]{4,3,2,1,0:T(8,128)S(1)}, f32[4,4,4,48,128]{4,3,2,1,0:T(8,128)S(1)}, u32[]{:S(2)}, u32[]{:S(2)}) collective-permute-start(f32[4,4,4,48,128]{4,3,2,1,0:T(8,128)S(1)} %slice_bitcast_fusion), channel_id=1, source_target_pairs={{0,1},{1,0},{2,3},{3,2},{4,5},{5,4},{6,7},{7,6},{8,9},{9,8},{10,11... | collective-permute-start | bytes 4718600 | tf_op jit(solution)/shard_map/ppermute | solution.py:184
  40.2 3.0 %collective-permute-done = f32[4,4,4,48,128]{4,3,2,1,0:T(8,128)S(1)} collective-permute-done((f32[4,4,4,48,128]{4,3,2,1,0:T(8,128)S(1)}, f32[4,4,4,48,128]{4,3,2,1,0:T(8,128)S(1)}, u32[]{:S(2)}, u32[]{:S(2)}) %collective-permute-start) | collective-permute-done | bytes 1572896 | tf_op jit(solution)/shard_map/ppermute | solution.py:184
  43.2 0.3 fusion
  43.5 23.2 %all_to_all.20.parts = f32[4,768,128]{2,1,0:T(8,128)S(1)} all-to-all(f32[4,768,128]{2,1,0:T(8,128)S(1)} %bitcast.34), channel_id=1, replica_groups=mesh['layer'=8,'x'=4,'y'=8,'c'=2] {'x'}, dimensions={0} | all-to-all | bytes 3145728 | tf_op jit(solution)/shard_map/all_to_all | solution.py:186
  66.7 0.0 copy-start.4
  66.7 0.3 sum_x.1
  67.0 22.1 %all_to_all.21.parts = f32[8,96,128]{2,1,0:T(8,128)S(1)} all-to-all(f32[8,96,128]{2,1,0:T(8,128)S(1)} %sum_x.1), channel_id=1, replica_groups=mesh['layer'=8,'x'=4,'y'=8,'c'=2] {'y'}, dimensions={0} | all-to-all | bytes 786432 | tf_op jit(solution)/shard_map/all_to_all | solution.py:195
  89.1 20.6 %all-gather.3.cloned.1.call-done = f32[64,10,8,512]{3,2,1,0:T(8,128)} async-done(((f32[4,10,8,512]{3,2,1,0:T(8,128)}), f32[64,10,8,512]{3,2,1,0:T(8,128)}) %all-gather.3.cloned.1.call-update) | async-done | bytes 10485776 | tf_op jit(solution)/shard_map/all_gather | solution.py:180
  109.7 0.0 copy-done.4
  109.7 0.0 copy-start
  109.7 4.0 %copy-done = f32[64,10,8,512]{3,2,1,0:T(8,128)S(1)} copy-done((f32[64,10,8,512]{3,2,1,0:T(8,128)S(1)}, f32[64,10,8,512]{3,2,1,0:T(8,128)}, u32[]{:S(2)}) %copy-start) | copy-done | bytes 10485784
  113.7 6.4 %chain.1 = (f32[64,8,128]{2,1,0:T(8,128)S(1)}, f32[8,384]{1,0:T(8,128)S(1)}) custom-call(s32[1]{0:T(128)} %bitcast.meta, f32[8,96,128]{2,1,0:T(8,128)S(1)} %all_to_all.21.parts, f32[8,512]{1,0:T(8,128)S(1)} %copy-done.4, f32[16,4,10,8,512]{4,3,2,1,0:T(8,128)S(1)} %bitcast.33), custom_call_target="tpu_custom_call" | custom-call | tf_op jit(solution)/shard_map/chain/pallas_call | solution.py:197
  120.0 19.5 %all_to_all.22 = f32[64,8,128]{2,1,0:T(8,128)S(1)} all-to-all(f32[64,8,128]{2,1,0:T(8,128)S(1)} %get-tuple-element.4), channel_id=1, replica_groups=mesh['layer'=8,'x'=4,'y'=8,'c'=2] {'x','y','c'}, dimensions={0} | all-to-all | bytes 524288 | tf_op jit(solution)/shard_map/all_to_all | solution.py:214
  139.5 0.9 copy.19
  140.5 0.5 copy.21
  141.0 0.2 broadcast_in_dim.19
  141.1 0.6 broadcast_in_dim.20
  141.8 7.1 %all-to-all-start.3 = ((f32[8,8,384]{2,1,0:T(8,128)}), f32[8,8,384]{2,1,0:T(8,128)S(1)}, u32[]{:S(2)}, u32[]{:S(2)}) async-start(f32[8,8,384]{2,1,0:T(8,128)} %broadcast_in_dim.20), calls=%async_computation.3 | async-start | bytes 196608 | tf_op jit(solution)/shard_map/all_to_all | solution.py:217
  148.9 0.1 slice.25
  148.9 1.8 %copy.20 = f32[4,8,2,4,8,6]{5,4,3,2,1,0:T(8,128)S(1)} copy(f32[4,8,2,4,8,6]{1,2,4,3,5,0:T(2,128)S(1)} %slice.25) | data formatting | bytes 98304 | tf_op jit(solution)/shard_map/slice | solution.py:218
  150.8 1.1 broadcast_in_dim.18
  151.9 4.5 %all-to-all-done.3 = f32[8,8,384]{2,1,0:T(8,128)S(1)} async-done(((f32[8,8,384]{2,1,0:T(8,128)}), f32[8,8,384]{2,1,0:T(8,128)S(1)}, u32[]{:S(2)}, u32[]{:S(2)}) %all-to-all-start.3) | async-done | bytes 98336 | tf_op jit(solution)/shard_map/all_to_all | solution.py:217
  156.3 0.6 sub.3
  (2 shorter events, 0.0 us)
Async XLA Ops:
  7.2 20.3 %copy-start.1 = (f32[1,1,4,512,256]{4,3,2,1,0:T(8,128)S(1)}, f32[1,1,4,512,256]{4,3,2,1,0:T(8,128)}, u32[]{:S(2)}) copy-start(f32[1,1,4,512,256]{4,3,2,1,0:T(8,128)} %coupling.1) | copy-start | bytes 6291460
  7.2 20.3 %copy-start.5 = (f32[1,4,8,384]{3,2,1,0:T(8,128)S(1)}, f32[1,4,8,384]{3,2,1,0:T(8,128)}, u32[]{:S(2)}) copy-start(f32[1,4,8,384]{3,2,1,0:T(8,128)} %sep.1) | copy-start | bytes 147460
  7.2 102.5 %all-gather.3.cloned.1.call-start = ((), (), s32[]{:S(2)}) async-start(), calls=%async_computation.4 | async-start | bytes 11141120 | tf_op jit(solution)/shard_map/all_gather | solution.py:180
  11.2 11.4 %collective-permute-start.1 = (f32[10,8,512]{2,1,0:T(8,128)S(1)}, f32[10,8,512]{2,1,0:T(8,128)S(1)}, u32[]{:S(2)}, u32[]{:S(2)}) collective-permute-start(f32[10,8,512]{2,1,0:T(8,128)S(1)} %bitcast_dynamic-update-slice_fusion.2), channel_id=1, source_target_pairs={{0,16},{16,32},{32,48},{48,0},{1,17},{17,33},{33,49},{49,1},{2,18}... | collective-permute-start | bytes 491528 | tf_op jit(solution)/shard_map/ppermute | solution.py:178
  15.1 8.6 %collective-permute-start.2 = (f32[10,8,512]{2,1,0:T(8,128)S(1)}, f32[10,8,512]{2,1,0:T(8,128)S(1)}, u32[]{:S(2)}, u32[]{:S(2)}) collective-permute-start(f32[10,8,512]{2,1,0:T(8,128)S(1)} %bitcast_dynamic-update-slice_fusion.2), channel_id=1, source_target_pairs={{0,32},{16,48},{32,0},{48,16},{1,33},{17,49},{33,1},{49,17},{2,34}... | collective-permute-start | bytes 491528 | tf_op jit(solution)/shard_map/ppermute | solution.py:178
  19.5 6.4 %collective-permute-start.3 = (f32[10,8,512]{2,1,0:T(8,128)S(1)}, f32[10,8,512]{2,1,0:T(8,128)S(1)}, u32[]{:S(2)}, u32[]{:S(2)}) collective-permute-start(f32[10,8,512]{2,1,0:T(8,128)S(1)} %bitcast_dynamic-update-slice_fusion.2), channel_id=1, source_target_pairs={{0,48},{16,0},{32,16},{48,32},{1,49},{17,1},{33,17},{49,33},{2,50}... | collective-permute-start | bytes 491528 | tf_op jit(solution)/shard_map/ppermute | solution.py:178
  27.5 1.0 copy-start.2
  28.5 0.9 copy-start.3
  33.0 10.3 %collective-permute-start = (f32[4,4,4,48,128]{4,3,2,1,0:T(8,128)S(1)}, f32[4,4,4,48,128]{4,3,2,1,0:T(8,128)S(1)}, u32[]{:S(2)}, u32[]{:S(2)}) collective-permute-start(f32[4,4,4,48,128]{4,3,2,1,0:T(8,128)S(1)} %slice_bitcast_fusion), channel_id=1, source_target_pairs={{0,1},{1,0},{2,3},{3,2},{4,5},{5,4},{6,7},{7,6},{8,9},{9,8},{10,11... | collective-permute-start | bytes 4718600 | tf_op jit(solution)/shard_map/ppermute | solution.py:184
  66.7 43.0 %copy-start.4 = (f32[8,512]{1,0:T(8,128)S(1)}, f32[8,512]{1,0:T(8,128)}, u32[]{:S(2)}) copy-start(f32[8,512]{1,0:T(8,128)} %root_inverse.1) | copy-start | bytes 49156
  109.7 4.0 %copy-start = (f32[64,10,8,512]{3,2,1,0:T(8,128)S(1)}, f32[64,10,8,512]{3,2,1,0:T(8,128)}, u32[]{:S(2)}) copy-start(f32[64,10,8,512]{3,2,1,0:T(8,128)} %all-gather.3.cloned.1.call-done) | copy-start | bytes 31457284
  141.8 14.6 %all-to-all-start.3 = ((f32[8,8,384]{2,1,0:T(8,128)}), f32[8,8,384]{2,1,0:T(8,128)S(1)}, u32[]{:S(2)}, u32[]{:S(2)}) async-start(f32[8,8,384]{2,1,0:T(8,128)} %broadcast_in_dim.20), calls=%async_computation.3 | async-start | bytes 196608 | tf_op jit(solution)/shard_map/all_to_all | solution.py:217
Sparse Core Ops, SparseCore 0:
  26.9 82.7 all-gather.2

commit v3 on v2

v3 whole, which is shorter than its diff:
```python
import functools

import jax
import jax.numpy as jnp
from jax import lax
from jax.experimental import pallas as pl
from jax.experimental.pallas import tpu as pltpu
from jax.sharding import Mesh, PartitionSpec as P

ROW = ("xl", "xh", "y", "c")
X = ("xl", "xh")
NX, NY, NC = 4, 8, 2
NT = (((1,), (1,)), ((), ()))
NN = (((1,), (0,)), ((), ()))
VMEM = pl.BlockSpec(memory_space=pltpu.VMEM)
SMEM = pl.BlockSpec(memory_space=pltpu.SMEM)
HBM = pl.BlockSpec(memory_space=pltpu.HBM)
FLAT = jax.ShapeDtypeStruct


def split(a):
    high = a.astype(jnp.bfloat16)
    return high, (a - high.astype(jnp.float32)).astype(jnp.bfloat16)


def dot3(a, b, dims):
    mm = functools.partial(lax.dot_general, dimension_numbers=dims, preferred_element_type=jnp.float32)
    return mm(a[0], b[0]) + (mm(a[0], b[1]) + mm(a[1], b[0]))


def by_tiles(ref, part):
    tiles, rows, _ = ref.shape

    def column(tile):
        return jnp.concatenate(
            [
                ref[tile, pl.ds(base + t, 8, stride=part), :]
                for base in range(0, rows, 8 * part)
                for t in range(part)
            ],
            axis=0,
        )

    return jnp.concatenate([column(tile) for tile in range(tiles)], axis=1)


def pack_kernel(meta, sep_inverse, sep_coupling, root_coupling, root_rhs, root_inverse, same, other):
    zeros = jnp.zeros_like(root_inverse)
    rr = jnp.concatenate([root_rhs[...], zeros[:, root_rhs.shape[1] :]], axis=1)
    tables = (
        [sep_inverse[0, 0], sep_inverse[0, 1], sep_coupling[0, 0], rr, zeros, zeros],
        [
            sep_inverse[0, 2],
            sep_inverse[0, 3],
            sep_coupling[0, 1],
            sep_coupling[0, 2],
            root_coupling[0],
            root_inverse[...],
        ],
    )
    for side in range(2):

        @pl.when(meta[0] == side)
        def _():
            for m in range(same.shape[0]):
                same[m] = tables[side][m]
                other[m] = tables[1 - side][m]


def leaf_kernel(part, meta, rhs, inv, coupling, sep, out, xt, xt_hi, xt_lo, place, own):
    k = pl.program_id(0)
    parent, core, block = meta[0], meta[1], meta[2]

    @pl.when(k == 0)
    def _():
        solved = dot3(split(inv[0, 0]), split(rhs[0, 0]), NN).T
        for tile in range(xt.shape[0]):
            xt[tile] = solved[:, 128 * tile : 128 * (tile + 1)]
        xt_hi[...], xt_lo[...] = split(by_tiles(xt, part))
        place[...] = jnp.zeros_like(place)

    keep = jnp.where(k >= parent, 1.0, 0.0)
    got = dot3((xt_hi[...], xt_lo[...]), split(coupling[0, 0, 0]), NT) * -keep
    place[pl.ds(pl.multiple_of(8 * (block % 16), 8), 8), :] = sep[0, 0]
    own[0] = place[...].T
    mine = by_tiles(own, part)
    group = 8 * part
    for half in range(NC):
        slot = jnp.where(core == half, 1, 0)
        for side in range(2):
            rows = slice((half * 2 + side) * group, (half * 2 + side + 1) * group)
            for tile in range(out.shape[4]):
                out[slot, side, 0, 0, tile] = got[rows, 128 * tile : 128 * (tile + 1)]
            out[slot, side, 0, 0, block // 16] += mine[rows]


def leaves(meta, rhs, inv, coupling, sep):
    n, width = coupling.shape[2], coupling.shape[3]
    leaf, cols = rhs.shape[2], rhs.shape[3]
    part = cols // 32
    return pl.pallas_call(
        functools.partial(leaf_kernel, part),
        grid_spec=pltpu.PrefetchScalarGridSpec(
            num_scalar_prefetch=1,
            grid=(n,),
            in_specs=[
                pl.BlockSpec((1, 1, leaf, cols), lambda k, m: (0, 0, 0, 0)),
                pl.BlockSpec((1, 1, leaf, leaf), lambda k, m: (0, 0, 0, 0)),
                pl.BlockSpec((1, 1, 1, width, leaf), lambda k, m: (0, 0, k, 0, 0)),
                pl.BlockSpec((1, 1, 8, cols), lambda k, m: (0, k, 0, 0)),
            ],
            out_specs=pl.BlockSpec(
                (NC, 2, 1, 1, width // 128, 8 * part, 128),
                lambda k, m: (0, 0, k // 2, k % 2, 0, 0, 0),
            ),
            scratch_shapes=[
                pltpu.VMEM((leaf // 128, cols, 128), jnp.float32),
                pltpu.VMEM((cols, leaf), jnp.bfloat16),
                pltpu.VMEM((cols, leaf), jnp.bfloat16),
                pltpu.VMEM((128, cols), jnp.float32),
                pltpu.VMEM((1, cols, 128), jnp.float32),
            ],
        ),
        out_shape=FLAT((NC, 2, 2, 2, width // 128, 8 * part, 128), jnp.float32),
        compiler_params=pltpu.CompilerParams(vmem_limit_bytes=24 * 2**20),
        name="leaves",
    )(meta, rhs, inv, coupling, sep)


def sum_kernel(parts, out):
    count = out.shape[1]
    for s in range(8):
        rows = pl.ds(s, count, stride=8)
        out[s] = (parts[0, rows, :] + parts[1, rows, :]) + (parts[2, rows, :] + parts[3, rows, :])


def fetch(weights, full, sems, x, slots):
    copies = {}
    for at, m in enumerate(slots):
        copies[m] = []
        for back in range(NX):
            rows = pl.multiple_of(((x + NX - back) % NX) * 16, 16)
            copy = pltpu.make_async_copy(
                weights.at[:, back, m], full.at[at, pl.ds(rows, 16)], sems.at[at, back]
            )
            copy.start()
            copies[m].append(copy)

    def matrix(m):
        for copy in copies[m]:
            copy.wait()
        block = full[slots.index(m)]
        return split(block.reshape(-1, block.shape[-1]))

    return matrix


def first_kernel(part, meta, parts, weights, held, send, full, sems):
    matrix = fetch(weights, full, sems, meta[0], [0, 1, 2, 3])
    res = parts[0]
    for p in range(1, parts.shape[0]):
        res = res + parts[p]
    tiles = res.shape[0] // (2 * part)

    def residual(k):
        starts = [part * (tiles * k + tile) for tile in range(tiles)]
        return split(jnp.concatenate([res[at : at + part] for at in starts], axis=1))

    wide = held.shape[2]
    first = dot3(residual(0), matrix(0), NT)
    second = dot3(residual(1), matrix(1), NT)
    chained = second - dot3(split(first), matrix(2), NT)
    shape = (part, wide)
    mine = lax.broadcasted_iota(jnp.int32, shape, 1) == lax.broadcasted_iota(jnp.int32, shape, 0) + part * meta[1]
    pick = jnp.where(mine, jnp.where(meta[2] == 0, 1.0, 0.0), 0.0).astype(jnp.bfloat16)
    high, low = matrix(3)
    mm = functools.partial(lax.dot_general, dimension_numbers=NT, preferred_element_type=jnp.float32)
    held[0] = first
    held[1] = jnp.where(meta[0] % 2 == 0, chained, second)
    send[0] = chained
    send[1] = mm(pick, high) + mm(pick, low)


def second_kernel(part, meta, held, came, weights, out, full, wide, sems):
    wide[...] = jnp.zeros_like(wide)

    @pl.when(meta[0] % 2 == 0)
    def _():
        wide[:part, :] = held[0]
        wide[part : 2 * part, :] = held[1]

    @pl.when(meta[0] % 2 == 1)
    def _():
        matrix = fetch(weights, full, sems, meta[0], [2, 3, 4, 5])
        third = held[0] - dot3(split(came[0]), matrix(2), NT)
        wide[:part, :] = third
        fourth = held[1] - dot3(split(third), matrix(3), NT)
        wide[part : 2 * part, :] = fourth
        term = came[1] - dot3(split(fourth), matrix(4), NT)
        wide[2 * part : 3 * part, :] = dot3(split(term), matrix(5), NT)

    back = wide[...].T
    out[...] = back.reshape(out.shape)


def body(
    leaf_rhs,
    leaf_inverse,
    leaf_coupling,
    parent,
    sep_rhs,
    sep_inverse,
    sep_coupling,
    root_coupling,
    root_rhs,
    root_inverse,
):
    xl, xh = lax.axis_index("xl"), lax.axis_index("xh")
    y, c, layer = lax.axis_index("y"), lax.axis_index("c"), lax.axis_index("layer")
    width, cols = leaf_coupling.shape[3], leaf_rhs.shape[3]
    part = cols // 32
    tiles = width // 128
    call = pl.pallas_call

    same, other = call(
        pack_kernel,
        in_specs=[SMEM] + [VMEM] * 5,
        out_specs=[VMEM, VMEM],
        out_shape=[FLAT((6, 8, width), jnp.float32)] * 2,
        name="pack",
    )(xh.reshape(1).astype(jnp.int32), sep_inverse, sep_coupling, root_coupling, root_rhs, root_inverse)
    ring = [same] + [
        lax.ppermute(pack, X, [(i, (i + j) % NX) for i in range(NX)])
        for j, pack in ((1, other), (2, same), (3, other))
    ]

    meta = jnp.stack([parent[0, 0], c, lax.axis_index(ROW)]).astype(jnp.int32)
    update = leaves(meta, leaf_rhs, leaf_inverse, leaf_coupling, sep_rhs)
    ring, update = lax.optimization_barrier((ring, update))
    weights = lax.all_gather(jnp.stack(ring), ("y", "c"))
    res = update[1] + lax.ppermute(update[0], "c", [(0, 1), (1, 0)])
    res = lax.all_to_all(res.reshape(NX, 2 * tiles * 8 * part, 128), X, 0, 0)
    res = call(
        sum_kernel,
        in_specs=[VMEM],
        out_specs=VMEM,
        out_shape=FLAT((8, 2 * tiles * part, 128), jnp.float32),
        compiler_params=pltpu.CompilerParams(vmem_limit_bytes=16 * 2**20),
        name="sum_x",
    )(res)
    res = lax.all_to_all(res, "y", 0, 0)

    meta = jnp.stack([2 * xl + xh, (c * 2 + xl) * NY + y, layer]).astype(jnp.int32)
    scratch = [pltpu.VMEM((4, 64, 8, width), jnp.float32)]
    sems = [pltpu.SemaphoreType.DMA((4, NX))]
    params = pltpu.CompilerParams(vmem_limit_bytes=32 * 2**20)
    held, send = call(
        functools.partial(first_kernel, part),
        in_specs=[SMEM, VMEM, HBM],
        out_specs=[VMEM, VMEM],
        out_shape=[FLAT((2, part, width), jnp.float32)] * 2,
        scratch_shapes=scratch + sems,
        compiler_params=params,
        name="chain_first",
    )(meta, res, weights)
    came = lax.ppermute(send, "xh", [(0, 1)])
    out = call(
        functools.partial(second_kernel, part),
        in_specs=[SMEM, VMEM, VMEM, HBM],
        out_specs=VMEM,
        out_shape=FLAT((64, 8, 128), jnp.float32),
        scratch_shapes=scratch + [pltpu.VMEM((128, width), jnp.float32)] + sems,
        compiler_params=params,
        name="chain_second",
    )(meta, held, came, weights)

    out = lax.all_to_all(out, ROW, 0, 0)[:, :, : 3 * part]
    out = out.reshape(2, 2, NY, NC, 8, 3, part).transpose(1, 5, 4, 3, 0, 2, 6).reshape(2, 3, 8, cols)
    term = jnp.broadcast_to(out[1, 2][None], (8, 8, cols))
    root_out = lax.all_to_all(term, "layer", 0, 0).sum(0)
    return (out[:, :2].reshape(1, 4, 8, cols), root_out)


def solution(mesh):
    fine = Mesh(mesh.devices.reshape(-1, 2, 2, NY, NC), ("layer",) + ROW)
    return jax.shard_map(
        body,
        mesh=fine,
        in_specs=(
            P("layer", ROW, None, None),
            P("layer", ROW, None, None),
            P("layer", ROW, None, None, None),
            P("layer", ROW),
            P("layer", None, ROW, None),
            P("layer", None, ROW, None),
            P("layer", None, ROW, None),
            P("layer", ROW, None),
            P(ROW, None),
            P(ROW, None),
        ),
        out_specs=(P("layer", None, ROW, None), P(ROW, None)),
        check_vma=False,
    )
```

time: 165 us -> 150 us (0.909)
  blocking collectives: 64.8 us -> 47.7 us
  starting transfers between devices: 25.7 us -> 31.4 us
  local copies, waits for them, and re-layouts: 15.2 us -> 9.79 us
  waiting for transfers between devices: 31.4 us -> 33.5 us
    all_to_all x1 -> x2, waiting for transfers between devices: 4.46 us -> 25.3 us  [the longest x1 18.4 us: body(): res = lax.all_to_all(res, 'y', 0, 0)]
    all_to_all x3 -> x2, blocking collectives: 64.8 us -> 47.7 us  [the longest x1 24.2 us: body(): res = lax.all_to_all(res.reshape(NX, 2 * tiles * 8 * part, 128), X, 0, 0)]
    all_gather x1, waiting for transfers between devices: 20.6 us -> 3.91 us  [body(): weights = lax.all_gather(jnp.stack(ring), ('y', 'c'))]
    all_to_all x1 -> x2, starting transfers between devices: 7.1 us -> 10.6 us  [the longest x1 7.1 us: body(): root_out = lax.all_to_all(term, 'layer', 0, 0).sum(0)]
    slice x5 -> x1, local copies, waits for them, and re-layouts: 3.3 us -> 0.62 us  [body(): return (out[:, :2].reshape(1, 4, 8, cols), root_out)]
    ppermute x3 -> x4, starting transfers between devices: 11.4 us -> 13.8 us  [the longest x3 10.8 us: body(): lax.ppermute(pack, X, [(i, (i + j) % NX) for i in range(NX)])]
    unnamed x16 -> x14, local copies, waits for them, and re-layouts: 9.16 us -> 7.13 us
    ppermute x3 -> x4, waiting for transfers between devices: 3.28 us -> 1.32 us  [the longest x1 1.31 us: body(): came = lax.ppermute(send, 'xh', [(0, 1)])]
  transfers between devices with their start and end apart: 6 -> 8, of which waited for: 5 -> 5; matrix products, arithmetic and copies ran while one was open for 2% -> 1% of each run, Pallas kernels for 2% -> 3%
where the time goes in v3:
time: 150 us; the launch traced here: 149 us
  blocking collectives  47.7 us (32%)
  waiting for transfers between devices  33.5 us (22%)
  starting transfers between devices  31.4 us (21%)
  between operations  14.9 us (10%)
  Pallas kernels  10 us (7%)
  local copies, waits for them, and re-layouts  9.79 us (7%)
  other arithmetic  1.8 us (1%)
    all_to_all x1, blocking collectives, body(): res = lax.all_to_all(res.reshape(NX, 2 * tiles * 8 * part, 128), X, 0, 0)  24.2 us
    all_to_all x1, blocking collectives, body(): out = lax.all_to_all(out, ROW, 0, 0)[:, :, :3 * part]  23.5 us
    all_to_all x1, waiting for transfers between devices, body(): res = lax.all_to_all(res, 'y', 0, 0)  18.4 us
    ppermute x3, starting transfers between devices, body(): lax.ppermute(pack, X, [(i, (i + j) % NX) for i in range(NX)])  10.8 us
    unnamed x14, local copies, waits for them, and re-layouts  7.13 us
    all_to_all x1, starting transfers between devices, body(): root_out = lax.all_to_all(term, 'layer', 0, 0).sum(0)  7.1 us
    ppermute x1, starting transfers between devices, body(): res = update[1] + lax.ppermute(update[0], 'c', [(0, 1), (1, 0)])  7 us
    all_to_all x1, waiting for transfers between devices, body(): root_out = lax.all_to_all(term, 'layer', 0, 0).sum(0)  6.83 us
  transfers between devices with their start and end apart: 8, of which 5 were waited for; matrix products, arithmetic and copies ran while one was open for 1% of the time, Pallas kernels for 3%

profile of v3, /device:TPU:1, one launch (start us, length us, event | category | flops | bytes accessed | tf_op | source)
XLA Modules:
  0.0 149.1 jit_solution(18284127747541173918)
XLA Ops:
  7.2 0.0 all-gather.3.cloned.1.call-start
  7.2 1.6 %pack.1 = (f32[6,8,512]{2,1,0:T(8,128)}, f32[6,8,512]{2,1,0:T(8,128)}) custom-call(s32[1]{0:T(128)} %bitcast.3.meta, f32[1,4,8,512]{3,2,1,0:T(8,128)} %sep_inverse.1, f32[1,3,8,512]{3,2,1,0:T(8,128)} %sep_coupling.1, f32[1,8,512]{2,1,0:T(8,128)} %root_coupling.1, f32[8,384]{1,0:T(8,128)} %root_rhs.1, f32[8,512]{1,0:T(8,128)} %root_inverse.1), custom_call_target="tpu_custom_call" | custom-call | tf_op jit(solution)/shard_map/pack/pallas_call | solution.py:225
  8.8 3.9 %collective-permute-start = (f32[6,8,512]{2,1,0:T(8,128)}, f32[6,8,512]{2,1,0:T(8,128)S(1)}, u32[]{:S(2)}, u32[]{:S(2)}) collective-permute-start(f32[6,8,512]{2,1,0:T(8,128)} %get-tuple-element.12), channel_id=1, source_target_pairs={{0,16},{16,32},{32,48},{48,0},{1,17},{17,33},{33,49},{49,1},{2,18}... | collective-permute-start | bytes 294920 | tf_op jit(solution)/shard_map/ppermute | solution.py:233
  12.8 3.2 %collective-permute-start.2 = (f32[6,8,512]{2,1,0:T(8,128)}, f32[6,8,512]{2,1,0:T(8,128)S(1)}, u32[]{:S(2)}, u32[]{:S(2)}) collective-permute-start(f32[6,8,512]{2,1,0:T(8,128)} %get-tuple-element.12), channel_id=1, source_target_pairs={{0,48},{16,0},{32,16},{48,32},{1,49},{17,1},{33,17},{49,33},{2,50}... | collective-permute-start | bytes 294920 | tf_op jit(solution)/shard_map/ppermute | solution.py:233
  16.0 3.6 %collective-permute-start.1 = (f32[6,8,512]{2,1,0:T(8,128)}, f32[6,8,512]{2,1,0:T(8,128)S(1)}, u32[]{:S(2)}, u32[]{:S(2)}) collective-permute-start(f32[6,8,512]{2,1,0:T(8,128)} %get-tuple-element.14), channel_id=1, source_target_pairs={{0,32},{16,48},{32,0},{48,16},{1,33},{17,49},{33,1},{49,17},{2,34}... | collective-permute-start | bytes 294920 | tf_op jit(solution)/shard_map/ppermute | solution.py:233
  20.3 0.1 pad_add_fusion.1.meta
  20.3 0.0 copy-start.2
  20.3 1.6 %copy-done.2 = f32[1,1,4,512,256]{4,3,2,1,0:T(8,128)S(1)} copy-done((f32[1,1,4,512,256]{4,3,2,1,0:T(8,128)S(1)}, f32[1,1,4,512,256]{4,3,2,1,0:T(8,128)}, u32[]{:S(2)}) %copy-start.2) | copy-done | bytes 2097176
  21.9 0.0 copy-start.3
  21.9 1.0 copy-done.3
  22.9 0.0 copy-start.4
  22.9 0.9 copy-done.4
  23.9 0.0 copy-start.5
  23.9 0.8 copy-done.5
  24.7 0.0 copy-start.6
  24.7 3.5 %leaves.1 = f32[2,2,2,2,4,96,128]{6,5,4,3,2,1,0:T(8,128)S(1)} custom-call(s32[3]{0:T(128)S(1)} %pad_add_fusion.1.meta, f32[1,1,256,384]{3,2,1,0:T(8,128)S(1)} %copy-done.3, f32[1,1,256,256]{3,2,1,0:T(8,128)S(1)} %copy-done.4, f32[1,1,4,512,256]{4,3,2,1,0:T(8,128)S(1)} %copy-done.2, f32[1,4,8,384]{3,2,1,0:T(8,128)S(1)} %copy-done.5), custom_call_target="tpu_custom_call" | custom-call | tf_op jit(solution)/shard_map/leaves/pallas_call | solution.py:101
  28.2 0.0 collective-permute-done
  28.2 0.0 collective-permute-done.1
  28.2 0.0 collective-permute-done.2
  28.2 0.0 copy-done.6
  28.2 0.8 pad_maximum_fusion
  29.0 0.0 all-gather.3.cloned.1.call-update
  29.0 0.1 slice_bitcast_fusion
  29.1 7.0 %collective-permute-start.3 = (f32[2,2,2,4,96,128]{5,4,3,2,1,0:T(8,128)S(1)}, f32[2,2,2,4,96,128]{5,4,3,2,1,0:T(8,128)S(1)}, u32[]{:S(2)}, u32[]{:S(2)}) collective-permute-start(f32[2,2,2,4,96,128]{5,4,3,2,1,0:T(8,128)S(1)} %slice_bitcast_fusion), channel_id=1, source_target_pairs={{0,1},{1,0},{2,3},{3,2},{4,5},{5,4},{6,7},{7,6},{8,9},{9,8},{10,11... | collective-permute-start | bytes 4718600 | tf_op jit(solution)/shard_map/ppermute | solution.py:241
  36.1 3.0 %collective-permute-done.3 = f32[2,2,2,4,96,128]{5,4,3,2,1,0:T(8,128)S(1)} collective-permute-done((f32[2,2,2,4,96,128]{5,4,3,2,1,0:T(8,128)S(1)}, f32[2,2,2,4,96,128]{5,4,3,2,1,0:T(8,128)S(1)}, u32[]{:S(2)}, u32[]{:S(2)}) %collective-permute-start.3) | collective-permute-done | bytes 1572896 | tf_op jit(solution)/shard_map/ppermute | solution.py:241
  39.2 0.2 bitcast_add_fusion
  39.4 24.2 %all_to_all.20.parts = f32[4,768,128]{2,1,0:T(8,128)S(1)} all-to-all(f32[4,768,128]{2,1,0:T(8,128)S(1)} %bitcast.27), channel_id=1, replica_groups=mesh['layer'=8,'xl'=2,'xh'=2,'y'=8,'c'=2] {'xl','xh'}, dimensions={0} | all-to-all | bytes 3145728 | tf_op jit(solution)/shard_map/all_to_all | solution.py:242
  63.6 1.1 sum_x.1
  64.7 3.5 %all-to-all-start.1 = ((f32[8,96,128]{2,1,0:T(8,128)}), f32[8,96,128]{2,1,0:T(8,128)S(1)}, u32[]{:S(2)}, u32[]{:S(2)}) async-start(f32[8,96,128]{2,1,0:T(8,128)} %sum_x.1), calls=%async_computation.1 | async-start | bytes 786432 | tf_op jit(solution)/shard_map/all_to_all | solution.py:251
  68.2 0.1 pad_add_fusion.meta
  68.2 18.4 %all-to-all-done.1.parts = f32[8,96,128]{2,1,0:T(8,128)S(1)} async-done(((f32[8,96,128]{2,1,0:T(8,128)}), f32[8,96,128]{2,1,0:T(8,128)S(1)}, u32[]{:S(2)}, u32[]{:S(2)}) %all-to-all-start.1) | async-done | bytes 393248 | tf_op jit(solution)/shard_map/all_to_all | solution.py:251
  86.7 3.9 %all-gather.3.cloned.1.call-done = f32[64,6,8,512]{3,2,1,0:T(8,128)} async-done(((f32[4,6,8,512]{3,2,1,0:T(8,128)}), f32[64,6,8,512]{3,2,1,0:T(8,128)}) %all-gather.3.cloned.1.call-update) | async-done | bytes 6291472 | tf_op jit(solution)/shard_map/all_gather | solution.py:240
  90.6 0.0 copy-start
  90.6 2.8 %copy-done = f32[64,6,8,512]{3,2,1,0:T(8,128)S(1)} copy-done((f32[64,6,8,512]{3,2,1,0:T(8,128)S(1)}, f32[64,6,8,512]{3,2,1,0:T(8,128)}, u32[]{:S(2)}) %copy-start) | copy-done | bytes 6291480
  93.4 3.0 %chain_first.1 = (f32[2,12,512]{2,1,0:T(8,128)S(1)}, f32[2,12,512]{2,1,0:T(8,128)S(1)}) custom-call(s32[3]{0:T(128)S(1)} %pad_add_fusion.meta, f32[8,96,128]{2,1,0:T(8,128)S(1)} %all-to-all-done.1.parts, f32[16,4,6,8,512]{4,3,2,1,0:T(8,128)S(1)} %bitcast.25), custom_call_target="tpu_custom_call" | custom-call | tf_op jit(solution)/shard_map/chain_first/pallas_call | solution.py:257
  96.4 3.1 %collective-permute-start.4 = (f32[2,12,512]{2,1,0:T(8,128)S(1)}, f32[2,12,512]{2,1,0:T(8,128)S(1)}, u32[]{:S(2)}, u32[]{:S(2)}) collective-permute-start(f32[2,12,512]{2,1,0:T(8,128)S(1)} %get-tuple-element.19), channel_id=1, source_target_pairs={{0,16},{1,17},{2,18},{3,19},{4,20},{5,21},{6,22},{7,23},{8,24},{9,... | collective-permute-start | bytes 147464 | tf_op jit(solution)/shard_map/ppermute | solution.py:266
  99.5 1.3 collective-permute-done.4.came
  100.8 0.0 copy-done.1
  100.8 0.9 chain_second.1
  101.7 23.5 %all_to_all.21 = f32[64,8,128]{2,1,0:T(8,128)S(1)} all-to-all(f32[64,8,128]{2,1,0:T(8,128)S(1)} %chain_second.1), channel_id=1, replica_groups=mesh['layer'=8,'xl'=2,'xh'=2,'y'=8,'c'=2] {'xl','xh','y','c'}, dimensions={0} | all-to-all | bytes 524288 | tf_op jit(solution)/shard_map/all_to_all | solution.py:277
  125.1 0.4 reshape.22
  125.5 0.5 copy.14
  126.0 0.4 reshape.23
  126.4 0.7 broadcast_in_dim.8
  127.1 7.1 %all-to-all-start.3 = ((f32[8,8,384]{2,1,0:T(8,128)}), f32[8,8,384]{2,1,0:T(8,128)S(1)}, u32[]{:S(2)}, u32[]{:S(2)}) async-start(f32[8,8,384]{2,1,0:T(8,128)} %broadcast_in_dim.8), calls=%async_computation.3 | async-start | bytes 196608 | tf_op jit(solution)/shard_map/all_to_all | solution.py:280
  134.2 0.6 slice.21
  134.8 6.8 %all-to-all-done.3 = f32[8,8,384]{2,1,0:T(8,128)S(1)} async-done(((f32[8,8,384]{2,1,0:T(8,128)}), f32[8,8,384]{2,1,0:T(8,128)S(1)}, u32[]{:S(2)}, u32[]{:S(2)}) %all-to-all-start.3) | async-done | bytes 98336 | tf_op jit(solution)/shard_map/all_to_all | solution.py:280
  141.6 0.6 reduce_sum.9
  (2 shorter events, 0.0 us)
Async XLA Ops:
  7.2 83.4 %all-gather.3.cloned.1.call-start = ((), (), s32[]{:S(2)}) async-start(), calls=%async_computation.4 | async-start | bytes 6684672 | tf_op jit(solution)/shard_map/all_gather | solution.py:240
  8.8 19.3 %collective-permute-start = (f32[6,8,512]{2,1,0:T(8,128)}, f32[6,8,512]{2,1,0:T(8,128)S(1)}, u32[]{:S(2)}, u32[]{:S(2)}) collective-permute-start(f32[6,8,512]{2,1,0:T(8,128)} %get-tuple-element.12), channel_id=1, source_target_pairs={{0,16},{16,32},{32,48},{48,0},{1,17},{17,33},{33,49},{49,1},{2,18}... | collective-permute-start | bytes 294920 | tf_op jit(solution)/shard_map/ppermute | solution.py:233
  12.8 15.4 %collective-permute-start.2 = (f32[6,8,512]{2,1,0:T(8,128)}, f32[6,8,512]{2,1,0:T(8,128)S(1)}, u32[]{:S(2)}, u32[]{:S(2)}) collective-permute-start(f32[6,8,512]{2,1,0:T(8,128)} %get-tuple-element.12), channel_id=1, source_target_pairs={{0,48},{16,0},{32,16},{48,32},{1,49},{17,1},{33,17},{49,33},{2,50}... | collective-permute-start | bytes 294920 | tf_op jit(solution)/shard_map/ppermute | solution.py:233
  16.0 12.2 %collective-permute-start.1 = (f32[6,8,512]{2,1,0:T(8,128)}, f32[6,8,512]{2,1,0:T(8,128)S(1)}, u32[]{:S(2)}, u32[]{:S(2)}) collective-permute-start(f32[6,8,512]{2,1,0:T(8,128)} %get-tuple-element.14), channel_id=1, source_target_pairs={{0,32},{16,48},{32,0},{48,16},{1,33},{17,49},{33,1},{49,17},{2,34}... | collective-permute-start | bytes 294920 | tf_op jit(solution)/shard_map/ppermute | solution.py:233
  20.3 1.6 %copy-start.2 = (f32[1,1,4,512,256]{4,3,2,1,0:T(8,128)S(1)}, f32[1,1,4,512,256]{4,3,2,1,0:T(8,128)}, u32[]{:S(2)}) copy-start(f32[1,1,4,512,256]{4,3,2,1,0:T(8,128)} %coupling.1) | copy-start | bytes 6291460
  21.9 1.0 copy-start.3
  22.9 0.9 copy-start.4
  23.9 0.8 copy-start.5
  24.7 3.5 %copy-start.6 = (f32[6,8,512]{2,1,0:T(8,128)S(1)}, f32[6,8,512]{2,1,0:T(8,128)}, u32[]{:S(2)}) copy-start(f32[6,8,512]{2,1,0:T(8,128)} %get-tuple-element.14) | copy-start | bytes 294916
  29.1 10.0 %collective-permute-start.3 = (f32[2,2,2,4,96,128]{5,4,3,2,1,0:T(8,128)S(1)}, f32[2,2,2,4,96,128]{5,4,3,2,1,0:T(8,128)S(1)}, u32[]{:S(2)}, u32[]{:S(2)}) collective-permute-start(f32[2,2,2,4,96,128]{5,4,3,2,1,0:T(8,128)S(1)} %slice_bitcast_fusion), channel_id=1, source_target_pairs={{0,1},{1,0},{2,3},{3,2},{4,5},{5,4},{6,7},{7,6},{8,9},{9,8},{10,11... | collective-permute-start | bytes 4718600 | tf_op jit(solution)/shard_map/ppermute | solution.py:241
  64.7 22.0 %all-to-all-start.1 = ((f32[8,96,128]{2,1,0:T(8,128)}), f32[8,96,128]{2,1,0:T(8,128)S(1)}, u32[]{:S(2)}, u32[]{:S(2)}) async-start(f32[8,96,128]{2,1,0:T(8,128)} %sum_x.1), calls=%async_computation.1 | async-start | bytes 786432 | tf_op jit(solution)/shard_map/all_to_all | solution.py:251
  90.6 2.8 %copy-start = (f32[64,6,8,512]{3,2,1,0:T(8,128)S(1)}, f32[64,6,8,512]{3,2,1,0:T(8,128)}, u32[]{:S(2)}) copy-start(f32[64,6,8,512]{3,2,1,0:T(8,128)} %all-gather.3.cloned.1.call-done) | copy-start | bytes 18874372
  93.3 7.4 %copy-start.1 = (f32[64,6,8,512]{3,2,1,0:T(8,128)S(1)}, f32[64,6,8,512]{3,2,1,0:T(8,128)}, u32[]{:S(2)}) copy-start(f32[64,6,8,512]{3,2,1,0:T(8,128)} %all-gather.3.cloned.1.call-done) | copy-start | bytes 18874372
  96.4 4.4 %collective-permute-start.4 = (f32[2,12,512]{2,1,0:T(8,128)S(1)}, f32[2,12,512]{2,1,0:T(8,128)S(1)}, u32[]{:S(2)}, u32[]{:S(2)}) collective-permute-start(f32[2,12,512]{2,1,0:T(8,128)S(1)} %get-tuple-element.19), channel_id=1, source_target_pairs={{0,16},{1,17},{2,18},{3,19},{4,20},{5,21},{6,22},{7,23},{8,24},{9,... | collective-permute-start | bytes 147464 | tf_op jit(solution)/shard_map/ppermute | solution.py:266
  127.1 14.6 %all-to-all-start.3 = ((f32[8,8,384]{2,1,0:T(8,128)}), f32[8,8,384]{2,1,0:T(8,128)S(1)}, u32[]{:S(2)}, u32[]{:S(2)}) async-start(f32[8,8,384]{2,1,0:T(8,128)} %broadcast_in_dim.8), calls=%async_computation.3 | async-start | bytes 196608 | tf_op jit(solution)/shard_map/all_to_all | solution.py:280
Sparse Core Ops, SparseCore 0:
  29.1 61.3 all-gather.2

commit v4 on v3

--- a/solution.py
+++ b/solution.py
@@ -134,29 +134,24 @@
         out[s] = (parts[0, rows, :] + parts[1, rows, :]) + (parts[2, rows, :] + parts[3, rows, :])
 
 
-def fetch(weights, full, sems, x, slots):
-    copies = {}
-    for at, m in enumerate(slots):
-        copies[m] = []
+def first_kernel(part, meta, parts, weights, held, send, high, low, full, sems):
+    x = meta[0]
+    copies = []
+    for m in range(full.shape[0]):
+        copies.append([])
         for back in range(NX):
             rows = pl.multiple_of(((x + NX - back) % NX) * 16, 16)
             copy = pltpu.make_async_copy(
-                weights.at[:, back, m], full.at[at, pl.ds(rows, 16)], sems.at[at, back]
+                weights.at[:, back, m], full.at[m, pl.ds(rows, 16)], sems.at[m, back]
             )
             copy.start()
-            copies[m].append(copy)
+            copies[-1].append(copy)
 
     def matrix(m):
         for copy in copies[m]:
             copy.wait()
-        block = full[slots.index(m)]
-        return split(block.reshape(-1, block.shape[-1]))
-
-    return matrix
-
-
-def first_kernel(part, meta, parts, weights, held, send, full, sems):
-    matrix = fetch(weights, full, sems, meta[0], [0, 1, 2, 3])
+        return split(full[m].reshape(-1, full.shape[3]))
+
     res = parts[0]
     for p in range(1, parts.shape[0]):
         res = res + parts[p]
@@ -166,41 +161,94 @@
         starts = [part * (tiles * k + tile) for tile in range(tiles)]
         return split(jnp.concatenate([res[at : at + part] for at in starts], axis=1))
 
-    wide = held.shape[2]
     first = dot3(residual(0), matrix(0), NT)
     second = dot3(residual(1), matrix(1), NT)
-    chained = second - dot3(split(first), matrix(2), NT)
-    shape = (part, wide)
-    mine = lax.broadcasted_iota(jnp.int32, shape, 1) == lax.broadcasted_iota(jnp.int32, shape, 0) + part * meta[1]
-    pick = jnp.where(mine, jnp.where(meta[2] == 0, 1.0, 0.0), 0.0).astype(jnp.bfloat16)
-    high, low = matrix(3)
-    mm = functools.partial(lax.dot_general, dimension_numbers=NT, preferred_element_type=jnp.float32)
     held[0] = first
-    held[1] = jnp.where(meta[0] % 2 == 0, chained, second)
-    send[0] = chained
-    send[1] = mm(pick, high) + mm(pick, low)
-
-
-def second_kernel(part, meta, held, came, weights, out, full, wide, sems):
+    held[1] = second
+    last = [matrix(m) for m in range(2, full.shape[0])]
+
+    @pl.when(x % 2 == 0)
+    def _():
+        chained = second - dot3(split(first), last[0], NT)
+        shape = (part, held.shape[2])
+        column = lax.broadcasted_iota(jnp.int32, shape, 0) + part * meta[1]
+        mine = lax.broadcasted_iota(jnp.int32, shape, 1) == column
+        pick = jnp.where(mine, jnp.where(meta[2] == 0, 1.0, 0.0), 0.0).astype(jnp.bfloat16)
+        mm = functools.partial(lax.dot_general, dimension_numbers=NT, preferred_element_type=jnp.float32)
+        held[1] = chained
+        send[0] = chained
+        send[1] = mm(pick, last[1][0]) + mm(pick, last[1][1])
+
+    @pl.when(x % 2 == 1)
+    def _():
+        for at, pair in enumerate(last):
+            high[at], low[at] = pair
+
+
+def second_kernel(part, meta, held, came, high, low, out, wide):
     wide[...] = jnp.zeros_like(wide)
+    step = 40
+
+    def store(at, value):
+        for copy in range(3):
+            wide[step * copy + part * at : step * copy + part * (at + 1), :] = value
 
     @pl.when(meta[0] % 2 == 0)
     def _():
-        wide[:part, :] = held[0]
-        wide[part : 2 * part, :] = held[1]
+        store(0, held[0])
+        store(1, held[1])
 
     @pl.when(meta[0] % 2 == 1)
     def _():
-        matrix = fetch(weights, full, sems, meta[0], [2, 3, 4, 5])
-        third = held[0] - dot3(split(came[0]), matrix(2), NT)
-        wide[:part, :] = third
-        fourth = held[1] - dot3(split(third), matrix(3), NT)
-        wide[part : 2 * part, :] = fourth
-        term = came[1] - dot3(split(fourth), matrix(4), NT)
-        wide[2 * part : 3 * part, :] = dot3(split(term), matrix(5), NT)
-
-    back = wide[...].T
-    out[...] = back.reshape(out.shape)
+        third = held[0] - dot3(split(came[0]), (high[0], low[0]), NT)
+        store(0, third)
+        fourth = held[1] - dot3(split(third), (high[1], low[1]), NT)
+        store(1, fourth)
+        term = came[1] - dot3(split(fourth), (high[2], low[2]), NT)
+        store(2, dot3(split(term), (high[3], low[3]), NT))
+
+    rows = wide[...].T.reshape(-1, 8, 128)
+    lane = lax.broadcasted_iota(jnp.int32, (rows.shape[0], 1, 128), 2)
+    for j in range(3):
+        far = min(6 + j, 7)
+        low_rows = jnp.where(lane < 80, rows[:, 3 + j : 4 + j], rows[:, far : far + 1])
+        out[:, j : j + 1, :] = jnp.where(lane < 40, rows[:, j : j + 1], low_rows)
+
+
+def unpack_kernel(part, got, sep, term, tall):
+    for src in range(got.shape[0]):
+        tall[8 * src : 8 * src + 3, :] = got[src]
+        tall[8 * src + 3 : 8 * src + 6, :] = got[src]
+        tall[8 * src + 6 : 8 * src + 8, :] = got[src, 0:2]
+    flat = tall[...]
+    row = lax.broadcasted_iota(jnp.int32, flat.shape, 0) % 8
+    flat = jnp.where(
+        row < 3, flat, jnp.where(row < 6, pltpu.roll(flat, 128 - 40, 1), pltpu.roll(flat, 128 - 80, 1))
+    )
+    lane = lax.broadcasted_iota(jnp.int32, (8, 128), 1)
+    tiles = sep.shape[3] // 128
+    full = [[jnp.zeros((8, 128), jnp.float32) for _ in range(tiles)] for _ in range(5)]
+    for src in range(got.shape[0]):
+        xl, xh, y, c = src // 32, src // 16 % 2, src // 2 % 8, src % 2
+        block = flat[8 * src : 8 * src + 8]
+        start = part * ((c * 2 + xl) * NY + y)
+        for at in range(2 + xh):
+            moved = pltpu.roll(block, (start - part * at) % 128, 1)
+            to = 2 * xh + at
+            for tile in range(start // 128, (start + part - 1) // 128 + 1):
+                at_lane = lane + 128 * tile
+                here = (at_lane >= start) & (at_lane < start + part)
+                full[to][tile] = jnp.where(here, moved, full[to][tile])
+    for tile in range(tiles):
+        lanes = slice(128 * tile, 128 * (tile + 1))
+        for k in range(4):
+            sep[0, k, :, lanes] = full[k][tile]
+        for layer in range(term.shape[0]):
+            term[layer, :, lanes] = full[4][tile]
+
+
+def in_hbm(array):
+    return pltpu.with_memory_space_constraint(array, pltpu.HBM)
 
 
 def body(
@@ -235,7 +283,7 @@
     ]
 
     meta = jnp.stack([parent[0, 0], c, lax.axis_index(ROW)]).astype(jnp.int32)
-    update = leaves(meta, leaf_rhs, leaf_inverse, leaf_coupling, sep_rhs)
+    update = leaves(meta, *map(in_hbm, (leaf_rhs, leaf_inverse, leaf_coupling, sep_rhs)))
     ring, update = lax.optimization_barrier((ring, update))
     weights = lax.all_gather(jnp.stack(ring), ("y", "c"))
     res = update[1] + lax.ppermute(update[0], "c", [(0, 1), (1, 0)])
@@ -251,34 +299,37 @@
     res = lax.all_to_all(res, "y", 0, 0)
 
     meta = jnp.stack([2 * xl + xh, (c * 2 + xl) * NY + y, layer]).astype(jnp.int32)
-    scratch = [pltpu.VMEM((4, 64, 8, width), jnp.float32)]
-    sems = [pltpu.SemaphoreType.DMA((4, NX))]
-    params = pltpu.CompilerParams(vmem_limit_bytes=32 * 2**20)
-    held, send = call(
+    held, send, high, low = call(
         functools.partial(first_kernel, part),
         in_specs=[SMEM, VMEM, HBM],
-        out_specs=[VMEM, VMEM],
-        out_shape=[FLAT((2, part, width), jnp.float32)] * 2,
-        scratch_shapes=scratch + sems,
-        compiler_params=params,
+        out_specs=[VMEM] * 4,
+        out_shape=[FLAT((2, part, width), jnp.float32)] * 2 + [FLAT((4, width, width), jnp.bfloat16)] * 2,
+        scratch_shapes=[pltpu.VMEM((6, 64, 8, width), jnp.float32), pltpu.SemaphoreType.DMA((6, NX))],
+        compiler_params=pltpu.CompilerParams(vmem_limit_bytes=32 * 2**20),
         name="chain_first",
-    )(meta, res, weights)
+    )(meta, res, in_hbm(weights))
     came = lax.ppermute(send, "xh", [(0, 1)])
     out = call(
         functools.partial(second_kernel, part),
-        in_specs=[SMEM, VMEM, VMEM, HBM],
+        in_specs=[SMEM] + [VMEM] * 4,
         out_specs=VMEM,
-        out_shape=FLAT((64, 8, 128), jnp.float32),
-        scratch_shapes=scratch + [pltpu.VMEM((128, width), jnp.float32)] + sems,
-        compiler_params=params,
+        out_shape=FLAT((64, 3, 128), jnp.float32),
+        scratch_shapes=[pltpu.VMEM((128, width), jnp.float32)],
+        compiler_params=pltpu.CompilerParams(vmem_limit_bytes=16 * 2**20),
         name="chain_second",
-    )(meta, held, came, weights)
-
-    out = lax.all_to_all(out, ROW, 0, 0)[:, :, : 3 * part]
-    out = out.reshape(2, 2, NY, NC, 8, 3, part).transpose(1, 5, 4, 3, 0, 2, 6).reshape(2, 3, 8, cols)
-    term = jnp.broadcast_to(out[1, 2][None], (8, 8, cols))
+    )(meta, held, came, high, low)
+
+    out = lax.all_to_all(out, ROW, 0, 0)
+    sep_out, term = call(
+        functools.partial(unpack_kernel, part),
+        in_specs=[VMEM],
+        out_specs=[VMEM] * 2,
+        out_shape=[FLAT((1, 4, 8, cols), jnp.float32), FLAT((8, 8, cols), jnp.float32)],
+        scratch_shapes=[pltpu.VMEM((64 * 8, 128), jnp.float32)],
+        name="unpack",
+    )(out)
     root_out = lax.all_to_all(term, "layer", 0, 0).sum(0)
-    return (out[:, :2].reshape(1, 4, 8, cols), root_out)
+    return (sep_out, root_out)
 
 
 def solution(mesh):

time: 150 us -> 144 us (0.960)
  blocking collectives: 47.7 us -> 59.9 us
  local copies, waits for them, and re-layouts: 9.79 us -> 0.12 us
  starting transfers between devices: 31.4 us -> 24.2 us
  waiting for transfers between devices: 33.5 us -> 26.7 us
  Pallas kernels: 10 us -> 15.1 us
    all_to_all x1 -> x2, blocking collectives: 23.5 us -> 35.9 us  [the longest x1 21.4 us: body(): out = lax.all_to_all(out, ROW, 0, 0)]
    unnamed x14 -> x2, local copies, waits for them, and re-layouts: 7.13 us -> 0.01 us
    all_to_all x1 -> x0, starting transfers between devices: 7.1 us -> none  [body(): root_out = lax.all_to_all(term, 'layer', 0, 0).sum(0)]
    all_to_all x1 -> x0, waiting for transfers between devices: 6.83 us -> none  [body(): root_out = lax.all_to_all(term, 'layer', 0, 0).sum(0)]
    pallas_call x1 -> x2, Pallas kernels: 0.85 us -> 2.67 us  [the longest x1 1.95 us: body(): call(functools.partial(unpack_kernel, part), in_specs=[VMEM], out_specs=[...]
    pallas_call x1, Pallas kernels: 3.48 us -> 5.22 us  [leaves(): pl.pallas_call(functools.partial(leaf_kernel, part), grid_spec=pltpu.Pref...]
    pallas_call x1, Pallas kernels: 3.02 us -> 4.59 us  [body(): call(functools.partial(first_kernel, part), in_specs=[SMEM, VMEM, HBM], o...]
  transfers between devices with their start and end apart: 8 -> 7, of which waited for: 5 -> 4; matrix products, arithmetic and copies ran while one was open for 1% -> 0% of each run, Pallas kernels for 3% -> 4%
where the time goes in v4:
time: 144 us; the launch traced here: 143 us
  blocking collectives  59.9 us (42%)
  waiting for transfers between devices  26.7 us (19%)
  starting transfers between devices  24.2 us (17%)
  Pallas kernels  15.1 us (10%)
  between operations  14.8 us (10%)
  other arithmetic  1.8 us (1%)
    all_to_all x1, blocking collectives, body(): res = lax.all_to_all(res.reshape(NX, 2 * tiles * 8 * part, 128), X, 0, 0)  23.9 us
    all_to_all x1, blocking collectives, body(): out = lax.all_to_all(out, ROW, 0, 0)  21.4 us
    all_to_all x1, waiting for transfers between devices, body(): res = lax.all_to_all(res, 'y', 0, 0)  18.4 us
    all_to_all x1, blocking collectives, body(): root_out = lax.all_to_all(term, 'layer', 0, 0).sum(0)  14.5 us
    ppermute x3, starting transfers between devices, body(): lax.ppermute(pack, X, [(i, (i + j) % NX) for i in range(NX)])  10.8 us
    ppermute x1, starting transfers between devices, body(): res = update[1] + lax.ppermute(update[0], 'c', [(0, 1), (1, 0)])  7.29 us
    pallas_call x1, Pallas kernels, leaves(): pl.pallas_call(functools.partial(leaf_kernel, part), grid_spec=pltpu.Pref...  5.22 us
    pallas_call x1, Pallas kernels, body(): call(functools.partial(first_kernel, part), in_specs=[SMEM, VMEM, HBM], o...  4.59 us
  transfers between devices with their start and end apart: 7, of which 4 were waited for; matrix products, arithmetic and copies ran while one was open for 0% of the time, Pallas kernels for 4%

profile of v4, /device:TPU:1, one launch (start us, length us, event | category | flops | bytes accessed | tf_op | source)
XLA Modules:
  0.0 142.7 jit_solution(7222060707910744584)
XLA Ops:
  7.2 0.0 all-gather.3.cloned.1.call-start
  7.2 1.6 %pack.1 = (f32[6,8,512]{2,1,0:T(8,128)}, f32[6,8,512]{2,1,0:T(8,128)}) custom-call(s32[1]{0:T(128)} %bitcast.3.meta, f32[1,4,8,512]{3,2,1,0:T(8,128)} %sep_inverse.1, f32[1,3,8,512]{3,2,1,0:T(8,128)} %sep_coupling.1, f32[1,8,512]{2,1,0:T(8,128)} %root_coupling.1, f32[8,384]{1,0:T(8,128)} %root_rhs.1, f32[8,512]{1,0:T(8,128)} %root_inverse.1), custom_call_target="tpu_custom_call" | custom-call | tf_op jit(solution)/shard_map/pack/pallas_call | solution.py:273
  8.8 3.9 %collective-permute-start = (f32[6,8,512]{2,1,0:T(8,128)}, f32[6,8,512]{2,1,0:T(8,128)S(1)}, u32[]{:S(2)}, u32[]{:S(2)}) collective-permute-start(f32[6,8,512]{2,1,0:T(8,128)} %get-tuple-element.16), channel_id=1, source_target_pairs={{0,16},{16,32},{32,48},{48,0},{1,17},{17,33},{33,49},{49,1},{2,18}... | collective-permute-start | bytes 294920 | tf_op jit(solution)/shard_map/ppermute | solution.py:281
  12.8 3.2 %collective-permute-start.2 = (f32[6,8,512]{2,1,0:T(8,128)}, f32[6,8,512]{2,1,0:T(8,128)S(1)}, u32[]{:S(2)}, u32[]{:S(2)}) collective-permute-start(f32[6,8,512]{2,1,0:T(8,128)} %get-tuple-element.16), channel_id=1, source_target_pairs={{0,48},{16,0},{32,16},{48,32},{1,49},{17,1},{33,17},{49,33},{2,50}... | collective-permute-start | bytes 294920 | tf_op jit(solution)/shard_map/ppermute | solution.py:281
  15.9 3.6 %collective-permute-start.1 = (f32[6,8,512]{2,1,0:T(8,128)}, f32[6,8,512]{2,1,0:T(8,128)S(1)}, u32[]{:S(2)}, u32[]{:S(2)}) collective-permute-start(f32[6,8,512]{2,1,0:T(8,128)} %get-tuple-element.18), channel_id=1, source_target_pairs={{0,32},{16,48},{32,0},{48,16},{1,33},{17,49},{33,1},{49,17},{2,34}... | collective-permute-start | bytes 294920 | tf_op jit(solution)/shard_map/ppermute | solution.py:281
  20.2 0.1 pad_add_fusion.1.meta
  20.3 0.0 copy-start
  20.3 5.2 %leaves.1 = f32[2,2,2,2,4,96,128]{6,5,4,3,2,1,0:T(8,128)S(1)} custom-call(s32[3]{0:T(128)S(1)} %pad_add_fusion.1.meta, f32[1,1,256,384]{3,2,1,0:T(8,128)} %rhs.1, f32[1,1,256,256]{3,2,1,0:T(8,128)} %inv.1, f32[1,1,4,512,256]{4,3,2,1,0:T(8,128)} %coupling.1, f32[1,4,8,384]{3,2,1,0:T(8,128)} %sep.1), custom_call_target="tpu_custom_call" | custom-call | tf_op jit(solution)/shard_map/leaves/pallas_call | solution.py:101
  25.6 0.0 collective-permute-done
  25.6 0.0 collective-permute-done.1
  25.6 0.0 collective-permute-done.2
  25.6 0.0 copy-done
  25.6 0.8 pad_maximum_fusion
  26.4 0.0 all-gather.3.cloned.1.call-update
  26.4 0.1 slice_bitcast_fusion
  26.5 7.3 %collective-permute-start.3 = (f32[2,2,2,4,96,128]{5,4,3,2,1,0:T(8,128)S(1)}, f32[2,2,2,4,96,128]{5,4,3,2,1,0:T(8,128)S(1)}, u32[]{:S(2)}, u32[]{:S(2)}) collective-permute-start(f32[2,2,2,4,96,128]{5,4,3,2,1,0:T(8,128)S(1)} %slice_bitcast_fusion), channel_id=1, source_target_pairs={{0,1},{1,0},{2,3},{3,2},{4,5},{5,4},{6,7},{7,6},{8,9},{9,8},{10,11... | collective-permute-start | bytes 4718600 | tf_op jit(solution)/shard_map/ppermute | solution.py:289
  33.8 3.0 %collective-permute-done.3 = f32[2,2,2,4,96,128]{5,4,3,2,1,0:T(8,128)S(1)} collective-permute-done((f32[2,2,2,4,96,128]{5,4,3,2,1,0:T(8,128)S(1)}, f32[2,2,2,4,96,128]{5,4,3,2,1,0:T(8,128)S(1)}, u32[]{:S(2)}, u32[]{:S(2)}) %collective-permute-start.3) | collective-permute-done | bytes 1572896 | tf_op jit(solution)/shard_map/ppermute | solution.py:289
  36.8 0.2 bitcast_add_fusion
  37.1 23.9 %all_to_all.20.parts = f32[4,768,128]{2,1,0:T(8,128)S(1)} all-to-all(f32[4,768,128]{2,1,0:T(8,128)S(1)} %bitcast.19), channel_id=1, replica_groups=mesh['layer'=8,'xl'=2,'xh'=2,'y'=8,'c'=2] {'xl','xh'}, dimensions={0} | all-to-all | bytes 3145728 | tf_op jit(solution)/shard_map/all_to_all | solution.py:290
  61.0 1.1 sum_x.1
  62.1 3.5 %all-to-all-start.1 = ((f32[8,96,128]{2,1,0:T(8,128)}), f32[8,96,128]{2,1,0:T(8,128)S(1)}, u32[]{:S(2)}, u32[]{:S(2)}) async-start(f32[8,96,128]{2,1,0:T(8,128)} %sum_x.1), calls=%async_computation.1 | async-start | bytes 786432 | tf_op jit(solution)/shard_map/all_to_all | solution.py:299
  65.6 0.1 pad_add_fusion.meta
  65.6 18.4 %all-to-all-done.1.parts = f32[8,96,128]{2,1,0:T(8,128)S(1)} async-done(((f32[8,96,128]{2,1,0:T(8,128)}), f32[8,96,128]{2,1,0:T(8,128)S(1)}, u32[]{:S(2)}, u32[]{:S(2)}) %all-to-all-start.1) | async-done | bytes 393248 | tf_op jit(solution)/shard_map/all_to_all | solution.py:299
  84.0 4.0 %all-gather.3.cloned.1.call-done = f32[64,6,8,512]{3,2,1,0:T(8,128)} async-done(((f32[4,6,8,512]{3,2,1,0:T(8,128)}), f32[64,6,8,512]{3,2,1,0:T(8,128)}) %all-gather.3.cloned.1.call-update) | async-done | bytes 6291472 | tf_op jit(solution)/shard_map/all_gather | solution.py:288
  88.0 4.6 %chain_first.1 = (f32[2,12,512]{2,1,0:T(8,128)S(1)}, f32[2,12,512]{2,1,0:T(8,128)S(1)}, bf16[4,512,512]{2,1,0:T(8,128)(2,1)S(1)}, bf16[4,512,512]{2,1,0:T(8,128)(2,1)S(1)}) custom-call(s32[3]{0:T(128)S(1)} %pad_add_fusion.meta, f32[8,96,128]{2,1,0:T(8,128)S(1)} %all-to-all-done.1.parts, f32[16,4,6,8,512]{4,3,2,1,0:T(8,128)} %bitcast.18), custom_call_target="tpu_custom_call" | custom-call | tf_op jit(solution)/shard_map/chain_first/pallas_call | solution.py:302
  92.6 2.7 %collective-permute-start.4 = (f32[2,12,512]{2,1,0:T(8,128)S(1)}, f32[2,12,512]{2,1,0:T(8,128)S(1)}, u32[]{:S(2)}, u32[]{:S(2)}) collective-permute-start(f32[2,12,512]{2,1,0:T(8,128)S(1)} %get-tuple-element.23), channel_id=1, source_target_pairs={{0,16},{1,17},{2,18},{3,19},{4,20},{5,21},{6,22},{7,23},{8,24},{9,... | collective-permute-start | bytes 147464 | tf_op jit(solution)/shard_map/ppermute | solution.py:311
  95.3 1.3 collective-permute-done.4.came
  96.6 0.7 chain_second.1
  97.3 21.4 %all_to_all.21.got = f32[64,3,128]{2,1,0:T(4,128)} all-to-all(f32[64,3,128]{2,1,0:T(4,128)S(1)} %chain_second.1), channel_id=1, replica_groups=mesh['layer'=8,'xl'=2,'xh'=2,'y'=8,'c'=2] {'xl','xh','y','c'}, dimensions={0} | all-to-all | bytes 196608 | tf_op jit(solution)/shard_map/all_to_all | solution.py:322
  118.7 2.0 %unpack.1 = (f32[1,4,8,384]{3,2,1,0:T(8,128)}, f32[8,8,384]{2,1,0:T(8,128)}) custom-call(f32[64,3,128]{2,1,0:T(4,128)} %all_to_all.21.got), custom_call_target="tpu_custom_call" | custom-call | tf_op jit(solution)/shard_map/unpack/pallas_call | solution.py:323
  120.7 14.5 %all_to_all.22 = f32[8,8,384]{2,1,0:T(8,128)S(1)} all-to-all(f32[8,8,384]{2,1,0:T(8,128)} %get-tuple-element.27), channel_id=1, replica_groups=mesh['layer'=8,'xl'=2,'xh'=2,'y'=8,'c'=2] {'layer'}, dimensions={0} | all-to-all | bytes 196608 | tf_op jit(solution)/shard_map/all_to_all | solution.py:331
  135.2 0.6 reduce_sum.9
Async XLA Ops:
  7.2 80.8 %all-gather.3.cloned.1.call-start = ((), (), s32[]{:S(2)}) async-start(), calls=%async_computation.4 | async-start | bytes 6684672 | tf_op jit(solution)/shard_map/all_gather | solution.py:288
  8.8 16.7 %collective-permute-start = (f32[6,8,512]{2,1,0:T(8,128)}, f32[6,8,512]{2,1,0:T(8,128)S(1)}, u32[]{:S(2)}, u32[]{:S(2)}) collective-permute-start(f32[6,8,512]{2,1,0:T(8,128)} %get-tuple-element.16), channel_id=1, source_target_pairs={{0,16},{16,32},{32,48},{48,0},{1,17},{17,33},{33,49},{49,1},{2,18}... | collective-permute-start | bytes 294920 | tf_op jit(solution)/shard_map/ppermute | solution.py:281
  12.8 12.8 %collective-permute-start.2 = (f32[6,8,512]{2,1,0:T(8,128)}, f32[6,8,512]{2,1,0:T(8,128)S(1)}, u32[]{:S(2)}, u32[]{:S(2)}) collective-permute-start(f32[6,8,512]{2,1,0:T(8,128)} %get-tuple-element.16), channel_id=1, source_target_pairs={{0,48},{16,0},{32,16},{48,32},{1,49},{17,1},{33,17},{49,33},{2,50}... | collective-permute-start | bytes 294920 | tf_op jit(solution)/shard_map/ppermute | solution.py:281
  15.9 9.6 %collective-permute-start.1 = (f32[6,8,512]{2,1,0:T(8,128)}, f32[6,8,512]{2,1,0:T(8,128)S(1)}, u32[]{:S(2)}, u32[]{:S(2)}) collective-permute-start(f32[6,8,512]{2,1,0:T(8,128)} %get-tuple-element.18), channel_id=1, source_target_pairs={{0,32},{16,48},{32,0},{48,16},{1,33},{17,49},{33,1},{49,17},{2,34}... | collective-permute-start | bytes 294920 | tf_op jit(solution)/shard_map/ppermute | solution.py:281
  20.3 5.3 %copy-start = (f32[6,8,512]{2,1,0:T(8,128)S(1)}, f32[6,8,512]{2,1,0:T(8,128)}, u32[]{:S(2)}) copy-start(f32[6,8,512]{2,1,0:T(8,128)} %get-tuple-element.18) | copy-start | bytes 294916
  26.5 10.3 %collective-permute-start.3 = (f32[2,2,2,4,96,128]{5,4,3,2,1,0:T(8,128)S(1)}, f32[2,2,2,4,96,128]{5,4,3,2,1,0:T(8,128)S(1)}, u32[]{:S(2)}, u32[]{:S(2)}) collective-permute-start(f32[2,2,2,4,96,128]{5,4,3,2,1,0:T(8,128)S(1)} %slice_bitcast_fusion), channel_id=1, source_target_pairs={{0,1},{1,0},{2,3},{3,2},{4,5},{5,4},{6,7},{7,6},{8,9},{9,8},{10,11... | collective-permute-start | bytes 4718600 | tf_op jit(solution)/shard_map/ppermute | solution.py:289
  62.1 21.9 %all-to-all-start.1 = ((f32[8,96,128]{2,1,0:T(8,128)}), f32[8,96,128]{2,1,0:T(8,128)S(1)}, u32[]{:S(2)}, u32[]{:S(2)}) async-start(f32[8,96,128]{2,1,0:T(8,128)} %sum_x.1), calls=%async_computation.1 | async-start | bytes 786432 | tf_op jit(solution)/shard_map/all_to_all | solution.py:299
  92.6 4.0 %collective-permute-start.4 = (f32[2,12,512]{2,1,0:T(8,128)S(1)}, f32[2,12,512]{2,1,0:T(8,128)S(1)}, u32[]{:S(2)}, u32[]{:S(2)}) collective-permute-start(f32[2,12,512]{2,1,0:T(8,128)S(1)} %get-tuple-element.23), channel_id=1, source_target_pairs={{0,16},{1,17},{2,18},{3,19},{4,20},{5,21},{6,22},{7,23},{8,24},{9,... | collective-permute-start | bytes 147464 | tf_op jit(solution)/shard_map/ppermute | solution.py:311
Sparse Core Ops, SparseCore 0:
  26.5 61.3 all-gather.2

commit v5 on v4

--- a/solution.py
+++ b/solution.py
@@ -28,14 +28,14 @@
     return mm(a[0], b[0]) + (mm(a[0], b[1]) + mm(a[1], b[0]))
 
 
-def by_tiles(ref, part):
+def by_tiles(ref, part, base):
     tiles, rows, _ = ref.shape
 
     def column(tile):
         return jnp.concatenate(
             [
-                ref[tile, pl.ds(base + t, 8, stride=part), :]
-                for base in range(0, rows, 8 * part)
+                ref[tile, pl.ds(base + block + t, 8, stride=part), :]
+                for block in range(0, rows // NC, 8 * part)
                 for t in range(part)
             ],
             axis=0,
@@ -44,7 +44,12 @@
     return jnp.concatenate([column(tile) for tile in range(tiles)], axis=1)
 
 
-def pack_kernel(meta, sep_inverse, sep_coupling, root_coupling, root_rhs, root_inverse, same, other):
+def place():
+    x = 2 * lax.axis_index("xl") + lax.axis_index("xh")
+    return x, (x * NY + lax.axis_index("y")) * NC + lax.axis_index("c")
+
+
+def pack_kernel(sep_inverse, sep_coupling, root_coupling, root_rhs, root_inverse, same, other):
     zeros = jnp.zeros_like(root_inverse)
     rr = jnp.concatenate([root_rhs[...], zeros[:, root_rhs.shape[1] :]], axis=1)
     tables = (
@@ -60,71 +65,90 @@
     )
     for side in range(2):
 
-        @pl.when(meta[0] == side)
+        @pl.when(lax.axis_index("xh") == side)
         def _():
             for m in range(same.shape[0]):
                 same[m] = tables[side][m]
                 other[m] = tables[1 - side][m]
 
 
-def leaf_kernel(part, meta, rhs, inv, coupling, sep, out, xt, xt_hi, xt_lo, place, own):
+def half_update(part, other, parent, xt, coupling, sep, out, xt_hi, xt_lo, tall, own):
     k = pl.program_id(0)
-    parent, core, block = meta[0], meta[1], meta[2]
+    core = lax.axis_index("c")
+    base = (1 - core if other else core) * (xt.shape[1] // NC)
 
     @pl.when(k == 0)
+    def _():
+        xt_hi[...], xt_lo[...] = split(by_tiles(xt, part, base))
+        tall[...] = jnp.zeros_like(tall)
+
+    keep = jnp.where(k >= parent[0, 0], 1.0, 0.0)
+    got = dot3((xt_hi[...], xt_lo[...]), split(coupling[0, 0, 0]), NT) * -keep
+    block = place()[1]
+    tall[pl.ds(pl.multiple_of(8 * (block % 16), 8), 8), :] = sep[0, 0]
+    own[0] = tall[...].T
+    mine = by_tiles(own, part, base)
+    group = 8 * part
+    for side in range(2):
+        rows = slice(side * group, (side + 1) * group)
+        for tile in range(out.shape[3]):
+            out[side, 0, 0, tile] = got[rows, 128 * tile : 128 * (tile + 1)]
+        out[side, 0, 0, block // 16] += mine[rows]
+
+
+def send_kernel(part, parent, rhs, inv, coupling, sep, out, xt, *scratch):
+    @pl.when(pl.program_id(0) == 0)
     def _():
         solved = dot3(split(inv[0, 0]), split(rhs[0, 0]), NN).T
         for tile in range(xt.shape[0]):
             xt[tile] = solved[:, 128 * tile : 128 * (tile + 1)]
-        xt_hi[...], xt_lo[...] = split(by_tiles(xt, part))
-        place[...] = jnp.zeros_like(place)
-
-    keep = jnp.where(k >= parent, 1.0, 0.0)
-    got = dot3((xt_hi[...], xt_lo[...]), split(coupling[0, 0, 0]), NT) * -keep
-    place[pl.ds(pl.multiple_of(8 * (block % 16), 8), 8), :] = sep[0, 0]
-    own[0] = place[...].T
-    mine = by_tiles(own, part)
-    group = 8 * part
-    for half in range(NC):
-        slot = jnp.where(core == half, 1, 0)
-        for side in range(2):
-            rows = slice((half * 2 + side) * group, (half * 2 + side + 1) * group)
-            for tile in range(out.shape[4]):
-                out[slot, side, 0, 0, tile] = got[rows, 128 * tile : 128 * (tile + 1)]
-            out[slot, side, 0, 0, block // 16] += mine[rows]
-
-
-def leaves(meta, rhs, inv, coupling, sep):
+
+    half_update(part, True, parent, xt, coupling, sep, out, *scratch)
+
+
+def keep_kernel(part, parent, xt, coupling, sep, out, *scratch):
+    half_update(part, False, parent, xt, coupling, sep, out, *scratch)
+
+
+def leaves(parent, rhs, inv, coupling, sep):
     n, width = coupling.shape[2], coupling.shape[3]
     leaf, cols = rhs.shape[2], rhs.shape[3]
-    part = cols // 32
-    return pl.pallas_call(
-        functools.partial(leaf_kernel, part),
-        grid_spec=pltpu.PrefetchScalarGridSpec(
-            num_scalar_prefetch=1,
-            grid=(n,),
-            in_specs=[
-                pl.BlockSpec((1, 1, leaf, cols), lambda k, m: (0, 0, 0, 0)),
-                pl.BlockSpec((1, 1, leaf, leaf), lambda k, m: (0, 0, 0, 0)),
-                pl.BlockSpec((1, 1, 1, width, leaf), lambda k, m: (0, 0, k, 0, 0)),
-                pl.BlockSpec((1, 1, 8, cols), lambda k, m: (0, k, 0, 0)),
-            ],
-            out_specs=pl.BlockSpec(
-                (NC, 2, 1, 1, width // 128, 8 * part, 128),
-                lambda k, m: (0, 0, k // 2, k % 2, 0, 0, 0),
-            ),
-            scratch_shapes=[
-                pltpu.VMEM((leaf // 128, cols, 128), jnp.float32),
-                pltpu.VMEM((cols, leaf), jnp.bfloat16),
-                pltpu.VMEM((cols, leaf), jnp.bfloat16),
-                pltpu.VMEM((128, cols), jnp.float32),
-                pltpu.VMEM((1, cols, 128), jnp.float32),
-            ],
-        ),
-        out_shape=FLAT((NC, 2, 2, 2, width // 128, 8 * part, 128), jnp.float32),
+    part, tiles = cols // 32, width // 128
+    one = lambda *shape: pl.BlockSpec(shape, lambda k: (0,) * len(shape))
+    per_level = [
+        pl.BlockSpec((1, 1, 1, width, leaf), lambda k: (0, 0, k, 0, 0)),
+        pl.BlockSpec((1, 1, 8, cols), lambda k: (0, k, 0, 0)),
+    ]
+    half_spec = pl.BlockSpec((2, 1, 1, tiles, 8 * part, 128), lambda k: (0, k // 2, k % 2, 0, 0, 0))
+    half_shape = FLAT((2, 2, 2, tiles, 8 * part, 128), jnp.float32)
+    xt_spec = one(leaf // 128, cols, 128)
+    common = dict(
+        grid=(n,),
+        scratch_shapes=[
+            pltpu.VMEM((cols // NC, leaf), jnp.bfloat16),
+            pltpu.VMEM((cols // NC, leaf), jnp.bfloat16),
+            pltpu.VMEM((128, cols), jnp.float32),
+            pltpu.VMEM((1, cols, 128), jnp.float32),
+        ],
         compiler_params=pltpu.CompilerParams(vmem_limit_bytes=24 * 2**20),
-        name="leaves",
-    )(meta, rhs, inv, coupling, sep)
+    )
+    send, xt = pl.pallas_call(
+        functools.partial(send_kernel, part),
+        in_specs=[SMEM, one(1, 1, leaf, cols), one(1, 1, leaf, leaf)] + per_level,
+        out_specs=[half_spec, xt_spec],
+        out_shape=[half_shape, FLAT((leaf // 128, cols, 128), jnp.float32)],
+        name="leaves_send",
+        **common,
+    )(parent, rhs, inv, coupling, sep)
+    keep = pl.pallas_call(
+        functools.partial(keep_kernel, part),
+        in_specs=[SMEM, xt_spec] + per_level,
+        out_specs=half_spec,
+        out_shape=half_shape,
+        name="leaves_keep",
+        **common,
+    )(parent, xt, coupling, sep)
+    return send, keep
 
 
 def sum_kernel(parts, out):
@@ -134,23 +158,34 @@
         out[s] = (parts[0, rows, :] + parts[1, rows, :]) + (parts[2, rows, :] + parts[3, rows, :])
 
 
-def first_kernel(part, meta, parts, weights, held, send, high, low, full, sems):
-    x = meta[0]
-    copies = []
-    for m in range(full.shape[0]):
-        copies.append([])
-        for back in range(NX):
-            rows = pl.multiple_of(((x + NX - back) % NX) * 16, 16)
-            copy = pltpu.make_async_copy(
-                weights.at[:, back, m], full.at[m, pl.ds(rows, 16)], sems.at[m, back]
+def first_kernel(part, parts, weights, held, send, high, low, full, sems):
+    x, _ = place()
+    odd = x % 2 == 1
+
+    def copies(m):
+        return [
+            pltpu.make_async_copy(
+                weights.at[:, back, m],
+                full.at[m, pl.ds(pl.multiple_of(((x + NX - back) % NX) * 16, 16), 16)],
+                sems.at[m, back],
             )
-            copy.start()
-            copies[-1].append(copy)
+            for back in range(NX)
+        ]
 
     def matrix(m):
-        for copy in copies[m]:
+        for copy in copies(m):
             copy.wait()
         return split(full[m].reshape(-1, full.shape[3]))
+
+    for m in range(4):
+        for copy in copies(m):
+            copy.start()
+
+    @pl.when(odd)
+    def _():
+        for m in range(4, full.shape[0]):
+            for copy in copies(m):
+                copy.start()
 
     res = parts[0]
     for p in range(1, parts.shape[0]):
@@ -165,27 +200,30 @@
     second = dot3(residual(1), matrix(1), NT)
     held[0] = first
     held[1] = second
-    last = [matrix(m) for m in range(2, full.shape[0])]
-
-    @pl.when(x % 2 == 0)
+    last = [matrix(2), matrix(3)]
+
+    @pl.when(jnp.logical_not(odd))
     def _():
         chained = second - dot3(split(first), last[0], NT)
         shape = (part, held.shape[2])
-        column = lax.broadcasted_iota(jnp.int32, shape, 0) + part * meta[1]
+        group = (lax.axis_index("c") * 2 + lax.axis_index("xl")) * NY + lax.axis_index("y")
+        column = lax.broadcasted_iota(jnp.int32, shape, 0) + part * group
         mine = lax.broadcasted_iota(jnp.int32, shape, 1) == column
-        pick = jnp.where(mine, jnp.where(meta[2] == 0, 1.0, 0.0), 0.0).astype(jnp.bfloat16)
+        pick = jnp.where(mine, jnp.where(lax.axis_index("layer") == 0, 1.0, 0.0), 0.0).astype(jnp.bfloat16)
         mm = functools.partial(lax.dot_general, dimension_numbers=NT, preferred_element_type=jnp.float32)
         held[1] = chained
         send[0] = chained
         send[1] = mm(pick, last[1][0]) + mm(pick, last[1][1])
 
-    @pl.when(x % 2 == 1)
+    @pl.when(odd)
     def _():
         for at, pair in enumerate(last):
             high[at], low[at] = pair
-
-
-def second_kernel(part, meta, held, came, high, low, out, wide):
+        for m in range(4, full.shape[0]):
+            high[m - 2], low[m - 2] = matrix(m)
+
+
+def second_kernel(part, held, came, high, low, out, wide):
     wide[...] = jnp.zeros_like(wide)
     step = 40
 
@@ -193,12 +231,12 @@
         for copy in range(3):
             wide[step * copy + part * at : step * copy + part * (at + 1), :] = value
 
-    @pl.when(meta[0] % 2 == 0)
+    @pl.when(lax.axis_index("xh") == 0)
     def _():
         store(0, held[0])
         store(1, held[1])
 
-    @pl.when(meta[0] % 2 == 1)
+    @pl.when(lax.axis_index("xh") == 1)
     def _():
         third = held[0] - dot3(split(came[0]), (high[0], low[0]), NT)
         store(0, third)
@@ -263,8 +301,6 @@
     root_rhs,
     root_inverse,
 ):
-    xl, xh = lax.axis_index("xl"), lax.axis_index("xh")
-    y, c, layer = lax.axis_index("y"), lax.axis_index("c"), lax.axis_index("layer")
     width, cols = leaf_coupling.shape[3], leaf_rhs.shape[3]
     part = cols // 32
     tiles = width // 128
@@ -272,21 +308,19 @@
 
     same, other = call(
         pack_kernel,
-        in_specs=[SMEM] + [VMEM] * 5,
+        in_specs=[VMEM] * 5,
         out_specs=[VMEM, VMEM],
         out_shape=[FLAT((6, 8, width), jnp.float32)] * 2,
         name="pack",
-    )(xh.reshape(1).astype(jnp.int32), sep_inverse, sep_coupling, root_coupling, root_rhs, root_inverse)
+    )(sep_inverse, sep_coupling, root_coupling, root_rhs, root_inverse)
     ring = [same] + [
         lax.ppermute(pack, X, [(i, (i + j) % NX) for i in range(NX)])
         for j, pack in ((1, other), (2, same), (3, other))
     ]
 
-    meta = jnp.stack([parent[0, 0], c, lax.axis_index(ROW)]).astype(jnp.int32)
-    update = leaves(meta, *map(in_hbm, (leaf_rhs, leaf_inverse, leaf_coupling, sep_rhs)))
-    ring, update = lax.optimization_barrier((ring, update))
     weights = lax.all_gather(jnp.stack(ring), ("y", "c"))
-    res = update[1] + lax.ppermute(update[0], "c", [(0, 1), (1, 0)])
+    send, keep = leaves(parent, *map(in_hbm, (leaf_rhs, leaf_inverse, leaf_coupling, sep_rhs)))
+    res = keep + lax.ppermute(send, "c", [(0, 1), (1, 0)])
     res = lax.all_to_all(res.reshape(NX, 2 * tiles * 8 * part, 128), X, 0, 0)
     res = call(
         sum_kernel,
@@ -298,26 +332,25 @@
     )(res)
     res = lax.all_to_all(res, "y", 0, 0)
 
-    meta = jnp.stack([2 * xl + xh, (c * 2 + xl) * NY + y, layer]).astype(jnp.int32)
     held, send, high, low = call(
         functools.partial(first_kernel, part),
-        in_specs=[SMEM, VMEM, HBM],
+        in_specs=[VMEM, HBM],
         out_specs=[VMEM] * 4,
         out_shape=[FLAT((2, part, width), jnp.float32)] * 2 + [FLAT((4, width, width), jnp.bfloat16)] * 2,
         scratch_shapes=[pltpu.VMEM((6, 64, 8, width), jnp.float32), pltpu.SemaphoreType.DMA((6, NX))],
         compiler_params=pltpu.CompilerParams(vmem_limit_bytes=32 * 2**20),
         name="chain_first",
-    )(meta, res, in_hbm(weights))
+    )(res, in_hbm(weights))
     came = lax.ppermute(send, "xh", [(0, 1)])
     out = call(
         functools.partial(second_kernel, part),
-        in_specs=[SMEM] + [VMEM] * 4,
+        in_specs=[VMEM] * 4,
         out_specs=VMEM,
         out_shape=FLAT((64, 3, 128), jnp.float32),
         scratch_shapes=[pltpu.VMEM((128, width), jnp.float32)],
         compiler_params=pltpu.CompilerParams(vmem_limit_bytes=16 * 2**20),
         name="chain_second",
-    )(meta, held, came, high, low)
+    )(held, came, high, low)
 
     out = lax.all_to_all(out, ROW, 0, 0)
     sep_out, term = call(

time: 144 us -> 141 us (0.979)
  blocking collectives: 59.9 us -> 81.1 us
  waiting for transfers between devices: 26.7 us -> 5.58 us
  starting transfers between devices: 24.2 us -> 20.6 us
    all_to_all x0 -> x1, blocking collectives: none -> 21.4 us  [body(): res = lax.all_to_all(res, 'y', 0, 0)]
    all_to_all x1 -> x0, waiting for transfers between devices: 18.4 us -> none  [body(): res = lax.all_to_all(res, 'y', 0, 0)]
    ppermute x3, waiting for transfers between devices: 0.01 us -> 4.25 us  [body(): lax.ppermute(pack, X, [(i, (i + j) % NX) for i in range(NX)])]
    all_gather x1, waiting for transfers between devices: 3.95 us -> 0.01 us  [body(): weights = lax.all_gather(jnp.stack(ring), ('y', 'c'))]
    all_to_all x1 -> x0, starting transfers between devices: 3.45 us -> none  [body(): res = lax.all_to_all(res, 'y', 0, 0)]
    ppermute x1, waiting for transfers between devices: 3.01 us -> 0.01 us  [body(): res = keep + lax.ppermute(send, 'c', [(0, 1), (1, 0)])]
    pallas_call x4 -> x5, Pallas kernels: 12.1 us -> 13.5 us  [the longest x1 4.39 us: leaves(): pl.pallas_call(functools.partial(send_kernel, part), in_specs=[SMEM, one(...]
  transfers between devices with their start and end apart: 7 -> 6, of which waited for: 4 -> 3; matrix products, arithmetic and copies ran while one was open for 0% -> 0% of each run, Pallas kernels for 4% -> 6%
where the time goes in v5:
time: 141 us; the launch traced here: 140 us
  blocking collectives  81.1 us (58%)
  starting transfers between devices  20.6 us (15%)
  Pallas kernels  15.8 us (11%)
  between operations  14.8 us (10%)
  waiting for transfers between devices  5.58 us (4%)
  other arithmetic  2.48 us (2%)
    all_to_all x1, blocking collectives, body(): res = lax.all_to_all(res.reshape(NX, 2 * tiles * 8 * part, 128), X, 0, 0)  23.4 us
    all_to_all x1, blocking collectives, body(): out = lax.all_to_all(out, ROW, 0, 0)  21.9 us
    all_to_all x1, blocking collectives, body(): res = lax.all_to_all(res, 'y', 0, 0)  21.4 us
    all_to_all x1, blocking collectives, body(): root_out = lax.all_to_all(term, 'layer', 0, 0).sum(0)  14.4 us
    ppermute x3, starting transfers between devices, body(): lax.ppermute(pack, X, [(i, (i + j) % NX) for i in range(NX)])  10.1 us
    ppermute x1, starting transfers between devices, body(): res = keep + lax.ppermute(send, 'c', [(0, 1), (1, 0)])  7.58 us
    pallas_call x1, Pallas kernels, leaves(): pl.pallas_call(functools.partial(send_kernel, part), in_specs=[SMEM, one(...  4.39 us
    ppermute x3, waiting for transfers between devices, body(): lax.ppermute(pack, X, [(i, (i + j) % NX) for i in range(NX)])  4.25 us
  transfers between devices with their start and end apart: 6, of which 3 were waited for; matrix products, arithmetic and copies ran while one was open for 0% of the time, Pallas kernels for 6%

profile of v5, /device:TPU:1, one launch (start us, length us, event | category | flops | bytes accessed | tf_op | source)
XLA Modules:
  0.0 140.3 jit_solution(10469615376893139895)
XLA Ops:
  7.2 0.0 all-gather.3.cloned.1.call-start
  7.2 1.6 %pack.1 = (f32[6,8,512]{2,1,0:T(8,128)}, f32[6,8,512]{2,1,0:T(8,128)}) custom-call(f32[1,4,8,512]{3,2,1,0:T(8,128)} %sep_inverse.1, f32[1,3,8,512]{3,2,1,0:T(8,128)} %sep_coupling.1, f32[1,8,512]{2,1,0:T(8,128)} %root_coupling.1, f32[8,384]{1,0:T(8,128)} %root_rhs.1, f32[8,512]{1,0:T(8,128)} %root_inverse.1), custom_call_target="tpu_custom_call" | custom-call | tf_op jit(solution)/shard_map/pack/pallas_call | solution.py:309
  8.8 5.2 %collective-permute-start.3 = (f32[6,8,512]{2,1,0:T(8,128)}, f32[6,8,512]{2,1,0:T(8,128)S(1)}, u32[]{:S(2)}, u32[]{:S(2)}) collective-permute-start(f32[6,8,512]{2,1,0:T(8,128)} %get-tuple-element.15), channel_id=1, source_target_pairs={{0,48},{16,0},{32,16},{48,32},{1,49},{17,1},{33,17},{49,33},{2,50}... | collective-permute-start | bytes 294920 | tf_op jit(solution)/shard_map/ppermute | solution.py:317
  14.0 2.4 %collective-permute-start.2 = (f32[6,8,512]{2,1,0:T(8,128)}, f32[6,8,512]{2,1,0:T(8,128)S(1)}, u32[]{:S(2)}, u32[]{:S(2)}) collective-permute-start(f32[6,8,512]{2,1,0:T(8,128)} %get-tuple-element.14), channel_id=1, source_target_pairs={{0,32},{16,48},{32,0},{48,16},{1,33},{17,49},{33,1},{49,17},{2,34}... | collective-permute-start | bytes 294920 | tf_op jit(solution)/shard_map/ppermute | solution.py:317
  16.4 2.5 %collective-permute-start.1 = (f32[6,8,512]{2,1,0:T(8,128)}, f32[6,8,512]{2,1,0:T(8,128)S(1)}, u32[]{:S(2)}, u32[]{:S(2)}) collective-permute-start(f32[6,8,512]{2,1,0:T(8,128)} %get-tuple-element.15), channel_id=1, source_target_pairs={{0,16},{16,32},{32,48},{48,0},{1,17},{17,33},{33,49},{49,1},{2,18}... | collective-permute-start | bytes 294920 | tf_op jit(solution)/shard_map/ppermute | solution.py:317
  19.0 0.0 collective-permute-done.3
  19.0 2.1 %collective-permute-done.2 = f32[6,8,512]{2,1,0:T(8,128)S(1)} collective-permute-done((f32[6,8,512]{2,1,0:T(8,128)}, f32[6,8,512]{2,1,0:T(8,128)S(1)}, u32[]{:S(2)}, u32[]{:S(2)}) %collective-permute-start.2) | collective-permute-done | bytes 98336 | tf_op jit(solution)/shard_map/ppermute | solution.py:317
  21.1 2.1 %collective-permute-done.1 = f32[6,8,512]{2,1,0:T(8,128)S(1)} collective-permute-done((f32[6,8,512]{2,1,0:T(8,128)}, f32[6,8,512]{2,1,0:T(8,128)S(1)}, u32[]{:S(2)}, u32[]{:S(2)}) %collective-permute-start.1) | collective-permute-done | bytes 98336 | tf_op jit(solution)/shard_map/ppermute | solution.py:317
  23.2 1.7 %pad_maximum_fusion = f32[4,6,8,512]{3,2,1,0:T(8,128)} fusion(f32[1,6,8,512]{3,2,1,0:T(8,128)S(1)} %bitcast.9, f32[1,6,8,512]{3,2,1,0:T(8,128)S(1)} %bitcast.10, f32[1,6,8,512]{3,2,1,0:T(8,128)S(1)} %bitcast.11, f32[1,6,8,512]{3,2,1,0:T(8,128)} %bitcast.8), kind=kLoop, calls=%fused_computation | loop fusion | flops 294912 | bytes 786432 | tf_op jit(solution)/shard_map/stack | solution.py:321
  24.9 0.0 all-gather.3.cloned.1.call-update
  25.6 4.4 %leaves_send.1 = (f32[2,2,2,4,96,128]{5,4,3,2,1,0:T(8,128)S(1)}, f32[2,384,128]{2,1,0:T(8,128)S(1)}) custom-call(s32[1,1]{1,0:T(1,128)S(6)} %copy.12.parent, f32[1,1,256,384]{3,2,1,0:T(8,128)} %rhs.1, f32[1,1,256,256]{3,2,1,0:T(8,128)} %inv.1, f32[1,1,4,512,256]{4,3,2,1,0:T(8,128)} %coupling.3, f32[1,4,8,384]{3,2,1,0:T(8,128)} %sep.3), custom_call_target="tpu_custom_call" | custom-call | tf_op jit(solution)/shard_map/leaves_send/pallas_call | solution.py:135
  30.0 7.6 %collective-permute-start = (f32[2,2,2,4,96,128]{5,4,3,2,1,0:T(8,128)S(1)}, f32[2,2,2,4,96,128]{5,4,3,2,1,0:T(8,128)S(1)}, u32[]{:S(2)}, u32[]{:S(2)}) collective-permute-start(f32[2,2,2,4,96,128]{5,4,3,2,1,0:T(8,128)S(1)} %get-tuple-element.13), channel_id=1, source_target_pairs={{0,1},{1,0},{2,3},{3,2},{4,5},{5,4},{6,7},{7,6},{8,9},{9,8},{10,11... | collective-permute-start | bytes 4718600 | tf_op jit(solution)/shard_map/ppermute | solution.py:323
  37.6 3.7 %leaves_keep.1 = f32[2,2,2,4,96,128]{5,4,3,2,1,0:T(8,128)S(1)} custom-call(s32[1,1]{1,0:T(1,128)S(6)} %copy.12.parent, f32[2,384,128]{2,1,0:T(8,128)S(1)} %get-tuple-element.12.xt, f32[1,1,4,512,256]{4,3,2,1,0:T(8,128)} %coupling.3, f32[1,4,8,384]{3,2,1,0:T(8,128)} %sep.3), custom_call_target="tpu_custom_call" | custom-call | tf_op jit(solution)/shard_map/leaves_keep/pallas_call | solution.py:143
  41.2 0.0 collective-permute-done
  41.3 0.2 add.3
  41.5 23.4 %all_to_all.20.parts = f32[4,768,128]{2,1,0:T(8,128)S(1)} all-to-all(f32[4,768,128]{2,1,0:T(8,128)S(1)} %bitcast.7), channel_id=1, replica_groups=mesh['layer'=8,'xl'=2,'xh'=2,'y'=8,'c'=2] {'xl','xh'}, dimensions={0} | all-to-all | bytes 3145728 | tf_op jit(solution)/shard_map/all_to_all | solution.py:324
  64.8 0.3 sum_x.1
  65.1 21.4 %all_to_all.21.parts = f32[8,96,128]{2,1,0:T(8,128)S(1)} all-to-all(f32[8,96,128]{2,1,0:T(8,128)S(1)} %sum_x.1), channel_id=1, replica_groups=mesh['layer'=8,'xl'=2,'xh'=2,'y'=8,'c'=2] {'y'}, dimensions={0} | all-to-all | bytes 786432 | tf_op jit(solution)/shard_map/all_to_all | solution.py:333
  86.6 0.0 all-gather.3.cloned.1.call-done
  86.6 3.7 %chain_first.1 = (f32[2,12,512]{2,1,0:T(8,128)S(1)}, f32[2,12,512]{2,1,0:T(8,128)S(1)}, bf16[4,512,512]{2,1,0:T(8,128)(2,1)S(1)}, bf16[4,512,512]{2,1,0:T(8,128)(2,1)S(1)}) custom-call(f32[8,96,128]{2,1,0:T(8,128)S(1)} %all_to_all.21.parts, f32[16,4,6,8,512]{4,3,2,1,0:T(8,128)} %bitcast.6), custom_call_target="tpu_custom_call" | custom-call | tf_op jit(solution)/shard_map/chain_first/pallas_call | solution.py:335
  90.3 2.8 %collective-permute-start.4 = (f32[2,12,512]{2,1,0:T(8,128)S(1)}, f32[2,12,512]{2,1,0:T(8,128)S(1)}, u32[]{:S(2)}, u32[]{:S(2)}) collective-permute-start(f32[2,12,512]{2,1,0:T(8,128)S(1)} %get-tuple-element.17), channel_id=1, source_target_pairs={{0,16},{1,17},{2,18},{3,19},{4,20},{5,21},{6,22},{7,23},{8,24},{9,... | collective-permute-start | bytes 147464 | tf_op jit(solution)/shard_map/ppermute | solution.py:344
  93.1 1.3 collective-permute-done.4.came
  94.4 0.2 chain_second.1
  94.6 21.9 %all_to_all.22.got = f32[64,3,128]{2,1,0:T(4,128)} all-to-all(f32[64,3,128]{2,1,0:T(4,128)S(1)} %chain_second.1), channel_id=1, replica_groups=mesh['layer'=8,'xl'=2,'xh'=2,'y'=8,'c'=2] {'xl','xh','y','c'}, dimensions={0} | all-to-all | bytes 196608 | tf_op jit(solution)/shard_map/all_to_all | solution.py:355
  116.5 2.0 %unpack.1 = (f32[1,4,8,384]{3,2,1,0:T(8,128)}, f32[8,8,384]{2,1,0:T(8,128)}) custom-call(f32[64,3,128]{2,1,0:T(4,128)} %all_to_all.22.got), custom_call_target="tpu_custom_call" | custom-call | tf_op jit(solution)/shard_map/unpack/pallas_call | solution.py:356
  118.5 14.4 %all_to_all.23 = f32[8,8,384]{2,1,0:T(8,128)S(1)} all-to-all(f32[8,8,384]{2,1,0:T(8,128)} %get-tuple-element.21), channel_id=1, replica_groups=mesh['layer'=8,'xl'=2,'xh'=2,'y'=8,'c'=2] {'layer'}, dimensions={0} | all-to-all | bytes 196608 | tf_op jit(solution)/shard_map/all_to_all | solution.py:364
  132.9 0.6 reduce_sum.9
Async XLA Ops:
  7.2 79.4 %all-gather.3.cloned.1.call-start = ((), (), s32[]{:S(2)}) async-start(), calls=%async_computation.4 | async-start | bytes 6684672 | tf_op jit(solution)/shard_map/all_gather | solution.py:321
  8.8 10.2 %collective-permute-start.3 = (f32[6,8,512]{2,1,0:T(8,128)}, f32[6,8,512]{2,1,0:T(8,128)S(1)}, u32[]{:S(2)}, u32[]{:S(2)}) collective-permute-start(f32[6,8,512]{2,1,0:T(8,128)} %get-tuple-element.15), channel_id=1, source_target_pairs={{0,48},{16,0},{32,16},{48,32},{1,49},{17,1},{33,17},{49,33},{2,50}... | collective-permute-start | bytes 294920 | tf_op jit(solution)/shard_map/ppermute | solution.py:317
  14.0 7.1 %collective-permute-start.2 = (f32[6,8,512]{2,1,0:T(8,128)}, f32[6,8,512]{2,1,0:T(8,128)S(1)}, u32[]{:S(2)}, u32[]{:S(2)}) collective-permute-start(f32[6,8,512]{2,1,0:T(8,128)} %get-tuple-element.14), channel_id=1, source_target_pairs={{0,32},{16,48},{32,0},{48,16},{1,33},{17,49},{33,1},{49,17},{2,34}... | collective-permute-start | bytes 294920 | tf_op jit(solution)/shard_map/ppermute | solution.py:317
  16.4 6.8 %collective-permute-start.1 = (f32[6,8,512]{2,1,0:T(8,128)}, f32[6,8,512]{2,1,0:T(8,128)S(1)}, u32[]{:S(2)}, u32[]{:S(2)}) collective-permute-start(f32[6,8,512]{2,1,0:T(8,128)} %get-tuple-element.15), channel_id=1, source_target_pairs={{0,16},{16,32},{32,48},{48,0},{1,17},{17,33},{33,49},{49,1},{2,18}... | collective-permute-start | bytes 294920 | tf_op jit(solution)/shard_map/ppermute | solution.py:317
  30.0 11.3 %collective-permute-start = (f32[2,2,2,4,96,128]{5,4,3,2,1,0:T(8,128)S(1)}, f32[2,2,2,4,96,128]{5,4,3,2,1,0:T(8,128)S(1)}, u32[]{:S(2)}, u32[]{:S(2)}) collective-permute-start(f32[2,2,2,4,96,128]{5,4,3,2,1,0:T(8,128)S(1)} %get-tuple-element.13), channel_id=1, source_target_pairs={{0,1},{1,0},{2,3},{3,2},{4,5},{5,4},{6,7},{7,6},{8,9},{9,8},{10,11... | collective-permute-start | bytes 4718600 | tf_op jit(solution)/shard_map/ppermute | solution.py:323
  90.3 4.1 %collective-permute-start.4 = (f32[2,12,512]{2,1,0:T(8,128)S(1)}, f32[2,12,512]{2,1,0:T(8,128)S(1)}, u32[]{:S(2)}, u32[]{:S(2)}) collective-permute-start(f32[2,12,512]{2,1,0:T(8,128)S(1)} %get-tuple-element.17), channel_id=1, source_target_pairs={{0,16},{1,17},{2,18},{3,19},{4,20},{5,21},{6,22},{7,23},{8,24},{9,... | collective-permute-start | bytes 147464 | tf_op jit(solution)/shard_map/ppermute | solution.py:344
Sparse Core Ops, SparseCore 0:
  25.0 61.3 all-gather.2

commit v6 on v5

--- a/solution.py
+++ b/solution.py
@@ -28,14 +28,14 @@
     return mm(a[0], b[0]) + (mm(a[0], b[1]) + mm(a[1], b[0]))
 
 
-def by_tiles(ref, part, base):
+def by_tiles(ref, part):
     tiles, rows, _ = ref.shape
 
     def column(tile):
         return jnp.concatenate(
             [
-                ref[tile, pl.ds(base + block + t, 8, stride=part), :]
-                for block in range(0, rows // NC, 8 * part)
+                ref[tile, pl.ds(block + t, 8, stride=part), :]
+                for block in range(0, rows, 8 * part)
                 for t in range(part)
             ],
             axis=0,
@@ -49,7 +49,7 @@
     return x, (x * NY + lax.axis_index("y")) * NC + lax.axis_index("c")
 
 
-def pack_kernel(sep_inverse, sep_coupling, root_coupling, root_rhs, root_inverse, same, other):
+def pack_kernel(sep_inverse, sep_coupling, root_coupling, root_rhs, root_inverse, out):
     zeros = jnp.zeros_like(root_inverse)
     rr = jnp.concatenate([root_rhs[...], zeros[:, root_rhs.shape[1] :]], axis=1)
     tables = (
@@ -63,31 +63,28 @@
             root_inverse[...],
         ],
     )
-    for side in range(2):
-
-        @pl.when(lax.axis_index("xh") == side)
-        def _():
-            for m in range(same.shape[0]):
-                same[m] = tables[side][m]
-                other[m] = tables[1 - side][m]
-
-
-def half_update(part, other, parent, xt, coupling, sep, out, xt_hi, xt_lo, tall, own):
+    for x in range(out.shape[0]):
+        for m in range(out.shape[1]):
+            out[x, m] = tables[x % 2][m]
+
+
+def half_update(part, other, parent, xt, own, coupling, out, xt_hi, xt_lo):
     k = pl.program_id(0)
     core = lax.axis_index("c")
-    base = (1 - core if other else core) * (xt.shape[1] // NC)
+    count = xt.shape[0] // NC
+    half = pl.ds(pl.multiple_of((1 - core if other else core) * count, 64), count)
 
     @pl.when(k == 0)
     def _():
-        xt_hi[...], xt_lo[...] = split(by_tiles(xt, part, base))
-        tall[...] = jnp.zeros_like(tall)
+        xt_hi[...], xt_lo[...] = split(xt[half, :])
 
     keep = jnp.where(k >= parent[0, 0], 1.0, 0.0)
     got = dot3((xt_hi[...], xt_lo[...]), split(coupling[0, 0, 0]), NT) * -keep
     block = place()[1]
-    tall[pl.ds(pl.multiple_of(8 * (block % 16), 8), 8), :] = sep[0, 0]
-    own[0] = tall[...].T
-    mine = by_tiles(own, part, base)
+    first = 8 * (block % 16)
+    mine = pltpu.roll(own[half, :], (first - 8 * k + 128) % 128, 1)
+    lane = lax.broadcasted_iota(jnp.int32, mine.shape, 1)
+    mine = jnp.where((lane >= first) & (lane < first + 8), mine, 0.0)
     group = 8 * part
     for side in range(2):
         rows = slice(side * group, (side + 1) * group)
@@ -96,18 +93,24 @@
         out[side, 0, 0, block // 16] += mine[rows]
 
 
-def send_kernel(part, parent, rhs, inv, coupling, sep, out, xt, *scratch):
+def send_kernel(part, parent, rhs, inv, sep, coupling, out, xt, own, plain, tall, flat, *scratch):
     @pl.when(pl.program_id(0) == 0)
     def _():
         solved = dot3(split(inv[0, 0]), split(rhs[0, 0]), NN).T
-        for tile in range(xt.shape[0]):
-            xt[tile] = solved[:, 128 * tile : 128 * (tile + 1)]
-
-    half_update(part, True, parent, xt, coupling, sep, out, *scratch)
-
-
-def keep_kernel(part, parent, xt, coupling, sep, out, *scratch):
-    half_update(part, False, parent, xt, coupling, sep, out, *scratch)
+        for tile in range(plain.shape[0]):
+            plain[tile] = solved[:, 128 * tile : 128 * (tile + 1)]
+        xt[...] = by_tiles(plain, part)
+        tall[...] = jnp.zeros_like(tall)
+        for k in range(sep.shape[1]):
+            tall[8 * k : 8 * k + 8, :] = sep[0, k]
+        flat[0] = tall[...].T
+        own[...] = by_tiles(flat, part)
+
+    half_update(part, True, parent, xt, own, coupling, out, *scratch)
+
+
+def keep_kernel(part, parent, xt, own, coupling, out, *scratch):
+    half_update(part, False, parent, xt, own, coupling, out, *scratch)
 
 
 def leaves(parent, rhs, inv, coupling, sep):
@@ -115,39 +118,37 @@
     leaf, cols = rhs.shape[2], rhs.shape[3]
     part, tiles = cols // 32, width // 128
     one = lambda *shape: pl.BlockSpec(shape, lambda k: (0,) * len(shape))
-    per_level = [
-        pl.BlockSpec((1, 1, 1, width, leaf), lambda k: (0, 0, k, 0, 0)),
-        pl.BlockSpec((1, 1, 8, cols), lambda k: (0, k, 0, 0)),
-    ]
+    coupling_spec = pl.BlockSpec((1, 1, 1, width, leaf), lambda k: (0, 0, k, 0, 0))
     half_spec = pl.BlockSpec((2, 1, 1, tiles, 8 * part, 128), lambda k: (0, k // 2, k % 2, 0, 0, 0))
     half_shape = FLAT((2, 2, 2, tiles, 8 * part, 128), jnp.float32)
-    xt_spec = one(leaf // 128, cols, 128)
-    common = dict(
+    shared = [one(cols, leaf), one(cols, 128)]
+    parts = [pltpu.VMEM((cols // NC, leaf), jnp.bfloat16)] * 2
+    params = pltpu.CompilerParams(vmem_limit_bytes=24 * 2**20)
+    send, xt, own = pl.pallas_call(
+        functools.partial(send_kernel, part),
         grid=(n,),
+        in_specs=[SMEM, one(1, 1, leaf, cols), one(1, 1, leaf, leaf), one(1, n, 8, cols), coupling_spec],
+        out_specs=[half_spec] + shared,
+        out_shape=[half_shape, FLAT((cols, leaf), jnp.float32), FLAT((cols, 128), jnp.float32)],
         scratch_shapes=[
-            pltpu.VMEM((cols // NC, leaf), jnp.bfloat16),
-            pltpu.VMEM((cols // NC, leaf), jnp.bfloat16),
+            pltpu.VMEM((leaf // 128, cols, 128), jnp.float32),
             pltpu.VMEM((128, cols), jnp.float32),
             pltpu.VMEM((1, cols, 128), jnp.float32),
-        ],
-        compiler_params=pltpu.CompilerParams(vmem_limit_bytes=24 * 2**20),
-    )
-    send, xt = pl.pallas_call(
-        functools.partial(send_kernel, part),
-        in_specs=[SMEM, one(1, 1, leaf, cols), one(1, 1, leaf, leaf)] + per_level,
-        out_specs=[half_spec, xt_spec],
-        out_shape=[half_shape, FLAT((leaf // 128, cols, 128), jnp.float32)],
+        ]
+        + parts,
+        compiler_params=params,
         name="leaves_send",
-        **common,
-    )(parent, rhs, inv, coupling, sep)
+    )(parent, rhs, inv, sep, coupling)
     keep = pl.pallas_call(
         functools.partial(keep_kernel, part),
-        in_specs=[SMEM, xt_spec] + per_level,
+        grid=(n,),
+        in_specs=[SMEM] + shared + [coupling_spec],
         out_specs=half_spec,
         out_shape=half_shape,
+        scratch_shapes=parts,
+        compiler_params=params,
         name="leaves_keep",
-        **common,
-    )(parent, xt, coupling, sep)
+    )(parent, xt, own, coupling)
     return send, keep
 
 
@@ -159,17 +160,14 @@
 
 
 def first_kernel(part, parts, weights, held, send, high, low, full, sems):
-    x, _ = place()
-    odd = x % 2 == 1
+    odd = lax.axis_index("xh") == 1
 
     def copies(m):
         return [
             pltpu.make_async_copy(
-                weights.at[:, back, m],
-                full.at[m, pl.ds(pl.multiple_of(((x + NX - back) % NX) * 16, 16), 16)],
-                sems.at[m, back],
+                weights.at[:, src, m], full.at[m, pl.ds(16 * src, 16)], sems.at[m, src]
             )
-            for back in range(NX)
+            for src in range(NX)
         ]
 
     def matrix(m):
@@ -289,6 +287,10 @@
     return pltpu.with_memory_space_constraint(array, pltpu.HBM)
 
 
+def in_vmem(array):
+    return pltpu.with_memory_space_constraint(array, pltpu.VMEM)
+
+
 def body(
     leaf_rhs,
     leaf_inverse,
@@ -306,19 +308,14 @@
     tiles = width // 128
     call = pl.pallas_call
 
-    same, other = call(
+    pack = call(
         pack_kernel,
         in_specs=[VMEM] * 5,
-        out_specs=[VMEM, VMEM],
-        out_shape=[FLAT((6, 8, width), jnp.float32)] * 2,
+        out_specs=VMEM,
+        out_shape=FLAT((NX, 6, 8, width), jnp.float32),
         name="pack",
     )(sep_inverse, sep_coupling, root_coupling, root_rhs, root_inverse)
-    ring = [same] + [
-        lax.ppermute(pack, X, [(i, (i + j) % NX) for i in range(NX)])
-        for j, pack in ((1, other), (2, same), (3, other))
-    ]
-
-    weights = lax.all_gather(jnp.stack(ring), ("y", "c"))
+    weights = lax.all_gather(lax.all_to_all(pack, X, 0, 0), ("y", "c"))
     send, keep = leaves(parent, *map(in_hbm, (leaf_rhs, leaf_inverse, leaf_coupling, sep_rhs)))
     res = keep + lax.ppermute(send, "c", [(0, 1), (1, 0)])
     res = lax.all_to_all(res.reshape(NX, 2 * tiles * 8 * part, 128), X, 0, 0)
@@ -346,7 +343,7 @@
         functools.partial(second_kernel, part),
         in_specs=[VMEM] * 4,
         out_specs=VMEM,
-        out_shape=FLAT((64, 3, 128), jnp.float32),
+        out_shape=pltpu.VMEM((64, 3, 128), jnp.float32),
         scratch_shapes=[pltpu.VMEM((128, width), jnp.float32)],
         compiler_params=pltpu.CompilerParams(vmem_limit_bytes=16 * 2**20),
         name="chain_second",
@@ -357,10 +354,10 @@
         functools.partial(unpack_kernel, part),
         in_specs=[VMEM],
         out_specs=[VMEM] * 2,
-        out_shape=[FLAT((1, 4, 8, cols), jnp.float32), FLAT((8, 8, cols), jnp.float32)],
+        out_shape=[FLAT((1, 4, 8, cols), jnp.float32), pltpu.VMEM((8, 8, cols), jnp.float32)],
         scratch_shapes=[pltpu.VMEM((64 * 8, 128), jnp.float32)],
         name="unpack",
-    )(out)
+    )(in_vmem(out))
     root_out = lax.all_to_all(term, "layer", 0, 0).sum(0)
     return (sep_out, root_out)
 

time: 141 us -> 135 us (0.957)
  blocking collectives: 81.1 us -> 90.4 us
  starting transfers between devices: 20.6 us -> 11.8 us
  waiting for transfers between devices: 5.58 us -> 1.33 us
  other arithmetic: 2.48 us -> 0.81 us
    all_to_all x0 -> x1, blocking collectives: none -> 11.2 us  [body(): weights = lax.all_gather(lax.all_to_all(pack, X, 0, 0), ('y', 'c'))]
    ppermute x3 -> x0, starting transfers between devices: 10.1 us -> none  [body(): lax.ppermute(pack, X, [(i, (i + j) % NX) for i in range(NX)])]
    ppermute x3 -> x0, waiting for transfers between devices: 4.25 us -> none  [body(): lax.ppermute(pack, X, [(i, (i + j) % NX) for i in range(NX)])]
    another operation x1 -> x0, other arithmetic: 1.67 us -> none  [body(): weights = lax.all_gather(jnp.stack(ring), ('y', 'c'))]
    ppermute x1, starting transfers between devices: 7.58 us -> 9.18 us  [body(): res = keep + lax.ppermute(send, 'c', [(0, 1), (1, 0)])]
  transfers between devices with their start and end apart: 6 -> 3, of which waited for: 3 -> 1; matrix products, arithmetic and copies ran while one was open for 0% -> 0% of each run, Pallas kernels for 6% -> 6%
where the time goes in v6:
time: 135 us; the launch traced here: 134 us
  blocking collectives  90.4 us (67%)
  Pallas kernels  14.9 us (11%)
  between operations  14.7 us (11%)
  starting transfers between devices  11.8 us (9%)
    all_to_all x1, blocking collectives, body(): res = lax.all_to_all(res.reshape(NX, 2 * tiles * 8 * part, 128), X, 0, 0)  23.1 us
    all_to_all x1, blocking collectives, body(): out = lax.all_to_all(out, ROW, 0, 0)  21.4 us
    all_to_all x1, blocking collectives, body(): res = lax.all_to_all(res, 'y', 0, 0)  20.9 us
    all_to_all x1, blocking collectives, body(): root_out = lax.all_to_all(term, 'layer', 0, 0).sum(0)  13.9 us
    all_to_all x1, blocking collectives, body(): weights = lax.all_gather(lax.all_to_all(pack, X, 0, 0), ('y', 'c'))  11.2 us
    ppermute x1, starting transfers between devices, body(): res = keep + lax.ppermute(send, 'c', [(0, 1), (1, 0)])  9.18 us
    pallas_call x1, Pallas kernels, leaves(): pl.pallas_call(functools.partial(send_kernel, part), grid=(n,), in_specs=...  4.42 us
    pallas_call x1, Pallas kernels, leaves(): pl.pallas_call(functools.partial(keep_kernel, part), grid=(n,), in_specs=...  3.66 us
  transfers between devices with their start and end apart: 3, of which 1 were waited for; matrix products, arithmetic and copies ran while one was open for 0% of the time, Pallas kernels for 6%

profile of v6, /device:TPU:1, one launch (start us, length us, event | category | flops | bytes accessed | tf_op | source)
XLA Modules:
  0.0 134.0 jit_solution(6882603602339222404)
XLA Ops:
  7.2 0.0 all-gather.3.cloned.1.call-start
  7.2 1.7 %pack.1 = f32[4,6,8,512]{3,2,1,0:T(8,128)} custom-call(f32[1,4,8,512]{3,2,1,0:T(8,128)} %sep_inverse.1, f32[1,3,8,512]{3,2,1,0:T(8,128)} %sep_coupling.1, f32[1,8,512]{2,1,0:T(8,128)} %root_coupling.1, f32[8,384]{1,0:T(8,128)} %root_rhs.1, f32[8,512]{1,0:T(8,128)} %root_inverse.1), custom_call_target="tpu_custom_call" | custom-call | tf_op jit(solution)/shard_map/pack/pallas_call | solution.py:311
  8.9 11.2 %all_to_all.25 = f32[4,6,8,512]{3,2,1,0:T(8,128)} all-to-all(f32[4,6,8,512]{3,2,1,0:T(8,128)} %pack.1), channel_id=1, replica_groups=mesh['layer'=8,'xl'=2,'xh'=2,'y'=8,'c'=2] {'xl','xh'}, dimensions={0} | all-to-all | bytes 786432 | tf_op jit(solution)/shard_map/all_to_all | solution.py:318
  20.0 0.0 all-gather.3.cloned.1.call-update
  20.7 4.4 %leaves_send.1 = (f32[2,2,2,4,96,128]{5,4,3,2,1,0:T(8,128)S(1)}, f32[384,256]{1,0:T(8,128)S(1)}, f32[384,128]{1,0:T(8,128)S(1)}) custom-call(s32[1,1]{1,0:T(1,128)S(6)} %copy.12.parent, f32[1,1,256,384]{3,2,1,0:T(8,128)} %rhs.1, f32[1,1,256,256]{3,2,1,0:T(8,128)} %inv.1, f32[1,4,8,384]{3,2,1,0:T(8,128)} %sep.1, f32[1,1,4,512,256]{4,3,2,1,0:T(8,128)} %coupling.3), custom_call_target="tpu_custom_call" | custom-call | tf_op jit(solution)/shard_map/leaves_send/pallas_call | solution.py:127
  25.1 9.2 %collective-permute-start = (f32[2,2,2,4,96,128]{5,4,3,2,1,0:T(8,128)S(1)}, f32[2,2,2,4,96,128]{5,4,3,2,1,0:T(8,128)S(1)}, u32[]{:S(2)}, u32[]{:S(2)}) collective-permute-start(f32[2,2,2,4,96,128]{5,4,3,2,1,0:T(8,128)S(1)} %get-tuple-element.13), channel_id=1, source_target_pairs={{0,1},{1,0},{2,3},{3,2},{4,5},{5,4},{6,7},{7,6},{8,9},{9,8},{10,11... | collective-permute-start | bytes 4718600 | tf_op jit(solution)/shard_map/ppermute | solution.py:320
  34.3 3.7 %leaves_keep.1 = f32[2,2,2,4,96,128]{5,4,3,2,1,0:T(8,128)S(1)} custom-call(s32[1,1]{1,0:T(1,128)S(6)} %copy.12.parent, f32[384,256]{1,0:T(8,128)S(1)} %get-tuple-element.11.xt, f32[384,128]{1,0:T(8,128)S(1)} %get-tuple-element.12.own, f32[1,1,4,512,256]{4,3,2,1,0:T(8,128)} %coupling.3), custom_call_target="tpu_custom_call" | custom-call | tf_op jit(solution)/shard_map/leaves_keep/pallas_call | solution.py:142
  38.0 0.0 collective-permute-done
  38.0 0.2 add.3
  38.2 23.1 %all_to_all.26.parts = f32[4,768,128]{2,1,0:T(8,128)S(1)} all-to-all(f32[4,768,128]{2,1,0:T(8,128)S(1)} %bitcast.3), channel_id=1, replica_groups=mesh['layer'=8,'xl'=2,'xh'=2,'y'=8,'c'=2] {'xl','xh'}, dimensions={0} | all-to-all | bytes 3145728 | tf_op jit(solution)/shard_map/all_to_all | solution.py:321
  61.3 0.3 sum_x.1
  61.6 20.9 %all_to_all.27.parts = f32[8,96,128]{2,1,0:T(8,128)S(1)} all-to-all(f32[8,96,128]{2,1,0:T(8,128)S(1)} %sum_x.1), channel_id=1, replica_groups=mesh['layer'=8,'xl'=2,'xh'=2,'y'=8,'c'=2] {'y'}, dimensions={0} | all-to-all | bytes 786432 | tf_op jit(solution)/shard_map/all_to_all | solution.py:330
  82.5 0.0 all-gather.3.cloned.1.call-done
  82.5 3.7 %chain_first.1 = (f32[2,12,512]{2,1,0:T(8,128)S(1)}, f32[2,12,512]{2,1,0:T(8,128)S(1)}, bf16[4,512,512]{2,1,0:T(8,128)(2,1)S(1)}, bf16[4,512,512]{2,1,0:T(8,128)(2,1)S(1)}) custom-call(f32[8,96,128]{2,1,0:T(8,128)S(1)} %all_to_all.27.parts, f32[16,4,6,8,512]{4,3,2,1,0:T(8,128)} %bitcast.2), custom_call_target="tpu_custom_call" | custom-call | tf_op jit(solution)/shard_map/chain_first/pallas_call | solution.py:332
  86.2 2.5 %collective-permute-start.1 = (f32[2,12,512]{2,1,0:T(8,128)S(1)}, f32[2,12,512]{2,1,0:T(8,128)S(1)}, u32[]{:S(2)}, u32[]{:S(2)}) collective-permute-start(f32[2,12,512]{2,1,0:T(8,128)S(1)} %get-tuple-element.15), channel_id=1, source_target_pairs={{0,16},{1,17},{2,18},{3,19},{4,20},{5,21},{6,22},{7,23},{8,24},{9,... | collective-permute-start | bytes 147464 | tf_op jit(solution)/shard_map/ppermute | solution.py:341
  88.7 1.3 collective-permute-done.1.came
  90.1 0.2 chain_second.1
  90.2 21.4 %all_to_all.28.got = f32[64,3,128]{2,1,0:T(4,128)S(1)} all-to-all(f32[64,3,128]{2,1,0:T(4,128)S(1)} %chain_second.1), channel_id=1, replica_groups=mesh['layer'=8,'xl'=2,'xh'=2,'y'=8,'c'=2] {'xl','xh','y','c'}, dimensions={0} | all-to-all | bytes 196608 | tf_op jit(solution)/shard_map/all_to_all | solution.py:352
  111.6 1.0 unpack.1
  112.6 13.9 %all_to_all.29 = f32[8,8,384]{2,1,0:T(8,128)S(1)} all-to-all(f32[8,8,384]{2,1,0:T(8,128)S(1)} %get-tuple-element.19), channel_id=1, replica_groups=mesh['layer'=8,'xl'=2,'xh'=2,'y'=8,'c'=2] {'layer'}, dimensions={0} | all-to-all | bytes 196608 | tf_op jit(solution)/shard_map/all_to_all | solution.py:361
  126.5 0.6 reduce_sum.9
Async XLA Ops:
  7.2 75.4 %all-gather.3.cloned.1.call-start = ((), (), s32[]{:S(2)}) async-start(), calls=%async_computation.5 | async-start | bytes 6684672 | tf_op jit(solution)/shard_map/all_gather | solution.py:318
  25.1 12.9 %collective-permute-start = (f32[2,2,2,4,96,128]{5,4,3,2,1,0:T(8,128)S(1)}, f32[2,2,2,4,96,128]{5,4,3,2,1,0:T(8,128)S(1)}, u32[]{:S(2)}, u32[]{:S(2)}) collective-permute-start(f32[2,2,2,4,96,128]{5,4,3,2,1,0:T(8,128)S(1)} %get-tuple-element.13), channel_id=1, source_target_pairs={{0,1},{1,0},{2,3},{3,2},{4,5},{5,4},{6,7},{7,6},{8,9},{9,8},{10,11... | collective-permute-start | bytes 4718600 | tf_op jit(solution)/shard_map/ppermute | solution.py:320
  86.2 3.9 %collective-permute-start.1 = (f32[2,12,512]{2,1,0:T(8,128)S(1)}, f32[2,12,512]{2,1,0:T(8,128)S(1)}, u32[]{:S(2)}, u32[]{:S(2)}) collective-permute-start(f32[2,12,512]{2,1,0:T(8,128)S(1)} %get-tuple-element.15), channel_id=1, source_target_pairs={{0,16},{1,17},{2,18},{3,19},{4,20},{5,21},{6,22},{7,23},{8,24},{9,... | collective-permute-start | bytes 147464 | tf_op jit(solution)/shard_map/ppermute | solution.py:341
Sparse Core Ops, SparseCore 0:
  20.2 61.1 all-gather.2

commit v7 on v6

--- a/solution.py
+++ b/solution.py
@@ -23,9 +23,15 @@
     return high, (a - high.astype(jnp.float32)).astype(jnp.bfloat16)
 
 
+def stack(a):
+    return jnp.concatenate(split(a), axis=0)
+
+
 def dot3(a, b, dims):
     mm = functools.partial(lax.dot_general, dimension_numbers=dims, preferred_element_type=jnp.float32)
-    return mm(a[0], b[0]) + (mm(a[0], b[1]) + mm(a[1], b[0]))
+    rows = a.shape[0] // 2
+    both = mm(a, b[0])
+    return both[:rows] + (both[rows:] + mm(a[:rows], b[1]))
 
 
 def by_tiles(ref, part):
@@ -68,7 +74,7 @@
             out[x, m] = tables[x % 2][m]
 
 
-def half_update(part, other, parent, xt, own, coupling, out, xt_hi, xt_lo):
+def half_update(part, other, parent, xt, own, coupling, out, pair):
     k = pl.program_id(0)
     core = lax.axis_index("c")
     count = xt.shape[0] // NC
@@ -76,10 +82,10 @@
 
     @pl.when(k == 0)
     def _():
-        xt_hi[...], xt_lo[...] = split(xt[half, :])
+        pair[...] = stack(xt[half, :])
 
     keep = jnp.where(k >= parent[0, 0], 1.0, 0.0)
-    got = dot3((xt_hi[...], xt_lo[...]), split(coupling[0, 0, 0]), NT) * -keep
+    got = dot3(pair[...], split(coupling[0, 0, 0]), NT) * -keep
     block = place()[1]
     first = 8 * (block % 16)
     mine = pltpu.roll(own[half, :], (first - 8 * k + 128) % 128, 1)
@@ -96,7 +102,7 @@
 def send_kernel(part, parent, rhs, inv, sep, coupling, out, xt, own, plain, tall, flat, *scratch):
     @pl.when(pl.program_id(0) == 0)
     def _():
-        solved = dot3(split(inv[0, 0]), split(rhs[0, 0]), NN).T
+        solved = dot3(stack(inv[0, 0]), split(rhs[0, 0]), NN).T
         for tile in range(plain.shape[0]):
             plain[tile] = solved[:, 128 * tile : 128 * (tile + 1)]
         xt[...] = by_tiles(plain, part)
@@ -113,18 +119,23 @@
     half_update(part, False, parent, xt, own, coupling, out, *scratch)
 
 
-def leaves(parent, rhs, inv, coupling, sep):
-    n, width = coupling.shape[2], coupling.shape[3]
-    leaf, cols = rhs.shape[2], rhs.shape[3]
+def leaf_specs(coupling, cols):
+    n, width, leaf = coupling.shape[2:]
     part, tiles = cols // 32, width // 128
     one = lambda *shape: pl.BlockSpec(shape, lambda k: (0,) * len(shape))
     coupling_spec = pl.BlockSpec((1, 1, 1, width, leaf), lambda k: (0, 0, k, 0, 0))
     half_spec = pl.BlockSpec((2, 1, 1, tiles, 8 * part, 128), lambda k: (0, k // 2, k % 2, 0, 0, 0))
     half_shape = FLAT((2, 2, 2, tiles, 8 * part, 128), jnp.float32)
     shared = [one(cols, leaf), one(cols, 128)]
-    parts = [pltpu.VMEM((cols // NC, leaf), jnp.bfloat16)] * 2
+    pair = pltpu.VMEM((2 * (cols // NC), leaf), jnp.bfloat16)
     params = pltpu.CompilerParams(vmem_limit_bytes=24 * 2**20)
-    send, xt, own = pl.pallas_call(
+    return part, one, coupling_spec, half_spec, half_shape, shared, pair, params
+
+
+def leaves_send(parent, rhs, inv, coupling, sep):
+    n, leaf, cols = coupling.shape[2], rhs.shape[2], rhs.shape[3]
+    part, one, coupling_spec, half_spec, half_shape, shared, pair, params = leaf_specs(coupling, cols)
+    return pl.pallas_call(
         functools.partial(send_kernel, part),
         grid=(n,),
         in_specs=[SMEM, one(1, 1, leaf, cols), one(1, 1, leaf, leaf), one(1, n, 8, cols), coupling_spec],
@@ -134,22 +145,25 @@
             pltpu.VMEM((leaf // 128, cols, 128), jnp.float32),
             pltpu.VMEM((128, cols), jnp.float32),
             pltpu.VMEM((1, cols, 128), jnp.float32),
-        ]
-        + parts,
+            pair,
+        ],
         compiler_params=params,
         name="leaves_send",
     )(parent, rhs, inv, sep, coupling)
-    keep = pl.pallas_call(
+
+
+def leaves_keep(parent, xt, own, coupling):
+    part, _, coupling_spec, half_spec, half_shape, shared, pair, params = leaf_specs(coupling, xt.shape[0])
+    return pl.pallas_call(
         functools.partial(keep_kernel, part),
-        grid=(n,),
+        grid=(coupling.shape[2],),
         in_specs=[SMEM] + shared + [coupling_spec],
         out_specs=half_spec,
         out_shape=half_shape,
-        scratch_shapes=parts,
+        scratch_shapes=[pair],
         compiler_params=params,
         name="leaves_keep",
     )(parent, xt, own, coupling)
-    return send, keep
 
 
 def sum_kernel(parts, out):
@@ -192,7 +206,8 @@
 
     def residual(k):
         starts = [part * (tiles * k + tile) for tile in range(tiles)]
-        return split(jnp.concatenate([res[at : at + part] for at in starts], axis=1))
+        rows = jnp.concatenate([res[at : at + part] for at in starts], axis=1)
+        return stack(jnp.concatenate([rows, jnp.zeros((16 - part, rows.shape[1]), jnp.float32)], axis=0))
 
     first = dot3(residual(0), matrix(0), NT)
     second = dot3(residual(1), matrix(1), NT)
@@ -202,8 +217,8 @@
 
     @pl.when(jnp.logical_not(odd))
     def _():
-        chained = second - dot3(split(first), last[0], NT)
-        shape = (part, held.shape[2])
+        chained = second - dot3(stack(first), last[0], NT)
+        shape = held.shape[1:]
         group = (lax.axis_index("c") * 2 + lax.axis_index("xl")) * NY + lax.axis_index("y")
         column = lax.broadcasted_iota(jnp.int32, shape, 0) + part * group
         mine = lax.broadcasted_iota(jnp.int32, shape, 1) == column
@@ -227,7 +242,7 @@
 
     def store(at, value):
         for copy in range(3):
-            wide[step * copy + part * at : step * copy + part * (at + 1), :] = value
+            wide[step * copy + part * at : step * copy + part * (at + 1), :] = value[:part]
 
     @pl.when(lax.axis_index("xh") == 0)
     def _():
@@ -236,12 +251,12 @@
 
     @pl.when(lax.axis_index("xh") == 1)
     def _():
-        third = held[0] - dot3(split(came[0]), (high[0], low[0]), NT)
+        third = held[0] - dot3(stack(came[0]), (high[0], low[0]), NT)
         store(0, third)
-        fourth = held[1] - dot3(split(third), (high[1], low[1]), NT)
+        fourth = held[1] - dot3(stack(third), (high[1], low[1]), NT)
         store(1, fourth)
-        term = came[1] - dot3(split(fourth), (high[2], low[2]), NT)
-        store(2, dot3(split(term), (high[3], low[3]), NT))
+        term = came[1] - dot3(stack(fourth), (high[2], low[2]), NT)
+        store(2, dot3(stack(term), (high[3], low[3]), NT))
 
     rows = wide[...].T.reshape(-1, 8, 128)
     lane = lax.broadcasted_iota(jnp.int32, (rows.shape[0], 1, 128), 2)
@@ -315,8 +330,15 @@
         out_shape=FLAT((NX, 6, 8, width), jnp.float32),
         name="pack",
     )(sep_inverse, sep_coupling, root_coupling, root_rhs, root_inverse)
-    weights = lax.all_gather(lax.all_to_all(pack, X, 0, 0), ("y", "c"))
-    send, keep = leaves(parent, *map(in_hbm, (leaf_rhs, leaf_inverse, leaf_coupling, sep_rhs)))
+    exchanged = lax.all_to_all(pack, X, 0, 0)
+
+    leaf_rhs, leaf_inverse, leaf_coupling, sep_rhs = map(
+        in_hbm, (leaf_rhs, leaf_inverse, leaf_coupling, sep_rhs)
+    )
+    send, xt, own = leaves_send(parent, leaf_rhs, leaf_inverse, leaf_coupling, sep_rhs)
+    exchanged, xt = lax.optimization_barrier((exchanged, xt))
+    weights = lax.all_gather(exchanged, ("y", "c"))
+    keep = leaves_keep(parent, xt, own, leaf_coupling)
     res = keep + lax.ppermute(send, "c", [(0, 1), (1, 0)])
     res = lax.all_to_all(res.reshape(NX, 2 * tiles * 8 * part, 128), X, 0, 0)
     res = call(
@@ -333,7 +355,7 @@
         functools.partial(first_kernel, part),
         in_specs=[VMEM, HBM],
         out_specs=[VMEM] * 4,
-        out_shape=[FLAT((2, part, width), jnp.float32)] * 2 + [FLAT((4, width, width), jnp.bfloat16)] * 2,
+        out_shape=[FLAT((2, 16, width), jnp.float32)] * 2 + [FLAT((4, width, width), jnp.bfloat16)] * 2,
         scratch_shapes=[pltpu.VMEM((6, 64, 8, width), jnp.float32), pltpu.SemaphoreType.DMA((6, NX))],
         compiler_params=pltpu.CompilerParams(vmem_limit_bytes=32 * 2**20),
         name="chain_first",

time: 135 us -> 135 us (level)
  blocking collectives: 90.4 us -> 79.6 us
  waiting for transfers between devices: 1.33 us -> 7.9 us
  starting transfers between devices: 11.8 us -> 16.4 us
    all_to_all x1 -> x0, blocking collectives: 11.2 us -> none  [body(): weights = lax.all_gather(lax.all_to_all(pack, X, 0, 0), ('y', 'c'))]
    all_gather x1, waiting for transfers between devices: 0.01 us -> 5.23 us  [body(): weights = lax.all_gather(exchanged, ('y', 'c'))]
    all_to_all x0 -> x1, starting transfers between devices: none -> 4.84 us  [body(): exchanged = lax.all_to_all(pack, X, 0, 0)]
  transfers between devices with their start and end apart: 3 -> 4, of which waited for: 1 -> 3; matrix products, arithmetic and copies ran while one was open for 0% -> 0% of each run, Pallas kernels for 6% -> 6%
where the time goes in v7:
time: 135 us; the launch traced here: 134 us
  blocking collectives  79.6 us (59%)
  starting transfers between devices  16.4 us (12%)
  between operations  14.7 us (11%)
  Pallas kernels  14.1 us (10%)
  waiting for transfers between devices  7.9 us (6%)
    all_to_all x1, blocking collectives, body(): res = lax.all_to_all(res.reshape(NX, 2 * tiles * 8 * part, 128), X, 0, 0)  23.1 us
    all_to_all x1, blocking collectives, body(): res = lax.all_to_all(res, 'y', 0, 0)  21.4 us
    all_to_all x1, blocking collectives, body(): out = lax.all_to_all(out, ROW, 0, 0)  20.7 us
    all_to_all x1, blocking collectives, body(): root_out = lax.all_to_all(term, 'layer', 0, 0).sum(0)  14.3 us
    ppermute x1, starting transfers between devices, body(): res = keep + lax.ppermute(send, 'c', [(0, 1), (1, 0)])  8.52 us
    all_gather x1, waiting for transfers between devices, body(): weights = lax.all_gather(exchanged, ('y', 'c'))  5.23 us
    all_to_all x1, starting transfers between devices, body(): exchanged = lax.all_to_all(pack, X, 0, 0)  4.84 us
    pallas_call x1, Pallas kernels, leaves_send(): pl.pallas_call(functools.partial(send_kernel, part), grid=(n,), in_specs=...  4.24 us
  transfers between devices with their start and end apart: 4, of which 3 were waited for; matrix products, arithmetic and copies ran while one was open for 0% of the time, Pallas kernels for 6%

profile of v7, /device:TPU:1, one launch (start us, length us, event | category | flops | bytes accessed | tf_op | source)
XLA Modules:
  0.0 134.3 jit_solution(6243927055151230006)
XLA Ops:
  7.2 1.7 %pack.1 = f32[4,6,8,512]{3,2,1,0:T(8,128)} custom-call(f32[1,4,8,512]{3,2,1,0:T(8,128)} %sep_inverse.1, f32[1,3,8,512]{3,2,1,0:T(8,128)} %sep_coupling.1, f32[1,8,512]{2,1,0:T(8,128)} %root_coupling.1, f32[8,384]{1,0:T(8,128)} %root_rhs.1, f32[8,512]{1,0:T(8,128)} %root_inverse.1), custom_call_target="tpu_custom_call" | custom-call | tf_op jit(solution)/shard_map/pack/pallas_call | solution.py:326
  8.8 4.8 %all-to-all-start = ((f32[4,6,8,512]{3,2,1,0:T(8,128)}), f32[4,6,8,512]{3,2,1,0:T(8,128)S(1)}, u32[]{:S(2)}, u32[]{:S(2)}) async-start(f32[4,6,8,512]{3,2,1,0:T(8,128)} %pack.1), calls=%async_computation | async-start | bytes 786432 | tf_op jit(solution)/shard_map/all_to_all | solution.py:333
  13.7 0.0 all-gather.3.cloned.1.call-start
  14.3 4.2 %leaves_send.1 = (f32[2,2,2,4,96,128]{5,4,3,2,1,0:T(8,128)S(1)}, f32[384,256]{1,0:T(8,128)S(1)}, f32[384,128]{1,0:T(8,128)S(1)}) custom-call(s32[1,1]{1,0:T(1,128)S(6)} %copy.12.parent, f32[1,1,256,384]{3,2,1,0:T(8,128)} %rhs.1, f32[1,1,256,256]{3,2,1,0:T(8,128)} %inv.1, f32[1,4,8,384]{3,2,1,0:T(8,128)} %sep.1, f32[1,1,4,512,256]{4,3,2,1,0:T(8,128)} %coupling.3), custom_call_target="tpu_custom_call" | custom-call | tf_op jit(solution)/shard_map/leaves_send/pallas_call | solution.py:138
  18.6 1.3 all-to-all-done
  19.9 0.0 copy-start
  19.9 0.7 copy-done
  20.6 0.0 all-gather.3.cloned.1.call-update
  20.7 8.5 %collective-permute-start = (f32[2,2,2,4,96,128]{5,4,3,2,1,0:T(8,128)S(1)}, f32[2,2,2,4,96,128]{5,4,3,2,1,0:T(8,128)S(1)}, u32[]{:S(2)}, u32[]{:S(2)}) collective-permute-start(f32[2,2,2,4,96,128]{5,4,3,2,1,0:T(8,128)S(1)} %get-tuple-element.16), channel_id=1, source_target_pairs={{0,1},{1,0},{2,3},{3,2},{4,5},{5,4},{6,7},{7,6},{8,9},{9,8},{10,11... | collective-permute-start | bytes 4718600 | tf_op jit(solution)/shard_map/ppermute | solution.py:342
  29.2 3.5 %leaves_keep.1 = f32[2,2,2,4,96,128]{5,4,3,2,1,0:T(8,128)S(1)} custom-call(s32[1,1]{1,0:T(1,128)S(6)} %copy.12.parent, f32[384,256]{1,0:T(8,128)S(1)} %get-tuple-element.14.xt, f32[384,128]{1,0:T(8,128)S(1)} %get-tuple-element.15.own, f32[1,1,4,512,256]{4,3,2,1,0:T(8,128)} %coupling.3), custom_call_target="tpu_custom_call" | custom-call | tf_op jit(solution)/shard_map/leaves_keep/pallas_call | solution.py:157
  32.7 0.0 collective-permute-done
  32.7 0.2 add.3
  32.9 23.1 %all_to_all.25.parts = f32[4,768,128]{2,1,0:T(8,128)S(1)} all-to-all(f32[4,768,128]{2,1,0:T(8,128)S(1)} %bitcast.3), channel_id=1, replica_groups=mesh['layer'=8,'xl'=2,'xh'=2,'y'=8,'c'=2] {'xl','xh'}, dimensions={0} | all-to-all | bytes 3145728 | tf_op jit(solution)/shard_map/all_to_all | solution.py:343
  56.0 0.3 sum_x.1
  56.3 21.4 %all_to_all.26.parts = f32[8,96,128]{2,1,0:T(8,128)S(1)} all-to-all(f32[8,96,128]{2,1,0:T(8,128)S(1)} %sum_x.1), channel_id=1, replica_groups=mesh['layer'=8,'xl'=2,'xh'=2,'y'=8,'c'=2] {'y'}, dimensions={0} | all-to-all | bytes 786432 | tf_op jit(solution)/shard_map/all_to_all | solution.py:352
  77.7 5.2 %all-gather.3.cloned.1.call-done = f32[64,6,8,512]{3,2,1,0:T(8,128)} async-done(((f32[4,6,8,512]{3,2,1,0:T(8,128)}), f32[64,6,8,512]{3,2,1,0:T(8,128)}) %all-gather.3.cloned.1.call-update) | async-done | bytes 6291472 | tf_op jit(solution)/shard_map/all_gather | solution.py:340
  82.9 3.3 %chain_first.1 = (f32[2,16,512]{2,1,0:T(8,128)S(1)}, f32[2,16,512]{2,1,0:T(8,128)S(1)}, bf16[4,512,512]{2,1,0:T(8,128)(2,1)S(1)}, bf16[4,512,512]{2,1,0:T(8,128)(2,1)S(1)}) custom-call(f32[8,96,128]{2,1,0:T(8,128)S(1)} %all_to_all.26.parts, f32[16,4,6,8,512]{4,3,2,1,0:T(8,128)} %bitcast.2), custom_call_target="tpu_custom_call" | custom-call | tf_op jit(solution)/shard_map/chain_first/pallas_call | solution.py:354
  86.2 3.0 %collective-permute-start.1 = (f32[2,16,512]{2,1,0:T(8,128)S(1)}, f32[2,16,512]{2,1,0:T(8,128)S(1)}, u32[]{:S(2)}, u32[]{:S(2)}) collective-permute-start(f32[2,16,512]{2,1,0:T(8,128)S(1)} %get-tuple-element.19), channel_id=1, source_target_pairs={{0,16},{1,17},{2,18},{3,19},{4,20},{5,21},{6,22},{7,23},{8,24},{9,... | collective-permute-start | bytes 196616 | tf_op jit(solution)/shard_map/ppermute | solution.py:363
  89.3 1.3 collective-permute-done.1.came
  90.6 0.2 chain_second.1
  90.7 20.7 %all_to_all.27.got = f32[64,3,128]{2,1,0:T(4,128)S(1)} all-to-all(f32[64,3,128]{2,1,0:T(4,128)S(1)} %chain_second.1), channel_id=1, replica_groups=mesh['layer'=8,'xl'=2,'xh'=2,'y'=8,'c'=2] {'xl','xh','y','c'}, dimensions={0} | all-to-all | bytes 196608 | tf_op jit(solution)/shard_map/all_to_all | solution.py:374
  111.5 1.0 unpack.1
  112.5 14.3 %all_to_all.28 = f32[8,8,384]{2,1,0:T(8,128)S(1)} all-to-all(f32[8,8,384]{2,1,0:T(8,128)S(1)} %get-tuple-element.23), channel_id=1, replica_groups=mesh['layer'=8,'xl'=2,'xh'=2,'y'=8,'c'=2] {'layer'}, dimensions={0} | all-to-all | bytes 196608 | tf_op jit(solution)/shard_map/all_to_all | solution.py:383
  126.8 0.6 reduce_sum.9
Async XLA Ops:
  8.8 11.1 %all-to-all-start = ((f32[4,6,8,512]{3,2,1,0:T(8,128)}), f32[4,6,8,512]{3,2,1,0:T(8,128)S(1)}, u32[]{:S(2)}, u32[]{:S(2)}) async-start(f32[4,6,8,512]{3,2,1,0:T(8,128)} %pack.1), calls=%async_computation | async-start | bytes 786432 | tf_op jit(solution)/shard_map/all_to_all | solution.py:333
  13.7 69.3 %all-gather.3.cloned.1.call-start = ((), (), s32[]{:S(2)}) async-start(), calls=%async_computation.5 | async-start | bytes 6684672 | tf_op jit(solution)/shard_map/all_gather | solution.py:340
  19.9 0.7 copy-start
  20.7 12.0 %collective-permute-start = (f32[2,2,2,4,96,128]{5,4,3,2,1,0:T(8,128)S(1)}, f32[2,2,2,4,96,128]{5,4,3,2,1,0:T(8,128)S(1)}, u32[]{:S(2)}, u32[]{:S(2)}) collective-permute-start(f32[2,2,2,4,96,128]{5,4,3,2,1,0:T(8,128)S(1)} %get-tuple-element.16), channel_id=1, source_target_pairs={{0,1},{1,0},{2,3},{3,2},{4,5},{5,4},{6,7},{7,6},{8,9},{9,8},{10,11... | collective-permute-start | bytes 4718600 | tf_op jit(solution)/shard_map/ppermute | solution.py:342
  86.2 4.3 %collective-permute-start.1 = (f32[2,16,512]{2,1,0:T(8,128)S(1)}, f32[2,16,512]{2,1,0:T(8,128)S(1)}, u32[]{:S(2)}, u32[]{:S(2)}) collective-permute-start(f32[2,16,512]{2,1,0:T(8,128)S(1)} %get-tuple-element.19), channel_id=1, source_target_pairs={{0,16},{1,17},{2,18},{3,19},{4,20},{5,21},{6,22},{7,23},{8,24},{9,... | collective-permute-start | bytes 196616 | tf_op jit(solution)/shard_map/ppermute | solution.py:363
Sparse Core Ops, SparseCore 0:
  20.8 62.1 all-gather.2

commit v8 on v7

--- a/solution.py
+++ b/solution.py
@@ -59,15 +59,8 @@
     zeros = jnp.zeros_like(root_inverse)
     rr = jnp.concatenate([root_rhs[...], zeros[:, root_rhs.shape[1] :]], axis=1)
     tables = (
-        [sep_inverse[0, 0], sep_inverse[0, 1], sep_coupling[0, 0], rr, zeros, zeros],
-        [
-            sep_inverse[0, 2],
-            sep_inverse[0, 3],
-            sep_coupling[0, 1],
-            sep_coupling[0, 2],
-            root_coupling[0],
-            root_inverse[...],
-        ],
+        [sep_inverse[0, 0], sep_inverse[0, 1], sep_coupling[0, 0], sep_coupling[0, 1], rr],
+        [sep_inverse[0, 2], sep_inverse[0, 3], sep_coupling[0, 2], root_coupling[0], root_inverse[...]],
     )
     for x in range(out.shape[0]):
         for m in range(out.shape[1]):
@@ -189,15 +182,9 @@
             copy.wait()
         return split(full[m].reshape(-1, full.shape[3]))
 
-    for m in range(4):
+    for m in range(full.shape[0]):
         for copy in copies(m):
             copy.start()
-
-    @pl.when(odd)
-    def _():
-        for m in range(4, full.shape[0]):
-            for copy in copies(m):
-                copy.start()
 
     res = parts[0]
     for p in range(1, parts.shape[0]):
@@ -213,26 +200,24 @@
     second = dot3(residual(1), matrix(1), NT)
     held[0] = first
     held[1] = second
-    last = [matrix(2), matrix(3)]
 
     @pl.when(jnp.logical_not(odd))
     def _():
-        chained = second - dot3(stack(first), last[0], NT)
+        chained = second - dot3(stack(first), matrix(2), NT)
+        held[1] = chained
+        send[0] = dot3(stack(chained), matrix(3), NT)
         shape = held.shape[1:]
         group = (lax.axis_index("c") * 2 + lax.axis_index("xl")) * NY + lax.axis_index("y")
         column = lax.broadcasted_iota(jnp.int32, shape, 0) + part * group
         mine = lax.broadcasted_iota(jnp.int32, shape, 1) == column
         pick = jnp.where(mine, jnp.where(lax.axis_index("layer") == 0, 1.0, 0.0), 0.0).astype(jnp.bfloat16)
         mm = functools.partial(lax.dot_general, dimension_numbers=NT, preferred_element_type=jnp.float32)
-        held[1] = chained
-        send[0] = chained
-        send[1] = mm(pick, last[1][0]) + mm(pick, last[1][1])
+        rhs_high, rhs_low = matrix(4)
+        send[1] = mm(pick, rhs_high) + mm(pick, rhs_low)
 
     @pl.when(odd)
     def _():
-        for at, pair in enumerate(last):
-            high[at], low[at] = pair
-        for m in range(4, full.shape[0]):
+        for m in range(2, full.shape[0]):
             high[m - 2], low[m - 2] = matrix(m)
 
 
@@ -251,12 +236,12 @@
 
     @pl.when(lax.axis_index("xh") == 1)
     def _():
-        third = held[0] - dot3(stack(came[0]), (high[0], low[0]), NT)
+        third = held[0] - came[0]
         store(0, third)
-        fourth = held[1] - dot3(stack(third), (high[1], low[1]), NT)
+        fourth = held[1] - dot3(stack(third), (high[0], low[0]), NT)
         store(1, fourth)
-        term = came[1] - dot3(stack(fourth), (high[2], low[2]), NT)
-        store(2, dot3(stack(term), (high[3], low[3]), NT))
+        term = came[1] - dot3(stack(fourth), (high[1], low[1]), NT)
+        store(2, dot3(stack(term), (high[2], low[2]), NT))
 
     rows = wide[...].T.reshape(-1, 8, 128)
     lane = lax.broadcasted_iota(jnp.int32, (rows.shape[0], 1, 128), 2)
@@ -327,7 +312,7 @@
         pack_kernel,
         in_specs=[VMEM] * 5,
         out_specs=VMEM,
-        out_shape=FLAT((NX, 6, 8, width), jnp.float32),
+        out_shape=FLAT((NX, 5, 8, width), jnp.float32),
         name="pack",
     )(sep_inverse, sep_coupling, root_coupling, root_rhs, root_inverse)
     exchanged = lax.all_to_all(pack, X, 0, 0)
@@ -355,8 +340,8 @@
         functools.partial(first_kernel, part),
         in_specs=[VMEM, HBM],
         out_specs=[VMEM] * 4,
-        out_shape=[FLAT((2, 16, width), jnp.float32)] * 2 + [FLAT((4, width, width), jnp.bfloat16)] * 2,
-        scratch_shapes=[pltpu.VMEM((6, 64, 8, width), jnp.float32), pltpu.SemaphoreType.DMA((6, NX))],
+        out_shape=[FLAT((2, 16, width), jnp.float32)] * 2 + [FLAT((3, width, width), jnp.bfloat16)] * 2,
+        scratch_shapes=[pltpu.VMEM((5, 64, 8, width), jnp.float32), pltpu.SemaphoreType.DMA((5, NX))],
         compiler_params=pltpu.CompilerParams(vmem_limit_bytes=32 * 2**20),
         name="chain_first",
     )(res, in_hbm(weights))

time: 135 us -> 129 us (0.956)
  waiting for transfers between devices: 7.9 us -> 4.22 us
  blocking collectives: 79.6 us -> 77.7 us
    all_gather x1, waiting for transfers between devices: 5.23 us -> 1.91 us  [body(): weights = lax.all_gather(exchanged, ('y', 'c'))]
where the time goes in v8:
time: 129 us
  blocking collectives  77.7 us (60%)
  starting transfers between devices  16.2 us (13%)
  between operations  14.7 us (11%)
  Pallas kernels  14.2 us (11%)
  waiting for transfers between devices  4.22 us (3%)
    all_to_all x1, blocking collectives, body(): res = lax.all_to_all(res.reshape(NX, 2 * tiles * 8 * part, 128), X, 0, 0)  23 us
    all_to_all x1, blocking collectives, body(): out = lax.all_to_all(out, ROW, 0, 0)  20.8 us
    all_to_all x1, blocking collectives, body(): res = lax.all_to_all(res, 'y', 0, 0)  20.6 us
    all_to_all x1, blocking collectives, body(): root_out = lax.all_to_all(term, 'layer', 0, 0).sum(0)  13.2 us
    ppermute x1, starting transfers between devices, body(): res = keep + lax.ppermute(send, 'c', [(0, 1), (1, 0)])  8.52 us
    all_to_all x1, starting transfers between devices, body(): exchanged = lax.all_to_all(pack, X, 0, 0)  4.84 us
    pallas_call x1, Pallas kernels, leaves_send(): pl.pallas_call(functools.partial(send_kernel, part), grid=(n,), in_specs=...  4.23 us
    pallas_call x1, Pallas kernels, leaves_keep(): pl.pallas_call(functools.partial(keep_kernel, part), grid=(coupling.shape...  3.46 us
  transfers between devices with their start and end apart: 4, of which 3 were waited for; matrix products, arithmetic and copies ran while one was open for 0% of the time, Pallas kernels for 6%

profile of v8, /device:TPU:1, one launch (start us, length us, event | category | flops | bytes accessed | tf_op | source)
XLA Modules:
  0.0 128.6 jit_solution(1593124820674502600)
XLA Ops:
  7.2 1.6 %pack.1 = f32[4,5,8,512]{3,2,1,0:T(8,128)} custom-call(f32[1,4,8,512]{3,2,1,0:T(8,128)} %sep_inverse.1, f32[1,3,8,512]{3,2,1,0:T(8,128)} %sep_coupling.1, f32[1,8,512]{2,1,0:T(8,128)} %root_coupling.1, f32[8,384]{1,0:T(8,128)} %root_rhs.1, f32[8,512]{1,0:T(8,128)} %root_inverse.1), custom_call_target="tpu_custom_call" | custom-call | tf_op jit(solution)/shard_map/pack/pallas_call | solution.py:311
  8.8 4.8 %all-to-all-start = ((f32[4,5,8,512]{3,2,1,0:T(8,128)}), f32[4,5,8,512]{3,2,1,0:T(8,128)S(1)}, u32[]{:S(2)}, u32[]{:S(2)}) async-start(f32[4,5,8,512]{3,2,1,0:T(8,128)} %pack.1), calls=%async_computation | async-start | bytes 655360 | tf_op jit(solution)/shard_map/all_to_all | solution.py:318
  13.6 0.0 all-gather.3.cloned.1.call-start
  14.3 4.2 %leaves_send.1 = (f32[2,2,2,4,96,128]{5,4,3,2,1,0:T(8,128)S(1)}, f32[384,256]{1,0:T(8,128)S(1)}, f32[384,128]{1,0:T(8,128)S(1)}) custom-call(s32[1,1]{1,0:T(1,128)S(6)} %copy.12.parent, f32[1,1,256,384]{3,2,1,0:T(8,128)} %rhs.1, f32[1,1,256,256]{3,2,1,0:T(8,128)} %inv.1, f32[1,4,8,384]{3,2,1,0:T(8,128)} %sep.1, f32[1,1,4,512,256]{4,3,2,1,0:T(8,128)} %coupling.3), custom_call_target="tpu_custom_call" | custom-call | tf_op jit(solution)/shard_map/leaves_send/pallas_call | solution.py:131
  18.5 1.0 all-to-all-done
  19.5 0.0 copy-start
  19.5 0.7 copy-done
  20.3 0.0 all-gather.3.cloned.1.call-update
  20.3 8.5 %collective-permute-start = (f32[2,2,2,4,96,128]{5,4,3,2,1,0:T(8,128)S(1)}, f32[2,2,2,4,96,128]{5,4,3,2,1,0:T(8,128)S(1)}, u32[]{:S(2)}, u32[]{:S(2)}) collective-permute-start(f32[2,2,2,4,96,128]{5,4,3,2,1,0:T(8,128)S(1)} %get-tuple-element.16), channel_id=1, source_target_pairs={{0,1},{1,0},{2,3},{3,2},{4,5},{5,4},{6,7},{7,6},{8,9},{9,8},{10,11... | collective-permute-start | bytes 4718600 | tf_op jit(solution)/shard_map/ppermute | solution.py:327
  28.8 3.5 %leaves_keep.1 = f32[2,2,2,4,96,128]{5,4,3,2,1,0:T(8,128)S(1)} custom-call(s32[1,1]{1,0:T(1,128)S(6)} %copy.12.parent, f32[384,256]{1,0:T(8,128)S(1)} %get-tuple-element.14.xt, f32[384,128]{1,0:T(8,128)S(1)} %get-tuple-element.15.own, f32[1,1,4,512,256]{4,3,2,1,0:T(8,128)} %coupling.3), custom_call_target="tpu_custom_call" | custom-call | tf_op jit(solution)/shard_map/leaves_keep/pallas_call | solution.py:150
  32.3 0.0 collective-permute-done
  32.3 0.2 add.3
  32.5 23.0 %all_to_all.25.parts = f32[4,768,128]{2,1,0:T(8,128)S(1)} all-to-all(f32[4,768,128]{2,1,0:T(8,128)S(1)} %bitcast.2), channel_id=1, replica_groups=mesh['layer'=8,'xl'=2,'xh'=2,'y'=8,'c'=2] {'xl','xh'}, dimensions={0} | all-to-all | bytes 3145728 | tf_op jit(solution)/shard_map/all_to_all | solution.py:328
  55.5 0.3 sum_x.1
  55.8 20.6 %all_to_all.26.parts = f32[8,96,128]{2,1,0:T(8,128)S(1)} all-to-all(f32[8,96,128]{2,1,0:T(8,128)S(1)} %sum_x.1), channel_id=1, replica_groups=mesh['layer'=8,'xl'=2,'xh'=2,'y'=8,'c'=2] {'y'}, dimensions={0} | all-to-all | bytes 786432 | tf_op jit(solution)/shard_map/all_to_all | solution.py:337
  76.5 1.9 %all-gather.3.cloned.1.call-done = f32[64,5,8,512]{3,2,1,0:T(8,128)} async-done(((f32[4,5,8,512]{3,2,1,0:T(8,128)}), f32[64,5,8,512]{3,2,1,0:T(8,128)}) %all-gather.3.cloned.1.call-update) | async-done | bytes 5242896 | tf_op jit(solution)/shard_map/all_gather | solution.py:325
  78.4 3.4 %chain_first.1 = (f32[2,16,512]{2,1,0:T(8,128)S(1)}, f32[2,16,512]{2,1,0:T(8,128)S(1)}, bf16[3,512,512]{2,1,0:T(8,128)(2,1)S(1)}, bf16[3,512,512]{2,1,0:T(8,128)(2,1)S(1)}) custom-call(f32[8,96,128]{2,1,0:T(8,128)S(1)} %all_to_all.26.parts, f32[16,4,5,8,512]{4,3,2,1,0:T(8,128)} %bitcast.3), custom_call_target="tpu_custom_call" | custom-call | tf_op jit(solution)/shard_map/chain_first/pallas_call | solution.py:339
  81.8 2.8 %collective-permute-start.1 = (f32[2,16,512]{2,1,0:T(8,128)S(1)}, f32[2,16,512]{2,1,0:T(8,128)S(1)}, u32[]{:S(2)}, u32[]{:S(2)}) collective-permute-start(f32[2,16,512]{2,1,0:T(8,128)S(1)} %get-tuple-element.19), channel_id=1, source_target_pairs={{0,16},{1,17},{2,18},{3,19},{4,20},{5,21},{6,22},{7,23},{8,24},{9,... | collective-permute-start | bytes 196616 | tf_op jit(solution)/shard_map/ppermute | solution.py:348
  84.6 1.3 %collective-permute-done.1.came = f32[2,16,512]{2,1,0:T(8,128)S(1)} collective-permute-done((f32[2,16,512]{2,1,0:T(8,128)S(1)}, f32[2,16,512]{2,1,0:T(8,128)S(1)}, u32[]{:S(2)}, u32[]{:S(2)}) %collective-permute-start.1) | collective-permute-done | bytes 65568 | tf_op jit(solution)/shard_map/ppermute | solution.py:348
  85.9 0.2 chain_second.1
  86.1 20.8 %all_to_all.27.got = f32[64,3,128]{2,1,0:T(4,128)S(1)} all-to-all(f32[64,3,128]{2,1,0:T(4,128)S(1)} %chain_second.1), channel_id=1, replica_groups=mesh['layer'=8,'xl'=2,'xh'=2,'y'=8,'c'=2] {'xl','xh','y','c'}, dimensions={0} | all-to-all | bytes 196608 | tf_op jit(solution)/shard_map/all_to_all | solution.py:359
  106.9 1.0 unpack.1
  107.9 13.2 %all_to_all.28 = f32[8,8,384]{2,1,0:T(8,128)S(1)} all-to-all(f32[8,8,384]{2,1,0:T(8,128)S(1)} %get-tuple-element.23), channel_id=1, replica_groups=mesh['layer'=8,'xl'=2,'xh'=2,'y'=8,'c'=2] {'layer'}, dimensions={0} | all-to-all | bytes 196608 | tf_op jit(solution)/shard_map/all_to_all | solution.py:368
  121.2 0.6 reduce_sum.9
Async XLA Ops:
  8.8 10.7 %all-to-all-start = ((f32[4,5,8,512]{3,2,1,0:T(8,128)}), f32[4,5,8,512]{3,2,1,0:T(8,128)S(1)}, u32[]{:S(2)}, u32[]{:S(2)}) async-start(f32[4,5,8,512]{3,2,1,0:T(8,128)} %pack.1), calls=%async_computation | async-start | bytes 655360 | tf_op jit(solution)/shard_map/all_to_all | solution.py:318
  13.6 64.7 %all-gather.3.cloned.1.call-start = ((), (), s32[]{:S(2)}) async-start(), calls=%async_computation.5 | async-start | bytes 5570560 | tf_op jit(solution)/shard_map/all_gather | solution.py:325
  19.5 0.7 copy-start
  20.3 12.0 %collective-permute-start = (f32[2,2,2,4,96,128]{5,4,3,2,1,0:T(8,128)S(1)}, f32[2,2,2,4,96,128]{5,4,3,2,1,0:T(8,128)S(1)}, u32[]{:S(2)}, u32[]{:S(2)}) collective-permute-start(f32[2,2,2,4,96,128]{5,4,3,2,1,0:T(8,128)S(1)} %get-tuple-element.16), channel_id=1, source_target_pairs={{0,1},{1,0},{2,3},{3,2},{4,5},{5,4},{6,7},{7,6},{8,9},{9,8},{10,11... | collective-permute-start | bytes 4718600 | tf_op jit(solution)/shard_map/ppermute | solution.py:327
  81.8 4.1 %collective-permute-start.1 = (f32[2,16,512]{2,1,0:T(8,128)S(1)}, f32[2,16,512]{2,1,0:T(8,128)S(1)}, u32[]{:S(2)}, u32[]{:S(2)}) collective-permute-start(f32[2,16,512]{2,1,0:T(8,128)S(1)} %get-tuple-element.19), channel_id=1, source_target_pairs={{0,16},{1,17},{2,18},{3,19},{4,20},{5,21},{6,22},{7,23},{8,24},{9,... | collective-permute-start | bytes 196616 | tf_op jit(solution)/shard_map/ppermute | solution.py:348
Sparse Core Ops, SparseCore 0:
  20.4 57.9 all-gather.2

commit v9 on v8

--- a/solution.py
+++ b/solution.py
@@ -34,6 +34,10 @@
     return both[:rows] + (both[rows:] + mm(a[:rows], b[1]))
 
 
+def pad(a):
+    return jnp.concatenate([a, jnp.zeros((16 - a.shape[0], a.shape[1]), jnp.float32)], axis=0)
+
+
 def by_tiles(ref, part):
     tiles, rows, _ = ref.shape
 
@@ -55,16 +59,20 @@
     return x, (x * NY + lax.axis_index("y")) * NC + lax.axis_index("c")
 
 
-def pack_kernel(sep_inverse, sep_coupling, root_coupling, root_rhs, root_inverse, out):
-    zeros = jnp.zeros_like(root_inverse)
-    rr = jnp.concatenate([root_rhs[...], zeros[:, root_rhs.shape[1] :]], axis=1)
+def pack_kernel(sep_inverse, sep_coupling, root_coupling, root_rhs, root_inverse, out, sems):
     tables = (
-        [sep_inverse[0, 0], sep_inverse[0, 1], sep_coupling[0, 0], sep_coupling[0, 1], rr],
-        [sep_inverse[0, 2], sep_inverse[0, 3], sep_coupling[0, 2], root_coupling[0], root_inverse[...]],
+        [sep_inverse.at[0, 0], sep_inverse.at[0, 1], sep_coupling.at[0, 0], sep_coupling.at[0, 1], root_rhs],
+        [sep_inverse.at[0, 2], sep_inverse.at[0, 3], sep_coupling.at[0, 2], root_coupling.at[0], root_inverse],
     )
+    copies = []
     for x in range(out.shape[0]):
-        for m in range(out.shape[1]):
-            out[x, m] = tables[x % 2][m]
+        for m, source in enumerate(tables[x % 2]):
+            target = out.at[x, m, :, pl.ds(0, source.shape[1])]
+            copies.append(pltpu.make_async_copy(source, target, sems.at[x, m]))
+    for copy in copies:
+        copy.start()
+    for copy in copies:
+        copy.wait()
 
 
 def half_update(part, other, parent, xt, own, coupling, out, pair):
@@ -166,7 +174,7 @@
         out[s] = (parts[0, rows, :] + parts[1, rows, :]) + (parts[2, rows, :] + parts[3, rows, :])
 
 
-def first_kernel(part, parts, weights, held, send, high, low, full, sems):
+def first_kernel(part, cols, parts, weights, held, send, high, low, full, sems):
     odd = lax.axis_index("xh") == 1
 
     def copies(m):
@@ -194,7 +202,7 @@
     def residual(k):
         starts = [part * (tiles * k + tile) for tile in range(tiles)]
         rows = jnp.concatenate([res[at : at + part] for at in starts], axis=1)
-        return stack(jnp.concatenate([rows, jnp.zeros((16 - part, rows.shape[1]), jnp.float32)], axis=0))
+        return stack(pad(rows))
 
     first = dot3(residual(0), matrix(0), NT)
     second = dot3(residual(1), matrix(1), NT)
@@ -205,15 +213,15 @@
     def _():
         chained = second - dot3(stack(first), matrix(2), NT)
         held[1] = chained
-        send[0] = dot3(stack(chained), matrix(3), NT)
-        shape = held.shape[1:]
+        send[:part] = dot3(stack(chained), matrix(3), NT)[:part]
+        shape = (16, cols)
         group = (lax.axis_index("c") * 2 + lax.axis_index("xl")) * NY + lax.axis_index("y")
         column = lax.broadcasted_iota(jnp.int32, shape, 0) + part * group
         mine = lax.broadcasted_iota(jnp.int32, shape, 1) == column
         pick = jnp.where(mine, jnp.where(lax.axis_index("layer") == 0, 1.0, 0.0), 0.0).astype(jnp.bfloat16)
         mm = functools.partial(lax.dot_general, dimension_numbers=NT, preferred_element_type=jnp.float32)
-        rhs_high, rhs_low = matrix(4)
-        send[1] = mm(pick, rhs_high) + mm(pick, rhs_low)
+        rhs_high, rhs_low = (half[:, :cols] for half in matrix(4))
+        send[part:] = (mm(pick, rhs_high) + mm(pick, rhs_low))[:part]
 
     @pl.when(odd)
     def _():
@@ -236,12 +244,12 @@
 
     @pl.when(lax.axis_index("xh") == 1)
     def _():
-        third = held[0] - came[0]
+        third = pad(held[0, :part] - came[:part])
         store(0, third)
         fourth = held[1] - dot3(stack(third), (high[0], low[0]), NT)
         store(1, fourth)
-        term = came[1] - dot3(stack(fourth), (high[1], low[1]), NT)
-        store(2, dot3(stack(term), (high[2], low[2]), NT))
+        term = came[part:] - dot3(stack(fourth), (high[1], low[1]), NT)[:part]
+        store(2, dot3(stack(pad(term)), (high[2], low[2]), NT))
 
     rows = wide[...].T.reshape(-1, 8, 128)
     lane = lax.broadcasted_iota(jnp.int32, (rows.shape[0], 1, 128), 2)
@@ -310,11 +318,12 @@
 
     pack = call(
         pack_kernel,
-        in_specs=[VMEM] * 5,
-        out_specs=VMEM,
-        out_shape=FLAT((NX, 5, 8, width), jnp.float32),
+        in_specs=[HBM] * 5,
+        out_specs=HBM,
+        out_shape=pltpu.HBM((NX, 5, 8, width), jnp.float32),
+        scratch_shapes=[pltpu.SemaphoreType.DMA((NX, 5))],
         name="pack",
-    )(sep_inverse, sep_coupling, root_coupling, root_rhs, root_inverse)
+    )(*map(in_hbm, (sep_inverse, sep_coupling, root_coupling, root_rhs, root_inverse)))
     exchanged = lax.all_to_all(pack, X, 0, 0)
 
     leaf_rhs, leaf_inverse, leaf_coupling, sep_rhs = map(
@@ -337,10 +346,11 @@
     res = lax.all_to_all(res, "y", 0, 0)
 
     held, send, high, low = call(
-        functools.partial(first_kernel, part),
+        functools.partial(first_kernel, part, cols),
         in_specs=[VMEM, HBM],
         out_specs=[VMEM] * 4,
-        out_shape=[FLAT((2, 16, width), jnp.float32)] * 2 + [FLAT((3, width, width), jnp.bfloat16)] * 2,
+        out_shape=[FLAT((2, 16, width), jnp.float32), FLAT((2 * part, width), jnp.float32)]
+        + [FLAT((3, width, width), jnp.bfloat16)] * 2,
         scratch_shapes=[pltpu.VMEM((5, 64, 8, width), jnp.float32), pltpu.SemaphoreType.DMA((5, NX))],
         compiler_params=pltpu.CompilerParams(vmem_limit_bytes=32 * 2**20),
         name="chain_first",

time: 129 us -> 138 us (1.070)
  Pallas kernels: 14.2 us -> 23.5 us
    pallas_call x2, Pallas kernels: 5.05 us -> 14.3 us  [the longest x1 11 us: body(): call(pack_kernel, in_specs=[HBM] * 5, out_specs=HBM, out_shape=pltpu.HBM(...]
where the time goes in v9:
time: 138 us
  blocking collectives  77.7 us (56%)
  Pallas kernels  23.5 us (17%)
  starting transfers between devices  16.3 us (12%)
  between operations  14.7 us (11%)
  waiting for transfers between devices  4.06 us (3%)
    all_to_all x1, blocking collectives, body(): res = lax.all_to_all(res.reshape(NX, 2 * tiles * 8 * part, 128), X, 0, 0)  23 us
    all_to_all x1, blocking collectives, body(): out = lax.all_to_all(out, ROW, 0, 0)  20.8 us
    all_to_all x1, blocking collectives, body(): res = lax.all_to_all(res, 'y', 0, 0)  20.6 us
    all_to_all x1, blocking collectives, body(): root_out = lax.all_to_all(term, 'layer', 0, 0).sum(0)  13.2 us
    pallas_call x1, Pallas kernels, body(): call(pack_kernel, in_specs=[HBM] * 5, out_specs=HBM, out_shape=pltpu.HBM(...  11 us
    ppermute x1, starting transfers between devices, body(): res = keep + lax.ppermute(send, 'c', [(0, 1), (1, 0)])  8.52 us
    all_to_all x1, starting transfers between devices, body(): exchanged = lax.all_to_all(pack, X, 0, 0)  4.85 us
    pallas_call x1, Pallas kernels, leaves_send(): pl.pallas_call(functools.partial(send_kernel, part), grid=(n,), in_specs=...  4.24 us
  transfers between devices with their start and end apart: 4, of which 3 were waited for; matrix products, arithmetic and copies ran while one was open for 0% of the time, Pallas kernels for 6%

profile of v9, /device:TPU:1, one launch (start us, length us, event | category | flops | bytes accessed | tf_op | source)
XLA Modules:
  0.0 137.8 jit_solution(269185881414155595)
XLA Ops:
  7.2 11.0 %pack.1 = f32[4,5,8,512]{3,2,1,0:T(8,128)} custom-call(f32[1,4,8,512]{3,2,1,0:T(8,128)} %sep_inverse.1, f32[1,3,8,512]{3,2,1,0:T(8,128)} %sep_coupling.1, f32[1,8,512]{2,1,0:T(8,128)} %root_coupling.1, f32[8,384]{1,0:T(8,128)} %root_rhs.1, f32[8,512]{1,0:T(8,128)} %root_inverse.1), custom_call_target="tpu_custom_call" | custom-call | tf_op jit(solution)/shard_map/pack/pallas_call | solution.py:319
  18.1 4.9 %all-to-all-start = ((f32[4,5,8,512]{3,2,1,0:T(8,128)}), f32[4,5,8,512]{3,2,1,0:T(8,128)S(1)}, u32[]{:S(2)}, u32[]{:S(2)}) async-start(f32[4,5,8,512]{3,2,1,0:T(8,128)} %pack.1), calls=%async_computation | async-start | bytes 655360 | tf_op jit(solution)/shard_map/all_to_all | solution.py:327
  23.0 0.0 all-gather.3.cloned.1.call-start
  23.6 4.2 %leaves_send.1 = (f32[2,2,2,4,96,128]{5,4,3,2,1,0:T(8,128)S(1)}, f32[384,256]{1,0:T(8,128)S(1)}, f32[384,128]{1,0:T(8,128)S(1)}) custom-call(s32[1,1]{1,0:T(1,128)S(6)} %copy.12.parent, f32[1,1,256,384]{3,2,1,0:T(8,128)} %rhs.1, f32[1,1,256,256]{3,2,1,0:T(8,128)} %inv.1, f32[1,4,8,384]{3,2,1,0:T(8,128)} %sep.1, f32[1,1,4,512,256]{4,3,2,1,0:T(8,128)} %coupling.3), custom_call_target="tpu_custom_call" | custom-call | tf_op jit(solution)/shard_map/leaves_send/pallas_call | solution.py:139
  27.9 1.0 all-to-all-done
  28.9 0.0 copy-start
  28.9 0.7 copy-done
  29.6 0.0 all-gather.3.cloned.1.call-update
  29.6 8.5 %collective-permute-start = (f32[2,2,2,4,96,128]{5,4,3,2,1,0:T(8,128)S(1)}, f32[2,2,2,4,96,128]{5,4,3,2,1,0:T(8,128)S(1)}, u32[]{:S(2)}, u32[]{:S(2)}) collective-permute-start(f32[2,2,2,4,96,128]{5,4,3,2,1,0:T(8,128)S(1)} %get-tuple-element.16), channel_id=1, source_target_pairs={{0,1},{1,0},{2,3},{3,2},{4,5},{5,4},{6,7},{7,6},{8,9},{9,8},{10,11... | collective-permute-start | bytes 4718600 | tf_op jit(solution)/shard_map/ppermute | solution.py:336
  38.2 3.5 %leaves_keep.1 = f32[2,2,2,4,96,128]{5,4,3,2,1,0:T(8,128)S(1)} custom-call(s32[1,1]{1,0:T(1,128)S(6)} %copy.12.parent, f32[384,256]{1,0:T(8,128)S(1)} %get-tuple-element.14.xt, f32[384,128]{1,0:T(8,128)S(1)} %get-tuple-element.15.own, f32[1,1,4,512,256]{4,3,2,1,0:T(8,128)} %coupling.3), custom_call_target="tpu_custom_call" | custom-call | tf_op jit(solution)/shard_map/leaves_keep/pallas_call | solution.py:158
  41.6 0.0 collective-permute-done
  41.6 0.2 add.3
  41.8 23.0 %all_to_all.25.parts = f32[4,768,128]{2,1,0:T(8,128)S(1)} all-to-all(f32[4,768,128]{2,1,0:T(8,128)S(1)} %bitcast.2), channel_id=1, replica_groups=mesh['layer'=8,'xl'=2,'xh'=2,'y'=8,'c'=2] {'xl','xh'}, dimensions={0} | all-to-all | bytes 3145728 | tf_op jit(solution)/shard_map/all_to_all | solution.py:337
  64.9 0.3 sum_x.1
  65.2 20.6 %all_to_all.26.parts = f32[8,96,128]{2,1,0:T(8,128)S(1)} all-to-all(f32[8,96,128]{2,1,0:T(8,128)S(1)} %sum_x.1), channel_id=1, replica_groups=mesh['layer'=8,'xl'=2,'xh'=2,'y'=8,'c'=2] {'y'}, dimensions={0} | all-to-all | bytes 786432 | tf_op jit(solution)/shard_map/all_to_all | solution.py:346
  85.8 1.9 %all-gather.3.cloned.1.call-done = f32[64,5,8,512]{3,2,1,0:T(8,128)} async-done(((f32[4,5,8,512]{3,2,1,0:T(8,128)}), f32[64,5,8,512]{3,2,1,0:T(8,128)}) %all-gather.3.cloned.1.call-update) | async-done | bytes 5242896 | tf_op jit(solution)/shard_map/all_gather | solution.py:334
  87.7 3.4 %chain_first.1 = (f32[2,16,512]{2,1,0:T(8,128)S(1)}, f32[24,512]{1,0:T(8,128)S(1)}, bf16[3,512,512]{2,1,0:T(8,128)(2,1)S(1)}, bf16[3,512,512]{2,1,0:T(8,128)(2,1)S(1)}) custom-call(f32[8,96,128]{2,1,0:T(8,128)S(1)} %all_to_all.26.parts, f32[16,4,5,8,512]{4,3,2,1,0:T(8,128)} %bitcast.3), custom_call_target="tpu_custom_call" | custom-call | tf_op jit(solution)/shard_map/chain_first/pallas_call | solution.py:348
  91.1 2.9 %collective-permute-start.1 = (f32[24,512]{1,0:T(8,128)S(1)}, f32[24,512]{1,0:T(8,128)S(1)}, u32[]{:S(2)}, u32[]{:S(2)}) collective-permute-start(f32[24,512]{1,0:T(8,128)S(1)} %get-tuple-element.19), channel_id=1, source_target_pairs={{0,16},{1,17},{2,18},{3,19},{4,20},{5,21},{6,22},{7,23},{8,24},{9,... | collective-permute-start | bytes 147464 | tf_op jit(solution)/shard_map/ppermute | solution.py:358
  94.0 1.2 collective-permute-done.1.came
  95.1 0.2 chain_second.1
  95.3 20.8 %all_to_all.27.got = f32[64,3,128]{2,1,0:T(4,128)S(1)} all-to-all(f32[64,3,128]{2,1,0:T(4,128)S(1)} %chain_second.1), channel_id=1, replica_groups=mesh['layer'=8,'xl'=2,'xh'=2,'y'=8,'c'=2] {'xl','xh','y','c'}, dimensions={0} | all-to-all | bytes 196608 | tf_op jit(solution)/shard_map/all_to_all | solution.py:369
  116.1 1.0 unpack.1
  117.1 13.2 %all_to_all.28 = f32[8,8,384]{2,1,0:T(8,128)S(1)} all-to-all(f32[8,8,384]{2,1,0:T(8,128)S(1)} %get-tuple-element.23), channel_id=1, replica_groups=mesh['layer'=8,'xl'=2,'xh'=2,'y'=8,'c'=2] {'layer'}, dimensions={0} | all-to-all | bytes 196608 | tf_op jit(solution)/shard_map/all_to_all | solution.py:378
  130.3 0.6 reduce_sum.9
Async XLA Ops:
  18.1 10.7 %all-to-all-start = ((f32[4,5,8,512]{3,2,1,0:T(8,128)}), f32[4,5,8,512]{3,2,1,0:T(8,128)S(1)}, u32[]{:S(2)}, u32[]{:S(2)}) async-start(f32[4,5,8,512]{3,2,1,0:T(8,128)} %pack.1), calls=%async_computation | async-start | bytes 655360 | tf_op jit(solution)/shard_map/all_to_all | solution.py:327
  23.0 64.7 %all-gather.3.cloned.1.call-start = ((), (), s32[]{:S(2)}) async-start(), calls=%async_computation.5 | async-start | bytes 5570560 | tf_op jit(solution)/shard_map/all_gather | solution.py:334
  28.9 0.7 copy-start
  29.6 12.0 %collective-permute-start = (f32[2,2,2,4,96,128]{5,4,3,2,1,0:T(8,128)S(1)}, f32[2,2,2,4,96,128]{5,4,3,2,1,0:T(8,128)S(1)}, u32[]{:S(2)}, u32[]{:S(2)}) collective-permute-start(f32[2,2,2,4,96,128]{5,4,3,2,1,0:T(8,128)S(1)} %get-tuple-element.16), channel_id=1, source_target_pairs={{0,1},{1,0},{2,3},{3,2},{4,5},{5,4},{6,7},{7,6},{8,9},{9,8},{10,11... | collective-permute-start | bytes 4718600 | tf_op jit(solution)/shard_map/ppermute | solution.py:336
  91.1 4.1 %collective-permute-start.1 = (f32[24,512]{1,0:T(8,128)S(1)}, f32[24,512]{1,0:T(8,128)S(1)}, u32[]{:S(2)}, u32[]{:S(2)}) collective-permute-start(f32[24,512]{1,0:T(8,128)S(1)} %get-tuple-element.19), channel_id=1, source_target_pairs={{0,16},{1,17},{2,18},{3,19},{4,20},{5,21},{6,22},{7,23},{8,24},{9,... | collective-permute-start | bytes 147464 | tf_op jit(solution)/shard_map/ppermute | solution.py:358
Sparse Core Ops, SparseCore 0:
  29.8 57.9 all-gather.2

commit v10 on v9

--- a/solution.py
+++ b/solution.py
@@ -59,20 +59,16 @@
     return x, (x * NY + lax.axis_index("y")) * NC + lax.axis_index("c")
 
 
-def pack_kernel(sep_inverse, sep_coupling, root_coupling, root_rhs, root_inverse, out, sems):
+def pack_kernel(sep_inverse, sep_coupling, root_coupling, root_rhs, root_inverse, out):
+    zeros = jnp.zeros_like(root_inverse)
+    rr = jnp.concatenate([root_rhs[...], zeros[:, root_rhs.shape[1] :]], axis=1)
     tables = (
-        [sep_inverse.at[0, 0], sep_inverse.at[0, 1], sep_coupling.at[0, 0], sep_coupling.at[0, 1], root_rhs],
-        [sep_inverse.at[0, 2], sep_inverse.at[0, 3], sep_coupling.at[0, 2], root_coupling.at[0], root_inverse],
+        [sep_inverse[0, 0], sep_inverse[0, 1], sep_coupling[0, 0], sep_coupling[0, 1], rr],
+        [sep_inverse[0, 2], sep_inverse[0, 3], sep_coupling[0, 2], root_coupling[0], root_inverse[...]],
     )
-    copies = []
     for x in range(out.shape[0]):
-        for m, source in enumerate(tables[x % 2]):
-            target = out.at[x, m, :, pl.ds(0, source.shape[1])]
-            copies.append(pltpu.make_async_copy(source, target, sems.at[x, m]))
-    for copy in copies:
-        copy.start()
-    for copy in copies:
-        copy.wait()
+        for m in range(out.shape[1]):
+            out[x, m] = tables[x % 2][m]
 
 
 def half_update(part, other, parent, xt, own, coupling, out, pair):
@@ -318,12 +314,11 @@
 
     pack = call(
         pack_kernel,
-        in_specs=[HBM] * 5,
-        out_specs=HBM,
-        out_shape=pltpu.HBM((NX, 5, 8, width), jnp.float32),
-        scratch_shapes=[pltpu.SemaphoreType.DMA((NX, 5))],
+        in_specs=[VMEM] * 5,
+        out_specs=VMEM,
+        out_shape=pltpu.VMEM((NX, 5, 8, width), jnp.float32),
         name="pack",
-    )(*map(in_hbm, (sep_inverse, sep_coupling, root_coupling, root_rhs, root_inverse)))
+    )(sep_inverse, sep_coupling, root_coupling, root_rhs, root_inverse)
     exchanged = lax.all_to_all(pack, X, 0, 0)
 
     leaf_rhs, leaf_inverse, leaf_coupling, sep_rhs = map(

time: 138 us -> 129 us (0.935)
  Pallas kernels: 23.5 us -> 14.2 us
    pallas_call x1, Pallas kernels: 11 us -> 1.63 us  [body(): call(pack_kernel, in_specs=[VMEM] * 5, out_specs=VMEM, out_shape=pltpu.VM...]
where the time goes in v10:
time: 129 us; the launch traced here: 128 us
  blocking collectives  77.7 us (60%)
  starting transfers between devices  16.3 us (13%)
  between operations  14.7 us (11%)
  Pallas kernels  14.2 us (11%)
  waiting for transfers between devices  4.07 us (3%)
    all_to_all x1, blocking collectives, body(): res = lax.all_to_all(res.reshape(NX, 2 * tiles * 8 * part, 128), X, 0, 0)  23 us
    all_to_all x1, blocking collectives, body(): out = lax.all_to_all(out, ROW, 0, 0)  20.8 us
    all_to_all x1, blocking collectives, body(): res = lax.all_to_all(res, 'y', 0, 0)  20.6 us
    all_to_all x1, blocking collectives, body(): root_out = lax.all_to_all(term, 'layer', 0, 0).sum(0)  13.2 us
    ppermute x1, starting transfers between devices, body(): res = keep + lax.ppermute(send, 'c', [(0, 1), (1, 0)])  8.52 us
    all_to_all x1, starting transfers between devices, body(): exchanged = lax.all_to_all(pack, X, 0, 0)  4.84 us
    pallas_call x1, Pallas kernels, leaves_send(): pl.pallas_call(functools.partial(send_kernel, part), grid=(n,), in_specs=...  4.23 us
    pallas_call x1, Pallas kernels, leaves_keep(): pl.pallas_call(functools.partial(keep_kernel, part), grid=(coupling.shape...  3.46 us
  transfers between devices with their start and end apart: 4, of which 3 were waited for; matrix products, arithmetic and copies ran while one was open for 0% of the time, Pallas kernels for 6%

profile of v10, /device:TPU:1, one launch (start us, length us, event | category | flops | bytes accessed | tf_op | source)
XLA Modules:
  0.0 128.4 jit_solution(12125583851304710205)
XLA Ops:
  7.2 1.6 %pack.1 = f32[4,5,8,512]{3,2,1,0:T(8,128)} custom-call(f32[1,4,8,512]{3,2,1,0:T(8,128)} %sep_inverse.1, f32[1,3,8,512]{3,2,1,0:T(8,128)} %sep_coupling.1, f32[1,8,512]{2,1,0:T(8,128)} %root_coupling.1, f32[8,384]{1,0:T(8,128)} %root_rhs.1, f32[8,512]{1,0:T(8,128)} %root_inverse.1), custom_call_target="tpu_custom_call" | custom-call | tf_op jit(solution)/shard_map/pack/pallas_call | solution.py:315
  8.8 4.8 %all-to-all-start = ((f32[4,5,8,512]{3,2,1,0:T(8,128)}), f32[4,5,8,512]{3,2,1,0:T(8,128)S(1)}, u32[]{:S(2)}, u32[]{:S(2)}) async-start(f32[4,5,8,512]{3,2,1,0:T(8,128)} %pack.1), calls=%async_computation | async-start | bytes 655360 | tf_op jit(solution)/shard_map/all_to_all | solution.py:322
  13.6 0.0 all-gather.3.cloned.1.call-start
  14.3 4.2 %leaves_send.1 = (f32[2,2,2,4,96,128]{5,4,3,2,1,0:T(8,128)S(1)}, f32[384,256]{1,0:T(8,128)S(1)}, f32[384,128]{1,0:T(8,128)S(1)}) custom-call(s32[1,1]{1,0:T(1,128)S(6)} %copy.12.parent, f32[1,1,256,384]{3,2,1,0:T(8,128)} %rhs.1, f32[1,1,256,256]{3,2,1,0:T(8,128)} %inv.1, f32[1,4,8,384]{3,2,1,0:T(8,128)} %sep.1, f32[1,1,4,512,256]{4,3,2,1,0:T(8,128)} %coupling.3), custom_call_target="tpu_custom_call" | custom-call | tf_op jit(solution)/shard_map/leaves_send/pallas_call | solution.py:135
  18.5 1.0 all-to-all-done
  19.5 0.0 copy-start
  19.5 0.7 copy-done
  20.3 0.0 all-gather.3.cloned.1.call-update
  20.3 8.5 %collective-permute-start = (f32[2,2,2,4,96,128]{5,4,3,2,1,0:T(8,128)S(1)}, f32[2,2,2,4,96,128]{5,4,3,2,1,0:T(8,128)S(1)}, u32[]{:S(2)}, u32[]{:S(2)}) collective-permute-start(f32[2,2,2,4,96,128]{5,4,3,2,1,0:T(8,128)S(1)} %get-tuple-element.16), channel_id=1, source_target_pairs={{0,1},{1,0},{2,3},{3,2},{4,5},{5,4},{6,7},{7,6},{8,9},{9,8},{10,11... | collective-permute-start | bytes 4718600 | tf_op jit(solution)/shard_map/ppermute | solution.py:331
  28.8 3.5 %leaves_keep.1 = f32[2,2,2,4,96,128]{5,4,3,2,1,0:T(8,128)S(1)} custom-call(s32[1,1]{1,0:T(1,128)S(6)} %copy.12.parent, f32[384,256]{1,0:T(8,128)S(1)} %get-tuple-element.14.xt, f32[384,128]{1,0:T(8,128)S(1)} %get-tuple-element.15.own, f32[1,1,4,512,256]{4,3,2,1,0:T(8,128)} %coupling.3), custom_call_target="tpu_custom_call" | custom-call | tf_op jit(solution)/shard_map/leaves_keep/pallas_call | solution.py:154
  32.3 0.0 collective-permute-done
  32.3 0.2 add.3
  32.5 23.0 %all_to_all.25.parts = f32[4,768,128]{2,1,0:T(8,128)S(1)} all-to-all(f32[4,768,128]{2,1,0:T(8,128)S(1)} %bitcast.2), channel_id=1, replica_groups=mesh['layer'=8,'xl'=2,'xh'=2,'y'=8,'c'=2] {'xl','xh'}, dimensions={0} | all-to-all | bytes 3145728 | tf_op jit(solution)/shard_map/all_to_all | solution.py:332
  55.5 0.3 sum_x.1
  55.8 20.6 %all_to_all.26.parts = f32[8,96,128]{2,1,0:T(8,128)S(1)} all-to-all(f32[8,96,128]{2,1,0:T(8,128)S(1)} %sum_x.1), channel_id=1, replica_groups=mesh['layer'=8,'xl'=2,'xh'=2,'y'=8,'c'=2] {'y'}, dimensions={0} | all-to-all | bytes 786432 | tf_op jit(solution)/shard_map/all_to_all | solution.py:341
  76.5 1.9 %all-gather.3.cloned.1.call-done = f32[64,5,8,512]{3,2,1,0:T(8,128)} async-done(((f32[4,5,8,512]{3,2,1,0:T(8,128)}), f32[64,5,8,512]{3,2,1,0:T(8,128)}) %all-gather.3.cloned.1.call-update) | async-done | bytes 5242896 | tf_op jit(solution)/shard_map/all_gather | solution.py:329
  78.4 3.4 %chain_first.1 = (f32[2,16,512]{2,1,0:T(8,128)S(1)}, f32[24,512]{1,0:T(8,128)S(1)}, bf16[3,512,512]{2,1,0:T(8,128)(2,1)S(1)}, bf16[3,512,512]{2,1,0:T(8,128)(2,1)S(1)}) custom-call(f32[8,96,128]{2,1,0:T(8,128)S(1)} %all_to_all.26.parts, f32[16,4,5,8,512]{4,3,2,1,0:T(8,128)} %bitcast.3), custom_call_target="tpu_custom_call" | custom-call | tf_op jit(solution)/shard_map/chain_first/pallas_call | solution.py:343
  81.7 2.9 %collective-permute-start.1 = (f32[24,512]{1,0:T(8,128)S(1)}, f32[24,512]{1,0:T(8,128)S(1)}, u32[]{:S(2)}, u32[]{:S(2)}) collective-permute-start(f32[24,512]{1,0:T(8,128)S(1)} %get-tuple-element.19), channel_id=1, source_target_pairs={{0,16},{1,17},{2,18},{3,19},{4,20},{5,21},{6,22},{7,23},{8,24},{9,... | collective-permute-start | bytes 147464 | tf_op jit(solution)/shard_map/ppermute | solution.py:353
  84.6 1.2 collective-permute-done.1.came
  85.8 0.2 chain_second.1
  86.0 20.8 %all_to_all.27.got = f32[64,3,128]{2,1,0:T(4,128)S(1)} all-to-all(f32[64,3,128]{2,1,0:T(4,128)S(1)} %chain_second.1), channel_id=1, replica_groups=mesh['layer'=8,'xl'=2,'xh'=2,'y'=8,'c'=2] {'xl','xh','y','c'}, dimensions={0} | all-to-all | bytes 196608 | tf_op jit(solution)/shard_map/all_to_all | solution.py:364
  106.7 1.0 unpack.1
  107.8 13.2 %all_to_all.28 = f32[8,8,384]{2,1,0:T(8,128)S(1)} all-to-all(f32[8,8,384]{2,1,0:T(8,128)S(1)} %get-tuple-element.23), channel_id=1, replica_groups=mesh['layer'=8,'xl'=2,'xh'=2,'y'=8,'c'=2] {'layer'}, dimensions={0} | all-to-all | bytes 196608 | tf_op jit(solution)/shard_map/all_to_all | solution.py:373
  121.0 0.6 reduce_sum.9
Async XLA Ops:
  8.8 10.7 %all-to-all-start = ((f32[4,5,8,512]{3,2,1,0:T(8,128)}), f32[4,5,8,512]{3,2,1,0:T(8,128)S(1)}, u32[]{:S(2)}, u32[]{:S(2)}) async-start(f32[4,5,8,512]{3,2,1,0:T(8,128)} %pack.1), calls=%async_computation | async-start | bytes 655360 | tf_op jit(solution)/shard_map/all_to_all | solution.py:322
  13.6 64.7 %all-gather.3.cloned.1.call-start = ((), (), s32[]{:S(2)}) async-start(), calls=%async_computation.5 | async-start | bytes 5570560 | tf_op jit(solution)/shard_map/all_gather | solution.py:329
  19.5 0.7 copy-start
  20.3 12.0 %collective-permute-start = (f32[2,2,2,4,96,128]{5,4,3,2,1,0:T(8,128)S(1)}, f32[2,2,2,4,96,128]{5,4,3,2,1,0:T(8,128)S(1)}, u32[]{:S(2)}, u32[]{:S(2)}) collective-permute-start(f32[2,2,2,4,96,128]{5,4,3,2,1,0:T(8,128)S(1)} %get-tuple-element.16), channel_id=1, source_target_pairs={{0,1},{1,0},{2,3},{3,2},{4,5},{5,4},{6,7},{7,6},{8,9},{9,8},{10,11... | collective-permute-start | bytes 4718600 | tf_op jit(solution)/shard_map/ppermute | solution.py:331
  81.7 4.1 %collective-permute-start.1 = (f32[24,512]{1,0:T(8,128)S(1)}, f32[24,512]{1,0:T(8,128)S(1)}, u32[]{:S(2)}, u32[]{:S(2)}) collective-permute-start(f32[24,512]{1,0:T(8,128)S(1)} %get-tuple-element.19), channel_id=1, source_target_pairs={{0,16},{1,17},{2,18},{3,19},{4,20},{5,21},{6,22},{7,23},{8,24},{9,... | collective-permute-start | bytes 147464 | tf_op jit(solution)/shard_map/ppermute | solution.py:353
Sparse Core Ops, SparseCore 0:
  20.4 57.9 all-gather.2

commit v11 on v10

--- a/solution.py
+++ b/solution.py
@@ -176,15 +176,16 @@
     def copies(m):
         return [
             pltpu.make_async_copy(
-                weights.at[:, src, m], full.at[m, pl.ds(16 * src, 16)], sems.at[m, src]
+                weights.at[pl.ds(NY * core, NY), src, m], full.at[m, src, :, core], sems.at[m, src, core]
             )
             for src in range(NX)
+            for core in range(NC)
         ]
 
     def matrix(m):
         for copy in copies(m):
             copy.wait()
-        return split(full[m].reshape(-1, full.shape[3]))
+        return split(full[m].reshape(-1, full.shape[-1]))
 
     for m in range(full.shape[0]):
         for copy in copies(m):
@@ -326,7 +327,7 @@
     )
     send, xt, own = leaves_send(parent, leaf_rhs, leaf_inverse, leaf_coupling, sep_rhs)
     exchanged, xt = lax.optimization_barrier((exchanged, xt))
-    weights = lax.all_gather(exchanged, ("y", "c"))
+    weights = lax.all_gather(exchanged, ("c", "y"))
     keep = leaves_keep(parent, xt, own, leaf_coupling)
     res = keep + lax.ppermute(send, "c", [(0, 1), (1, 0)])
     res = lax.all_to_all(res.reshape(NX, 2 * tiles * 8 * part, 128), X, 0, 0)
@@ -346,7 +347,10 @@
         out_specs=[VMEM] * 4,
         out_shape=[FLAT((2, 16, width), jnp.float32), FLAT((2 * part, width), jnp.float32)]
         + [FLAT((3, width, width), jnp.bfloat16)] * 2,
-        scratch_shapes=[pltpu.VMEM((5, 64, 8, width), jnp.float32), pltpu.SemaphoreType.DMA((5, NX))],
+        scratch_shapes=[
+            pltpu.VMEM((5, NX, NY, NC, 8, width), jnp.float32),
+            pltpu.SemaphoreType.DMA((5, NX, NC)),
+        ],
         compiler_params=pltpu.CompilerParams(vmem_limit_bytes=32 * 2**20),
         name="chain_first",
     )(res, in_hbm(weights))

time: 129 us -> 129 us (level)
  no operation moved by 1% of the time
where the time goes in v11:
time: 129 us
  blocking collectives  77.7 us (60%)
  starting transfers between devices  16.2 us (13%)
  between operations  14.7 us (11%)
  Pallas kernels  14.5 us (11%)
  waiting for transfers between devices  4.07 us (3%)
    all_to_all x1, blocking collectives, body(): res = lax.all_to_all(res.reshape(NX, 2 * tiles * 8 * part, 128), X, 0, 0)  23 us
    all_to_all x1, blocking collectives, body(): out = lax.all_to_all(out, ROW, 0, 0)  20.8 us
    all_to_all x1, blocking collectives, body(): res = lax.all_to_all(res, 'y', 0, 0)  20.6 us
    all_to_all x1, blocking collectives, body(): root_out = lax.all_to_all(term, 'layer', 0, 0).sum(0)  13.2 us
    ppermute x1, starting transfers between devices, body(): res = keep + lax.ppermute(send, 'c', [(0, 1), (1, 0)])  8.52 us
    all_to_all x1, starting transfers between devices, body(): exchanged = lax.all_to_all(pack, X, 0, 0)  4.84 us
    pallas_call x1, Pallas kernels, leaves_send(): pl.pallas_call(functools.partial(send_kernel, part), grid=(n,), in_specs=...  4.23 us
    pallas_call x1, Pallas kernels, body(): call(functools.partial(first_kernel, part, cols), in_specs=[VMEM, HBM], o...  3.65 us
  transfers between devices with their start and end apart: 4, of which 3 were waited for; matrix products, arithmetic and copies ran while one was open for 0% of the time, Pallas kernels for 6%

profile of v11, /device:TPU:1, one launch (start us, length us, event | category | flops | bytes accessed | tf_op | source)
XLA Modules:
  0.0 128.7 jit_solution(2451072777433704903)
XLA Ops:
  7.2 1.6 %pack.1 = f32[4,5,8,512]{3,2,1,0:T(8,128)} custom-call(f32[1,4,8,512]{3,2,1,0:T(8,128)} %sep_inverse.1, f32[1,3,8,512]{3,2,1,0:T(8,128)} %sep_coupling.1, f32[1,8,512]{2,1,0:T(8,128)} %root_coupling.1, f32[8,384]{1,0:T(8,128)} %root_rhs.1, f32[8,512]{1,0:T(8,128)} %root_inverse.1), custom_call_target="tpu_custom_call" | custom-call | tf_op jit(solution)/shard_map/pack/pallas_call | solution.py:316
  8.8 4.8 %all-to-all-start = ((f32[4,5,8,512]{3,2,1,0:T(8,128)}), f32[4,5,8,512]{3,2,1,0:T(8,128)S(1)}, u32[]{:S(2)}, u32[]{:S(2)}) async-start(f32[4,5,8,512]{3,2,1,0:T(8,128)} %pack.1), calls=%async_computation | async-start | bytes 655360 | tf_op jit(solution)/shard_map/all_to_all | solution.py:323
  13.6 0.0 all-gather.3.cloned.1.call-start
  14.3 4.2 %leaves_send.1 = (f32[2,2,2,4,96,128]{5,4,3,2,1,0:T(8,128)S(1)}, f32[384,256]{1,0:T(8,128)S(1)}, f32[384,128]{1,0:T(8,128)S(1)}) custom-call(s32[1,1]{1,0:T(1,128)S(6)} %copy.12.parent, f32[1,1,256,384]{3,2,1,0:T(8,128)} %rhs.1, f32[1,1,256,256]{3,2,1,0:T(8,128)} %inv.1, f32[1,4,8,384]{3,2,1,0:T(8,128)} %sep.1, f32[1,1,4,512,256]{4,3,2,1,0:T(8,128)} %coupling.3), custom_call_target="tpu_custom_call" | custom-call | tf_op jit(solution)/shard_map/leaves_send/pallas_call | solution.py:135
  18.5 1.0 all-to-all-done
  19.5 0.0 copy-start
  19.5 0.7 copy-done
  20.3 0.0 all-gather.3.cloned.1.call-update
  20.3 8.5 %collective-permute-start = (f32[2,2,2,4,96,128]{5,4,3,2,1,0:T(8,128)S(1)}, f32[2,2,2,4,96,128]{5,4,3,2,1,0:T(8,128)S(1)}, u32[]{:S(2)}, u32[]{:S(2)}) collective-permute-start(f32[2,2,2,4,96,128]{5,4,3,2,1,0:T(8,128)S(1)} %get-tuple-element.16), channel_id=1, source_target_pairs={{0,1},{1,0},{2,3},{3,2},{4,5},{5,4},{6,7},{7,6},{8,9},{9,8},{10,11... | collective-permute-start | bytes 4718600 | tf_op jit(solution)/shard_map/ppermute | solution.py:332
  28.8 3.5 %leaves_keep.1 = f32[2,2,2,4,96,128]{5,4,3,2,1,0:T(8,128)S(1)} custom-call(s32[1,1]{1,0:T(1,128)S(6)} %copy.12.parent, f32[384,256]{1,0:T(8,128)S(1)} %get-tuple-element.14.xt, f32[384,128]{1,0:T(8,128)S(1)} %get-tuple-element.15.own, f32[1,1,4,512,256]{4,3,2,1,0:T(8,128)} %coupling.3), custom_call_target="tpu_custom_call" | custom-call | tf_op jit(solution)/shard_map/leaves_keep/pallas_call | solution.py:154
  32.3 0.0 collective-permute-done
  32.3 0.2 add.3
  32.5 23.0 %all_to_all.25.parts = f32[4,768,128]{2,1,0:T(8,128)S(1)} all-to-all(f32[4,768,128]{2,1,0:T(8,128)S(1)} %bitcast.2), channel_id=1, replica_groups=mesh['layer'=8,'xl'=2,'xh'=2,'y'=8,'c'=2] {'xl','xh'}, dimensions={0} | all-to-all | bytes 3145728 | tf_op jit(solution)/shard_map/all_to_all | solution.py:333
  55.5 0.3 sum_x.1
  55.8 20.6 %all_to_all.26.parts = f32[8,96,128]{2,1,0:T(8,128)S(1)} all-to-all(f32[8,96,128]{2,1,0:T(8,128)S(1)} %sum_x.1), channel_id=1, replica_groups=mesh['layer'=8,'xl'=2,'xh'=2,'y'=8,'c'=2] {'y'}, dimensions={0} | all-to-all | bytes 786432 | tf_op jit(solution)/shard_map/all_to_all | solution.py:342
  76.5 1.9 %all-gather.3.cloned.1.call-done = f32[64,5,8,512]{3,2,1,0:T(8,128)} async-done(((f32[4,5,8,512]{3,2,1,0:T(8,128)}), f32[64,5,8,512]{3,2,1,0:T(8,128)}) %all-gather.3.cloned.1.call-update) | async-done | bytes 5242896 | tf_op jit(solution)/shard_map/all_gather | solution.py:330
  78.4 3.6 %chain_first.1 = (f32[2,16,512]{2,1,0:T(8,128)S(1)}, f32[24,512]{1,0:T(8,128)S(1)}, bf16[3,512,512]{2,1,0:T(8,128)(2,1)S(1)}, bf16[3,512,512]{2,1,0:T(8,128)(2,1)S(1)}) custom-call(f32[8,96,128]{2,1,0:T(8,128)S(1)} %all_to_all.26.parts, f32[16,4,5,8,512]{4,3,2,1,0:T(8,128)} %bitcast.3), custom_call_target="tpu_custom_call" | custom-call | tf_op jit(solution)/shard_map/chain_first/pallas_call | solution.py:344
  82.0 2.8 %collective-permute-start.1 = (f32[24,512]{1,0:T(8,128)S(1)}, f32[24,512]{1,0:T(8,128)S(1)}, u32[]{:S(2)}, u32[]{:S(2)}) collective-permute-start(f32[24,512]{1,0:T(8,128)S(1)} %get-tuple-element.19), channel_id=1, source_target_pairs={{0,16},{1,17},{2,18},{3,19},{4,20},{5,21},{6,22},{7,23},{8,24},{9,... | collective-permute-start | bytes 147464 | tf_op jit(solution)/shard_map/ppermute | solution.py:357
  84.9 1.2 collective-permute-done.1.came
  86.0 0.2 chain_second.1
  86.2 20.8 %all_to_all.27.got = f32[64,3,128]{2,1,0:T(4,128)S(1)} all-to-all(f32[64,3,128]{2,1,0:T(4,128)S(1)} %chain_second.1), channel_id=1, replica_groups=mesh['layer'=8,'xl'=2,'xh'=2,'y'=8,'c'=2] {'xl','xh','y','c'}, dimensions={0} | all-to-all | bytes 196608 | tf_op jit(solution)/shard_map/all_to_all | solution.py:368
  107.0 1.0 unpack.1
  108.0 13.2 %all_to_all.28 = f32[8,8,384]{2,1,0:T(8,128)S(1)} all-to-all(f32[8,8,384]{2,1,0:T(8,128)S(1)} %get-tuple-element.23), channel_id=1, replica_groups=mesh['layer'=8,'xl'=2,'xh'=2,'y'=8,'c'=2] {'layer'}, dimensions={0} | all-to-all | bytes 196608 | tf_op jit(solution)/shard_map/all_to_all | solution.py:377
  121.2 0.6 reduce_sum.9
Async XLA Ops:
  8.8 10.7 %all-to-all-start = ((f32[4,5,8,512]{3,2,1,0:T(8,128)}), f32[4,5,8,512]{3,2,1,0:T(8,128)S(1)}, u32[]{:S(2)}, u32[]{:S(2)}) async-start(f32[4,5,8,512]{3,2,1,0:T(8,128)} %pack.1), calls=%async_computation | async-start | bytes 655360 | tf_op jit(solution)/shard_map/all_to_all | solution.py:323
  13.6 64.7 %all-gather.3.cloned.1.call-start = ((), (), s32[]{:S(2)}) async-start(), calls=%async_computation.5 | async-start | bytes 5570560 | tf_op jit(solution)/shard_map/all_gather | solution.py:330
  19.5 0.7 copy-start
  20.3 12.0 %collective-permute-start = (f32[2,2,2,4,96,128]{5,4,3,2,1,0:T(8,128)S(1)}, f32[2,2,2,4,96,128]{5,4,3,2,1,0:T(8,128)S(1)}, u32[]{:S(2)}, u32[]{:S(2)}) collective-permute-start(f32[2,2,2,4,96,128]{5,4,3,2,1,0:T(8,128)S(1)} %get-tuple-element.16), channel_id=1, source_target_pairs={{0,1},{1,0},{2,3},{3,2},{4,5},{5,4},{6,7},{7,6},{8,9},{9,8},{10,11... | collective-permute-start | bytes 4718600 | tf_op jit(solution)/shard_map/ppermute | solution.py:332
  82.0 4.0 %collective-permute-start.1 = (f32[24,512]{1,0:T(8,128)S(1)}, f32[24,512]{1,0:T(8,128)S(1)}, u32[]{:S(2)}, u32[]{:S(2)}) collective-permute-start(f32[24,512]{1,0:T(8,128)S(1)} %get-tuple-element.19), channel_id=1, source_target_pairs={{0,16},{1,17},{2,18},{3,19},{4,20},{5,21},{6,22},{7,23},{8,24},{9,... | collective-permute-start | bytes 147464 | tf_op jit(solution)/shard_map/ppermute | solution.py:357
Sparse Core Ops, SparseCore 0:
  20.4 57.9 all-gather.2

commit v12 on v10

--- a/solution.py
+++ b/solution.py
@@ -184,9 +184,12 @@
     def matrix(m):
         for copy in copies(m):
             copy.wait()
+        if m < full.shape[0] - 3:
+            for copy in copies(m + 3):
+                copy.start()
         return split(full[m].reshape(-1, full.shape[3]))
 
-    for m in range(full.shape[0]):
+    for m in range(3):
         for copy in copies(m):
             copy.start()
 

time: 129 us -> 130 us (level)
  no operation moved by 1% of the time
where the time goes in v12:
time: 130 us; the launch traced here: 129 us
  blocking collectives  77.7 us (60%)
  starting transfers between devices  16.6 us (13%)
  between operations  14.7 us (11%)
  Pallas kernels  14.3 us (11%)
  waiting for transfers between devices  4.07 us (3%)
    all_to_all x1, blocking collectives, body(): res = lax.all_to_all(res.reshape(NX, 2 * tiles * 8 * part, 128), X, 0, 0)  23 us
    all_to_all x1, blocking collectives, body(): out = lax.all_to_all(out, ROW, 0, 0)  20.8 us
    all_to_all x1, blocking collectives, body(): res = lax.all_to_all(res, 'y', 0, 0)  20.6 us
    all_to_all x1, blocking collectives, body(): root_out = lax.all_to_all(term, 'layer', 0, 0).sum(0)  13.2 us
    ppermute x1, starting transfers between devices, body(): res = keep + lax.ppermute(send, 'c', [(0, 1), (1, 0)])  8.52 us
    all_to_all x1, starting transfers between devices, body(): exchanged = lax.all_to_all(pack, X, 0, 0)  4.84 us
    pallas_call x1, Pallas kernels, leaves_send(): pl.pallas_call(functools.partial(send_kernel, part), grid=(n,), in_specs=...  4.23 us
    pallas_call x1, Pallas kernels, leaves_keep(): pl.pallas_call(functools.partial(keep_kernel, part), grid=(coupling.shape...  3.46 us
  transfers between devices with their start and end apart: 4, of which 3 were waited for; matrix products, arithmetic and copies ran while one was open for 0% of the time, Pallas kernels for 6%

profile of v12, /device:TPU:1, one launch (start us, length us, event | category | flops | bytes accessed | tf_op | source)
XLA Modules:
  0.0 128.9 jit_solution(2179134183123764473)
XLA Ops:
  7.2 1.6 %pack.1 = f32[4,5,8,512]{3,2,1,0:T(8,128)} custom-call(f32[1,4,8,512]{3,2,1,0:T(8,128)} %sep_inverse.1, f32[1,3,8,512]{3,2,1,0:T(8,128)} %sep_coupling.1, f32[1,8,512]{2,1,0:T(8,128)} %root_coupling.1, f32[8,384]{1,0:T(8,128)} %root_rhs.1, f32[8,512]{1,0:T(8,128)} %root_inverse.1), custom_call_target="tpu_custom_call" | custom-call | tf_op jit(solution)/shard_map/pack/pallas_call | solution.py:318
  8.8 4.8 %all-to-all-start = ((f32[4,5,8,512]{3,2,1,0:T(8,128)}), f32[4,5,8,512]{3,2,1,0:T(8,128)S(1)}, u32[]{:S(2)}, u32[]{:S(2)}) async-start(f32[4,5,8,512]{3,2,1,0:T(8,128)} %pack.1), calls=%async_computation | async-start | bytes 655360 | tf_op jit(solution)/shard_map/all_to_all | solution.py:325
  13.6 0.0 all-gather.3.cloned.1.call-start
  14.3 4.2 %leaves_send.1 = (f32[2,2,2,4,96,128]{5,4,3,2,1,0:T(8,128)S(1)}, f32[384,256]{1,0:T(8,128)S(1)}, f32[384,128]{1,0:T(8,128)S(1)}) custom-call(s32[1,1]{1,0:T(1,128)S(6)} %copy.12.parent, f32[1,1,256,384]{3,2,1,0:T(8,128)} %rhs.1, f32[1,1,256,256]{3,2,1,0:T(8,128)} %inv.1, f32[1,4,8,384]{3,2,1,0:T(8,128)} %sep.1, f32[1,1,4,512,256]{4,3,2,1,0:T(8,128)} %coupling.3), custom_call_target="tpu_custom_call" | custom-call | tf_op jit(solution)/shard_map/leaves_send/pallas_call | solution.py:135
  18.5 1.0 all-to-all-done
  19.5 0.0 copy-start
  19.5 0.7 copy-done
  20.3 0.0 all-gather.3.cloned.1.call-update
  20.3 8.5 %collective-permute-start = (f32[2,2,2,4,96,128]{5,4,3,2,1,0:T(8,128)S(1)}, f32[2,2,2,4,96,128]{5,4,3,2,1,0:T(8,128)S(1)}, u32[]{:S(2)}, u32[]{:S(2)}) collective-permute-start(f32[2,2,2,4,96,128]{5,4,3,2,1,0:T(8,128)S(1)} %get-tuple-element.16), channel_id=1, source_target_pairs={{0,1},{1,0},{2,3},{3,2},{4,5},{5,4},{6,7},{7,6},{8,9},{9,8},{10,11... | collective-permute-start | bytes 4718600 | tf_op jit(solution)/shard_map/ppermute | solution.py:334
  28.8 3.5 %leaves_keep.1 = f32[2,2,2,4,96,128]{5,4,3,2,1,0:T(8,128)S(1)} custom-call(s32[1,1]{1,0:T(1,128)S(6)} %copy.12.parent, f32[384,256]{1,0:T(8,128)S(1)} %get-tuple-element.14.xt, f32[384,128]{1,0:T(8,128)S(1)} %get-tuple-element.15.own, f32[1,1,4,512,256]{4,3,2,1,0:T(8,128)} %coupling.3), custom_call_target="tpu_custom_call" | custom-call | tf_op jit(solution)/shard_map/leaves_keep/pallas_call | solution.py:154
  32.3 0.0 collective-permute-done
  32.3 0.2 add.3
  32.5 23.0 %all_to_all.25.parts = f32[4,768,128]{2,1,0:T(8,128)S(1)} all-to-all(f32[4,768,128]{2,1,0:T(8,128)S(1)} %bitcast.2), channel_id=1, replica_groups=mesh['layer'=8,'xl'=2,'xh'=2,'y'=8,'c'=2] {'xl','xh'}, dimensions={0} | all-to-all | bytes 3145728 | tf_op jit(solution)/shard_map/all_to_all | solution.py:335
  55.5 0.3 sum_x.1
  55.8 20.6 %all_to_all.26.parts = f32[8,96,128]{2,1,0:T(8,128)S(1)} all-to-all(f32[8,96,128]{2,1,0:T(8,128)S(1)} %sum_x.1), channel_id=1, replica_groups=mesh['layer'=8,'xl'=2,'xh'=2,'y'=8,'c'=2] {'y'}, dimensions={0} | all-to-all | bytes 786432 | tf_op jit(solution)/shard_map/all_to_all | solution.py:344
  76.5 1.9 %all-gather.3.cloned.1.call-done = f32[64,5,8,512]{3,2,1,0:T(8,128)} async-done(((f32[4,5,8,512]{3,2,1,0:T(8,128)}), f32[64,5,8,512]{3,2,1,0:T(8,128)}) %all-gather.3.cloned.1.call-update) | async-done | bytes 5242896 | tf_op jit(solution)/shard_map/all_gather | solution.py:332
  78.4 3.5 %chain_first.1 = (f32[2,16,512]{2,1,0:T(8,128)S(1)}, f32[24,512]{1,0:T(8,128)S(1)}, bf16[3,512,512]{2,1,0:T(8,128)(2,1)S(1)}, bf16[3,512,512]{2,1,0:T(8,128)(2,1)S(1)}) custom-call(f32[8,96,128]{2,1,0:T(8,128)S(1)} %all_to_all.26.parts, f32[16,4,5,8,512]{4,3,2,1,0:T(8,128)} %bitcast.3), custom_call_target="tpu_custom_call" | custom-call | tf_op jit(solution)/shard_map/chain_first/pallas_call | solution.py:346
  81.8 3.2 %collective-permute-start.1 = (f32[24,512]{1,0:T(8,128)S(1)}, f32[24,512]{1,0:T(8,128)S(1)}, u32[]{:S(2)}, u32[]{:S(2)}) collective-permute-start(f32[24,512]{1,0:T(8,128)S(1)} %get-tuple-element.19), channel_id=1, source_target_pairs={{0,16},{1,17},{2,18},{3,19},{4,20},{5,21},{6,22},{7,23},{8,24},{9,... | collective-permute-start | bytes 147464 | tf_op jit(solution)/shard_map/ppermute | solution.py:356
  85.1 1.2 collective-permute-done.1.came
  86.2 0.2 chain_second.1
  86.4 20.8 %all_to_all.27.got = f32[64,3,128]{2,1,0:T(4,128)S(1)} all-to-all(f32[64,3,128]{2,1,0:T(4,128)S(1)} %chain_second.1), channel_id=1, replica_groups=mesh['layer'=8,'xl'=2,'xh'=2,'y'=8,'c'=2] {'xl','xh','y','c'}, dimensions={0} | all-to-all | bytes 196608 | tf_op jit(solution)/shard_map/all_to_all | solution.py:367
  107.2 1.0 unpack.1
  108.2 13.2 %all_to_all.28 = f32[8,8,384]{2,1,0:T(8,128)S(1)} all-to-all(f32[8,8,384]{2,1,0:T(8,128)S(1)} %get-tuple-element.23), channel_id=1, replica_groups=mesh['layer'=8,'xl'=2,'xh'=2,'y'=8,'c'=2] {'layer'}, dimensions={0} | all-to-all | bytes 196608 | tf_op jit(solution)/shard_map/all_to_all | solution.py:376
  121.4 0.6 reduce_sum.9
Async XLA Ops:
  8.8 10.7 %all-to-all-start = ((f32[4,5,8,512]{3,2,1,0:T(8,128)}), f32[4,5,8,512]{3,2,1,0:T(8,128)S(1)}, u32[]{:S(2)}, u32[]{:S(2)}) async-start(f32[4,5,8,512]{3,2,1,0:T(8,128)} %pack.1), calls=%async_computation | async-start | bytes 655360 | tf_op jit(solution)/shard_map/all_to_all | solution.py:325
  13.6 64.7 %all-gather.3.cloned.1.call-start = ((), (), s32[]{:S(2)}) async-start(), calls=%async_computation.5 | async-start | bytes 5570560 | tf_op jit(solution)/shard_map/all_gather | solution.py:332
  19.5 0.7 copy-start
  20.3 12.0 %collective-permute-start = (f32[2,2,2,4,96,128]{5,4,3,2,1,0:T(8,128)S(1)}, f32[2,2,2,4,96,128]{5,4,3,2,1,0:T(8,128)S(1)}, u32[]{:S(2)}, u32[]{:S(2)}) collective-permute-start(f32[2,2,2,4,96,128]{5,4,3,2,1,0:T(8,128)S(1)} %get-tuple-element.16), channel_id=1, source_target_pairs={{0,1},{1,0},{2,3},{3,2},{4,5},{5,4},{6,7},{7,6},{8,9},{9,8},{10,11... | collective-permute-start | bytes 4718600 | tf_op jit(solution)/shard_map/ppermute | solution.py:334
  81.8 4.4 %collective-permute-start.1 = (f32[24,512]{1,0:T(8,128)S(1)}, f32[24,512]{1,0:T(8,128)S(1)}, u32[]{:S(2)}, u32[]{:S(2)}) collective-permute-start(f32[24,512]{1,0:T(8,128)S(1)} %get-tuple-element.19), channel_id=1, source_target_pairs={{0,16},{1,17},{2,18},{3,19},{4,20},{5,21},{6,22},{7,23},{8,24},{9,... | collective-permute-start | bytes 147464 | tf_op jit(solution)/shard_map/ppermute | solution.py:356
Sparse Core Ops, SparseCore 0:
  20.4 57.9 all-gather.2
